TPU v7x, 768 devices: a whole 4x8x12 slice. The times are simulated.
768 devices in a mesh: rows: 192 (over z, y, core), cols: 4 (over x).
Axes of the slice: x: 4, y: 8, z: 12, core: 2. Of those that a mesh axis runs over, the one named last changes fastest.
Arguments:
- features: bfloat16 [256, 393216], P('cols', 'rows'), may hold values from -6 to 6
- node_order: int32 [192, 2048], P('rows'), may hold values from 0 to 2047, each once within a row
- adj_values: bfloat16 [18432, 128, 128], P('rows'), may hold values from -0.3125 to 0.3125
- blk_dest: int32 [192, 96], P('rows'), may hold values from 0 to 15, as said below
- blk_src: int32 [192, 96], P('rows'), may hold values from 0 to 79, as said below
- blk_count: int32 [192], P('rows'), may hold values from 12 to 96, as said below
- weight: bfloat16 [256, 256], replicated, may hold values from -0.375 to 0.375
- bias: float32 [256], replicated, may hold values from -3 to 3
- cotangent: bfloat16 [256, 393216], P(None, ('rows', 'cols')), may hold values from -6 to 6
Outputs:
- output: bfloat16 [256, 393216], P(None, ('rows', 'cols'))
- grad_x: bfloat16 [256, 393216], P('cols', 'rows')
- grad_w: float32 [256, 256], replicated
- grad_b: float32 [256], replicated
Inputs may be any that keep to these rules, and one draw needn't show every extreme that they name: `blk_dest`: destination block of a slot within its shard's 16 blocks. `blk_src`: Slot's source block (t + 2) * 16 + b: block b of shard (s + t) mod 192. Slots j < blk_count[s] are in use, the others are ignored; some shard has exactly 96 in use. Blocks may repeat.
All inputs are finite; a program needn't handle non-finite values.
Results may differ from a plain program's by a relative error of at most 0.01.
Values may be sent and summed in bfloat16 or wider, within the bound.
No kernel may reach another device: no remote copies, remote signals or barrier semaphores. Data moves between devices by JAX's collectives and lax.ppermute only.
A program may use at most 32 MiB of HBM per device.

v0:
```python
import math

import jax
import jax.numpy as jnp
from jax import lax
from jax.sharding import PartitionSpec as P

HOP = 2


def passed_along(value, axis, steps):
    count = lax.axis_size(axis)
    pairs = [(source, (source + steps) % count) for source in range(count)]
    return lax.ppermute(value, axis, pairs)


def activation(values):
    return jax.nn.gelu(values, approximate=True)


def on_device(
    features, node_order, adj_values, blk_dest, blk_src, blk_count, weight, bias, cotangent
):
    order = node_order[0]
    permuted = jnp.take(features, order, axis=1)
    feat_dim, node_count = permuted.shape
    block_len = adj_values.shape[1]
    slots = adj_values.shape[0]
    nblocks = node_count // block_len
    spread = 2 * HOP + 1
    offsets = list(range(-HOP, HOP + 1))
    fetched = {0: permuted}
    for offset in offsets:
        if offset != 0:
            fetched[offset] = passed_along(permuted, "rows", -offset)
    window = jnp.concatenate([fetched[offset] for offset in offsets], axis=1)
    window = window.reshape(feat_dim, spread * nblocks, block_len)
    sources = blk_src[0]
    targets = blk_dest[0]
    in_use = jnp.arange(slots, dtype=jnp.int32) < blk_count[0]
    picked = jnp.take(window, sources, axis=1)
    products = jnp.einsum("fjs,jds->jfd", picked, adj_values, preferred_element_type=jnp.float32)
    dest_table = (
        (targets[None, :] == jnp.arange(nblocks, dtype=jnp.int32)[:, None]) & in_use[None, :]
    ).astype(jnp.float32)
    hidden = jnp.einsum("bj,jfd->fbd", dest_table, products, precision=lax.Precision.HIGHEST)
    hidden = hidden.reshape(feat_dim, node_count).astype(jnp.bfloat16)
    hidden_rows = lax.all_to_all(hidden, "cols", split_axis=1, concat_axis=0, tiled=True)
    preact = (
        lax.dot_general(
            weight, hidden_rows, (((0,), (0,)), ((), ())), preferred_element_type=jnp.float32
        )
        + bias[:, None]
    )
    output, pullback = jax.vjp(activation, preact)
    grad_pre = pullback(cotangent.astype(jnp.float32))[0].astype(jnp.bfloat16)
    local_w = lax.dot_general(
        hidden_rows, grad_pre, (((1,), (1,)), ((), ())), preferred_element_type=jnp.float32
    )
    local_b = jnp.sum(grad_pre.astype(jnp.float32), axis=1)
    total_w, total_b = lax.psum((local_w, local_b), ("rows", "cols"))
    scale = 1.0 / math.sqrt(node_count * lax.axis_size("rows"))
    grad_hidden = jnp.dot(weight, grad_pre, preferred_element_type=jnp.float32).astype(jnp.bfloat16)
    grad_cols = lax.all_to_all(grad_hidden, "cols", split_axis=0, concat_axis=1, tiled=True)
    grad_blocks = grad_cols.reshape(feat_dim, nblocks, block_len)
    back_picked = jnp.take(grad_blocks, targets, axis=1)
    back_products = jnp.einsum(
        "fjd,jds->jfs", back_picked, adj_values, preferred_element_type=jnp.float32
    )
    src_table = (
        (sources[None, :] == jnp.arange(spread * nblocks, dtype=jnp.int32)[:, None])
        & in_use[None, :]
    ).astype(jnp.float32)
    src_table = src_table.reshape(spread, nblocks, slots)
    parts = jnp.einsum("obj,jfs->ofbs", src_table, back_products, precision=lax.Precision.HIGHEST)
    parts = parts.reshape(spread, feat_dim, node_count)
    total = parts[HOP]
    for offset in offsets:
        if offset != 0:
            total = total + passed_along(
                parts[offset + HOP].astype(jnp.bfloat16), "rows", offset
            ).astype(jnp.float32)
    inverse = jnp.argsort(order)
    grad_x = jnp.take(total, inverse, axis=1).astype(jnp.bfloat16)
    return (output.astype(jnp.bfloat16), grad_x, total_w * scale, total_b * scale)


def solution(mesh):
    in_specs = (
        P("cols", "rows"),
        P("rows", None),
        P("rows", None, None),
        P("rows", None),
        P("rows", None),
        P("rows"),
        P(),
        P(),
        P(None, ("rows", "cols")),
    )
    out_specs = (P(None, ("rows", "cols")), P("cols", "rows"), P(), P())
    return jax.shard_map(
        on_device, mesh=mesh, in_specs=in_specs, out_specs=out_specs, check_vma=False
    )
```

profile of v0, /device:TPU:1, one launch (start us, length us, event | category | flops | bytes accessed | tf_op | source)
XLA Modules:
  0.0 599.1 jit_solution(4924344163837592302)
XLA Ops:
  9.0 2.0 copy.49
  10.9 8.8 %gather_fusion = bf16[2048,64]{1,0:T(8,128)(2,1)} fusion(bf16[64,2048]{0,1:T(8,128)(2,1)} %copy.49, s32[2048]{0:T(1024)S(1)} %broadcast_clamp_fusion), kind=kCustom, calls=%fused_computation | custom fusion | bytes 532480 | tf_op jit(solution)/shard_map/jit(_take)/gather | solution.py:25
  19.7 2.2 select_bitcast_fusion
  21.9 18.0 %collective-permute-start.3 = (bf16[64,2048]{0,1:T(8,128)(2,1)}, bf16[64,2048]{0,1:T(8,128)(2,1)}, u32[]{:S(2)}, u32[]{:S(2)}) collective-permute-start(bf16[64,2048]{0,1:T(8,128)(2,1)} %select_bitcast_fusion), channel_id=1, source_target_pairs={{0,760},{4,764},{8,0},{12,4},{16,8},{20,12},{24,16},{28,20},{32,24... | collective-permute-start | bytes 786440 | tf_op jit(solution)/shard_map/ppermute | solution.py:14
  40.0 2.9 collective-permute-start.2
  42.8 2.7 collective-permute-start.1
  45.5 1.9 collective-permute-start
  47.5 5.0 sort.17
  55.2 12.8 %collective-permute-done = bf16[64,2048]{0,1:T(8,128)(2,1)} collective-permute-done((bf16[64,2048]{0,1:T(8,128)(2,1)}, bf16[64,2048]{0,1:T(8,128)(2,1)}, u32[]{:S(2)}, u32[]{:S(2)}) %collective-permute-start) | collective-permute-done | bytes 262176 | tf_op jit(solution)/shard_map/ppermute | solution.py:14
  68.0 1.9 constant_dynamic-update-slice_fusion.4
  69.9 1.9 constant_dynamic-update-slice_fusion.3
  71.8 2.2 constant_dynamic-update-slice_fusion.2
  74.0 1.9 constant_dynamic-update-slice_fusion.1
  75.9 1.9 constant_dynamic-update-slice_fusion
  77.7 4.0 copy.50
  81.8 3.3 gather_fusion.1
  85.0 3.7 fusion.8
  88.7 2.9 fusion.18
  92.4 1.7 copy.52
  94.1 4.0 all-to-all-start
  98.1 1.2 compare_and_fusion.2
  99.3 4.3 all-to-all-done
  103.7 2.8 convert_reduce_fusion
  108.2 4.0 all-to-all-start.1
  112.3 1.9 fusion.56
  114.2 105.6 %psum.15 = f32[256]{0:T(256)S(1)} all-reduce(f32[256]{0:T(256)} %get-tuple-element.22), channel_id=1, replica_groups=mesh['rows'=192,'cols'=4] {'rows','cols'}, use_global_device_ids=true, to_apply=%region_3.4 | all-reduce | flops 256 | bytes 2048 | tf_op jit(solution)/shard_map/psum | solution.py:61
  219.8 1.2 copy.54
  221.8 1.0 copy.55
  222.8 2.1 gather_fusion.2
  224.9 2.4 convolution_bitcast_fusion
  227.4 5.0 fusion.55
  233.3 2.0 copy.68
  235.3 2.0 copy.71
  237.3 2.0 copy.70
  239.4 1.1 copy.69
  240.4 3.0 collective-permute-start.5
  243.4 2.6 collective-permute-start.6
  246.0 1.9 collective-permute-start.7
  247.9 6.7 %collective-permute-start.4 = (bf16[64,2048]{0,1:T(8,128)(2,1)}, bf16[64,2048]{0,1:T(8,128)(2,1)}, u32[]{:S(2)}, u32[]{:S(2)}) collective-permute-start(bf16[64,2048]{0,1:T(8,128)(2,1)} %bitcast.77), channel_id=1, source_target_pairs={{0,760},{4,764},{8,0},{12,4},{16,8},{20,12},{24,16},{28,20},{32,24... | collective-permute-start | bytes 786440 | tf_op jit(solution)/shard_map/ppermute | solution.py:14
  255.2 1.8 copy.62
  257.0 313.4 %all-reduce.2.cloned.1.call-done = f32[256,256]{1,0:T(8,128)} async-done(((f32[256,256]{1,0:T(8,128)}), f32[256,256]{1,0:T(8,128)}) %all-reduce.2.cloned.1.call-update) | async-done | bytes 262160 | tf_op jit(solution)/shard_map/psum | solution.py:61
  570.4 1.7 broadcast_multiply_fusion
  572.1 1.9 slice.37
  574.0 2.4 copy.67
  576.3 3.0 fusion.23
  579.3 8.8 %gather_fusion.3 = bf16[2048,64]{1,0:T(8,128)(2,1)} fusion(bf16[64,2048]{0,1:T(8,128)(2,1)} %fusion.23, s32[2048]{0:T(1024)S(1)} %fusion.46), kind=kCustom, calls=%fused_computation.3 | custom fusion | bytes 532480 | tf_op jit(solution)/shard_map/jit(_take)/gather | solution.py:84
  588.1 2.2 fusion.36
  590.3 1.9 copy.63
  (52 shorter events, 8.6 us)
Async XLA Ops:
  7.2 77.9 %copy-start = (bf16[96,128,128]{2,1,0:T(8,128)(2,1)S(1)}, bf16[96,128,128]{2,1,0:T(8,128)(2,1)}, u32[]{:S(2)}) copy-start(bf16[96,128,128]{2,1,0:T(8,128)(2,1)} %param.11) | copy-start | bytes 9437188
  7.2 40.3 %copy-start.4 = (s32[1,2048]{1,0:T(1,128)S(1)}, s32[1,2048]{1,0:T(1,128)}, u32[]{:S(2)}) copy-start(s32[1,2048]{1,0:T(1,128)} %param.10) | copy-start | bytes 24580
  7.2 40.3 %copy-start.9 = (s32[1,96]{1,0:T(1,128)S(1)}, s32[1,96]{1,0:T(1,128)}, u32[]{:S(2)}) copy-start(s32[1,96]{1,0:T(1,128)} %param.13) | copy-start | bytes 1156
  7.2 45.4 %copy-start.7 = (s32[1,96]{1,0:T(1,128)S(1)}, s32[1,96]{1,0:T(1,128)}, u32[]{:S(2)}) copy-start(s32[1,96]{1,0:T(1,128)} %param.12) | copy-start | bytes 1156
  7.2 47.2 %copy-start.2 = (bf16[256,512]{1,0:T(8,128)(2,1)S(1)}, bf16[256,512]{1,0:T(8,128)(2,1)}, u32[]{:S(2)}) copy-start(bf16[256,512]{1,0:T(8,128)(2,1)} %param.17) | copy-start | bytes 786436
  21.9 53.9 %collective-permute-start.3 = (bf16[64,2048]{0,1:T(8,128)(2,1)}, bf16[64,2048]{0,1:T(8,128)(2,1)}, u32[]{:S(2)}, u32[]{:S(2)}) collective-permute-start(bf16[64,2048]{0,1:T(8,128)(2,1)} %select_bitcast_fusion), channel_id=1, source_target_pairs={{0,760},{4,764},{8,0},{12,4},{16,8},{20,12},{24,16},{28,20},{32,24... | collective-permute-start | bytes 786440 | tf_op jit(solution)/shard_map/ppermute | solution.py:14
  40.0 34.0 %collective-permute-start.2 = (bf16[64,2048]{0,1:T(8,128)(2,1)}, bf16[64,2048]{0,1:T(8,128)(2,1)}, u32[]{:S(2)}, u32[]{:S(2)}) collective-permute-start(bf16[64,2048]{0,1:T(8,128)(2,1)} %select_bitcast_fusion), channel_id=1, source_target_pairs={{0,764},{4,0},{8,4},{12,8},{16,12},{20,16},{24,20},{28,24},{32,28}... | collective-permute-start | bytes 786440 | tf_op jit(solution)/shard_map/ppermute | solution.py:14
  42.8 27.1 %collective-permute-start.1 = (bf16[64,2048]{0,1:T(8,128)(2,1)}, bf16[64,2048]{0,1:T(8,128)(2,1)}, u32[]{:S(2)}, u32[]{:S(2)}) collective-permute-start(bf16[64,2048]{0,1:T(8,128)(2,1)} %select_bitcast_fusion), channel_id=1, source_target_pairs={{0,4},{4,8},{8,12},{12,16},{16,20},{20,24},{24,28},{28,32},{32,36}... | collective-permute-start | bytes 786440 | tf_op jit(solution)/shard_map/ppermute | solution.py:14
  45.5 22.5 %collective-permute-start = (bf16[64,2048]{0,1:T(8,128)(2,1)}, bf16[64,2048]{0,1:T(8,128)(2,1)}, u32[]{:S(2)}, u32[]{:S(2)}) collective-permute-start(bf16[64,2048]{0,1:T(8,128)(2,1)} %select_bitcast_fusion), channel_id=1, source_target_pairs={{0,8},{4,12},{8,16},{12,20},{16,24},{20,28},{24,32},{28,36},{32,40... | collective-permute-start | bytes 786440 | tf_op jit(solution)/shard_map/ppermute | solution.py:14
  85.0 3.7 copy-start.5
  85.0 3.7 copy-start.8
  88.7 15.0 %copy-start.3 = (bf16[256,256]{1,0:T(8,128)(2,1)S(1)}, bf16[256,256]{1,0:T(8,128)(2,1)}, u32[]{:S(2)}) copy-start(bf16[256,256]{1,0:T(8,128)(2,1)} %param.15) | copy-start | bytes 393220
  94.1 9.5 %all-to-all-start = ((bf16[64,4,512]{2,0,1:T(8,128)(2,1)}), bf16[64,4,512]{2,0,1:T(8,128)(2,1)S(1)}, u32[]{:S(2)}, u32[]{:S(2)}) async-start(bf16[64,4,512]{2,0,1:T(8,128)(2,1)} %copy.52), calls=%async_computation | async-start | bytes 524288 | tf_op jit(solution)/shard_map/all_to_all | solution.py:48
  106.5 0.7 copy-start.1
  108.2 111.6 %all-to-all-start.1 = ((bf16[4,64,512]{2,1,0:T(8,128)(2,1)}), bf16[4,64,512]{2,1,0:T(8,128)(2,1)}, u32[]{:S(2)}, u32[]{:S(2)}) async-start(bf16[4,64,512]{2,1,0:T(8,128)(2,1)} %bitcast.76), calls=%async_computation.1 | async-start | bytes 524288 | tf_op jit(solution)/shard_map/all_to_all | solution.py:64
  112.2 458.2 %all-reduce.2.cloned.1.call-start = ((), (), s32[]{:S(2)}) async-start(), calls=%async_computation.2 | async-start | bytes 524288 | tf_op jit(solution)/shard_map/psum | solution.py:61
  114.2 110.7 %copy-start.11 = (pred[96]{0:T(512)(128)(4,1)S(1)}, pred[96]{0:T(512)(128)(4,1)}, u32[]{:S(2)}) copy-start(pred[96]{0:T(512)(128)(4,1)} %compare_and_fusion.2) | copy-start | bytes 292
  224.9 2.4 copy-start.6
  224.9 2.4 copy-start.10
  240.4 335.9 %collective-permute-start.5 = (bf16[64,2048]{0,1:T(8,128)(2,1)}, bf16[64,2048]{0,1:T(8,128)(2,1)}, u32[]{:S(2)}, u32[]{:S(2)}) collective-permute-start(bf16[64,2048]{0,1:T(8,128)(2,1)} %bitcast.80), channel_id=1, source_target_pairs={{0,764},{4,0},{8,4},{12,8},{16,12},{20,16},{24,20},{28,24},{32,28}... | collective-permute-start | bytes 786440 | tf_op jit(solution)/shard_map/ppermute | solution.py:14
  243.4 332.9 %collective-permute-start.6 = (bf16[64,2048]{0,1:T(8,128)(2,1)}, bf16[64,2048]{0,1:T(8,128)(2,1)}, u32[]{:S(2)}, u32[]{:S(2)}) collective-permute-start(bf16[64,2048]{0,1:T(8,128)(2,1)} %bitcast.79), channel_id=1, source_target_pairs={{0,4},{4,8},{8,12},{12,16},{16,20},{20,24},{24,28},{28,32},{32,36}... | collective-permute-start | bytes 786440 | tf_op jit(solution)/shard_map/ppermute | solution.py:14
  246.0 330.3 %collective-permute-start.7 = (bf16[64,2048]{0,1:T(8,128)(2,1)}, bf16[64,2048]{0,1:T(8,128)(2,1)}, u32[]{:S(2)}, u32[]{:S(2)}) collective-permute-start(bf16[64,2048]{0,1:T(8,128)(2,1)} %bitcast.78), channel_id=1, source_target_pairs={{0,8},{4,12},{8,16},{12,20},{16,24},{20,28},{24,32},{28,36},{32,40... | collective-permute-start | bytes 786440 | tf_op jit(solution)/shard_map/ppermute | solution.py:14
  247.9 328.4 %collective-permute-start.4 = (bf16[64,2048]{0,1:T(8,128)(2,1)}, bf16[64,2048]{0,1:T(8,128)(2,1)}, u32[]{:S(2)}, u32[]{:S(2)}) collective-permute-start(bf16[64,2048]{0,1:T(8,128)(2,1)} %bitcast.77), channel_id=1, source_target_pairs={{0,760},{4,764},{8,0},{12,4},{16,8},{20,12},{24,16},{28,20},{32,24... | collective-permute-start | bytes 786440 | tf_op jit(solution)/shard_map/ppermute | solution.py:14
Sparse Core Ops, SparseCore 0:
  118.5 451.8 all-reduce.1
where the time goes:
time: 601 us; the launch traced here: 599 us
  waiting for transfers between devices  331 us (55%)
  blocking collectives  106 us (18%)
  local copies, waits for them, and re-layouts  59.6 us (10%)
  starting transfers between devices  47.8 us (8%)
  other arithmetic  20.9 us (3%)
  matrix products  19.7 us (3%)
  between operations  14.9 us (2%)
    psum x1, waiting for transfers between devices, on_device(): total_w, total_b = lax.psum((local_w, local_b), ('rows', 'cols'))  313 us
    psum x1, blocking collectives, on_device(): total_w, total_b = lax.psum((local_w, local_b), ('rows', 'cols'))  106 us
    ppermute x8, starting transfers between devices, passed_along(): return lax.ppermute(value, axis, pairs)  39.7 us
    unnamed x31, local copies, waits for them, and re-layouts  12.9 us
    ppermute x8, waiting for transfers between devices, passed_along(): return lax.ppermute(value, axis, pairs)  12.8 us
  transfers between devices with their start and end apart: 11, of which 3 were waited for; matrix products, arithmetic and copies ran while one was open for 8% of the time, Pallas kernels for 0%

commit v1 on v0

v1 whole, which is shorter than its diff:
```python
import math

import jax
import jax.numpy as jnp
from jax import lax
from jax.experimental import pallas as pl
from jax.experimental.pallas import tpu as pltpu
from jax.sharding import Mesh, PartitionSpec as P

BF16 = jnp.bfloat16
F32 = jnp.float32
BLOCK = 128
TILE = 256
ROWS = ("z", "y", "c")
CHUNK = 8
VMEM = pl.BlockSpec(memory_space=pltpu.VMEM)
SMEM = pl.BlockSpec(memory_space=pltpu.SMEM)
ANY = pl.BlockSpec(memory_space=pl.ANY)
PARAMS = pltpu.CompilerParams(vmem_limit_bytes=40 * 1024 * 1024)


def into_order(order_ref, x_ref, out_ref):
    count = x_ref.shape[1]
    for start in range(0, count, TILE):
        rows = lax.broadcasted_iota(jnp.int32, (count, TILE), 0)
        hot = jnp.where(order_ref[:, start : start + TILE] == rows, 1.0, 0.0).astype(BF16)
        moved = jnp.dot(x_ref[...], hot, preferred_element_type=F32)
        out_ref[:, start : start + TILE] = moved.astype(BF16)


def out_of_order(order_ref, own_ref, near_ref, first_ref, second_ref, out_ref, total_ref):
    count = own_ref.shape[1]
    total = own_ref[...] + near_ref[...].astype(F32)
    total = total + first_ref[...].astype(F32) + second_ref[...].astype(F32)
    total_ref[...] = total.astype(BF16)
    for start in range(0, count, TILE):
        rows = lax.broadcasted_iota(jnp.int32, (TILE, count), 0) + start
        hot = jnp.where(order_ref[...] == rows, 1.0, 0.0).astype(BF16)
        moved = lax.dot_general(
            total_ref[...], hot, (((1,), (1,)), ((), ())), preferred_element_type=F32
        )
        out_ref[:, start : start + TILE] = moved.astype(BF16)


def mirrored(source, core, nblocks, spread):
    offset = source // nblocks
    return jnp.where(core == 0, offset, spread - 1 - offset), source % nblocks


def adjacency_copies(adj_ref, adj, sems):
    slots = adj.shape[0]
    copies = []
    for index, start in enumerate(range(0, slots, CHUNK)):
        part = pl.ds(start, CHUNK)
        copies.append(pltpu.make_async_copy(adj_ref.at[part], adj.at[part], sems.at[index]))
    return copies


def aggregate(
    dest_ref, src_ref, count_ref, core_ref, w0, w1, w2, w3, w4, adj_ref, out_ref, win, adj, acc, wsem, asem
):
    slots = adj.shape[0]
    nblocks = acc.shape[0] - 1
    spread = win.shape[0]
    quarter = out_ref.shape[2] // BLOCK
    win_copies = [
        pltpu.make_async_copy(ref, win.at[i], wsem.at[i])
        for i, ref in enumerate((w0, w1, w2, w3, w4))
    ]
    adj_copies = adjacency_copies(adj_ref, adj, asem)
    for copy in win_copies + adj_copies:
        copy.start()
    acc[...] = jnp.zeros_like(acc)
    for copy in win_copies:
        copy.wait()
    core = core_ref[0]
    count = count_ref[0]
    for index, copy in enumerate(adj_copies):
        copy.wait()
        products = []
        for j in range(index * CHUNK, (index + 1) * CHUNK):
            offset, block = mirrored(src_ref[0, j], core, nblocks, spread)
            picked = win[offset, :, pl.ds(pl.multiple_of(block * BLOCK, BLOCK), BLOCK)]
            products.append(
                lax.dot_general(
                    picked, adj[j], (((1,), (1,)), ((), ())), preferred_element_type=F32
                )
            )
        for j, product in zip(range(index * CHUNK, (index + 1) * CHUNK), products):
            target = jnp.where(j < count, dest_ref[0, j], nblocks)
            acc[target] += product
    for block in range(nblocks):
        lane = (block % quarter) * BLOCK
        out_ref[block // quarter, :, lane : lane + BLOCK] = acc[block].astype(BF16)


def dense(hidden_ref, weight_ref, bias_ref, cot_ref, out_ref, send_ref):
    feat, width = hidden_ref.shape
    part = send_ref.shape[0]
    rows = feat // part
    hidden = hidden_ref[...]
    weight = weight_ref[...]
    v = (
        lax.dot_general(weight, hidden, (((0,), (0,)), ((), ())), preferred_element_type=F32)
        + bias_ref[...]
    )
    root = math.sqrt(2.0 / math.pi)
    square = v * v
    t = jnp.tanh(root * (v + 0.044715 * (square * v)))
    half = 0.5 * (1.0 + t)
    out_ref[...] = (v * half).astype(BF16)
    slope = half + (0.5 * root) * v * (1.0 - t * t) * (1.0 + (3.0 * 0.044715) * square)
    grad = (cot_ref[...].astype(F32) * slope).astype(BF16)
    back = jnp.dot(weight, grad, preferred_element_type=F32).astype(BF16)
    grad_w = lax.dot_general(hidden, grad, (((1,), (1,)), ((), ())), preferred_element_type=F32)
    ones = jnp.ones((16, width), BF16)
    grad_b = lax.dot_general(ones, grad, (((1,), (1,)), ((), ())), preferred_element_type=F32)
    high_w = grad_w.astype(BF16)
    low_w = (grad_w - high_w.astype(F32)).astype(BF16)
    high_b = grad_b.astype(BF16)
    low_b = (grad_b - high_b.astype(F32)).astype(BF16)
    half_width = grad_w.shape[1]
    for i in range(part):
        span = slice(i * rows, (i + 1) * rows)
        send_ref[i, 0:rows, :] = back[span]
        send_ref[i, rows : 2 * rows, 0:half_width] = high_w[span]
        send_ref[i, rows : 2 * rows, half_width:] = low_w[span]
        send_ref[i, 2 * rows :, 0:half_width] = high_b
        send_ref[i, 2 * rows :, half_width:] = low_b


def first_sum(recv_ref, out_ref):
    part, height, width = recv_ref.shape
    rows = (height - 16) // 2
    half_width = width // 2
    total = jnp.zeros((rows + 16, half_width), F32)
    for i in range(part):
        total = total + recv_ref[i, rows:, 0:half_width].astype(F32)
        total = total + recv_ref[i, rows:, half_width:].astype(F32)
    pieces = out_ref.shape[0] // 2
    for i in range(pieces):
        for c in range(2):
            lane = slice(c * BLOCK, (c + 1) * BLOCK)
            out_ref[2 * i + c, 0:8, :] = total[8 * i : 8 * i + 8, lane]
            out_ref[2 * i + c, 8:12, :] = total[rows : rows + 4, 0:BLOCK]
            out_ref[2 * i + c, 12:16, :] = total[rows : rows + 4, BLOCK : 2 * BLOCK]


def spread_back(
    dest_ref, src_ref, count_ref, core_ref, recv_ref, adj_ref,
    first_ref, far_ref, near_ref, own_ref, last_ref, grad, adj, acc, gsem, asem,
):
    slots = adj.shape[0]
    rows = grad.shape[1]
    quarter = grad.shape[2] // BLOCK
    nblocks = grad.shape[0] * quarter
    spread = (acc.shape[0] - 1) // nblocks
    grad_copy = pltpu.make_async_copy(recv_ref.at[:, pl.ds(0, rows), :], grad, gsem)
    grad_copy.start()
    adj_copies = adjacency_copies(adj_ref, adj, asem)
    for copy in adj_copies:
        copy.start()
    acc[...] = jnp.zeros_like(acc)
    core = core_ref[0]
    count = count_ref[0]
    grad_copy.wait()
    for index, copy in enumerate(adj_copies):
        copy.wait()
        products = []
        for j in range(index * CHUNK, (index + 1) * CHUNK):
            target = dest_ref[0, j]
            lane = pl.multiple_of((target % quarter) * BLOCK, BLOCK)
            picked = grad[target // quarter, :, pl.ds(lane, BLOCK)]
            products.append(jnp.dot(picked, adj[j], preferred_element_type=F32))
        for j, product in zip(range(index * CHUNK, (index + 1) * CHUNK), products):
            offset, block = mirrored(src_ref[0, j], core, nblocks, spread)
            place = jnp.where(j < count, offset * nblocks + block, spread * nblocks)
            acc[place] += product
    for offset, ref in enumerate((first_ref, far_ref, own_ref, near_ref, last_ref)):
        for block in range(nblocks):
            lane = slice(block * BLOCK, (block + 1) * BLOCK)
            ref[:, lane] = acc[offset * nblocks + block].astype(ref.dtype)


def on_device(
    features, node_order, adj_values, blk_dest, blk_src, blk_count, weight, bias, cotangent
):
    feat, nodes = features.shape
    slots = adj_values.shape[0]
    nblocks = nodes // BLOCK
    parts = lax.axis_size("x")
    out_feat, width = cotangent.shape
    shards = lax.axis_size(ROWS)
    ys, zs = lax.axis_size("y"), lax.axis_size("z")
    core = lax.axis_index("c").astype(jnp.int32).reshape(1)
    scale = 1.0 / math.sqrt(nodes * shards)

    def chip_step(value, sign):
        pairs = [(s, (s + (2 * sign if s % 2 == 0 else -2 * sign)) % shards) for s in range(shards)]
        return lax.ppermute(value, ROWS, pairs)

    def sibling(value):
        return lax.ppermute(value, "c", [(0, 1), (1, 0)])

    permuted = pl.pallas_call(
        into_order,
        out_shape=jax.ShapeDtypeStruct((feat, nodes), BF16),
        in_specs=[VMEM, VMEM],
        out_specs=VMEM,
        compiler_params=PARAMS,
        name="into_order",
    )(node_order, features)

    after = chip_step(permuted, -1)
    before = chip_step(permuted, 1)
    beside = sibling(permuted)
    across = sibling(after)

    hidden = pl.pallas_call(
        aggregate,
        out_shape=jax.ShapeDtypeStruct((parts, feat, width), BF16),
        in_specs=[SMEM] * 4 + [ANY] * 6,
        out_specs=VMEM,
        scratch_shapes=[
            pltpu.VMEM((5, feat, nodes), BF16),
            pltpu.VMEM((slots, BLOCK, BLOCK), BF16),
            pltpu.VMEM((nblocks + 1, feat, BLOCK), F32),
            pltpu.SemaphoreType.DMA((5,)),
            pltpu.SemaphoreType.DMA((slots // CHUNK,)),
        ],
        compiler_params=PARAMS,
        name="aggregate",
    )(blk_dest, blk_src, blk_count, core, before, across, permuted, beside, after, adj_values)

    hidden_rows = lax.all_to_all(hidden, "x", 0, 0).reshape(parts * feat, width)

    output, send = pl.pallas_call(
        dense,
        out_shape=(
            jax.ShapeDtypeStruct((out_feat, width), BF16),
            jax.ShapeDtypeStruct((parts, 2 * feat + 16, width), BF16),
        ),
        in_specs=[VMEM] * 4,
        out_specs=(VMEM, VMEM),
        compiler_params=PARAMS,
        name="dense",
    )(hidden_rows, weight, bias[:, None], cotangent)

    recv = lax.all_to_all(send, "x", 0, 0)

    partial = pl.pallas_call(
        first_sum,
        out_shape=jax.ShapeDtypeStruct((2 * ys, 16, BLOCK), F32),
        in_specs=[VMEM],
        out_specs=VMEM,
        compiler_params=PARAMS,
        name="first_sum",
    )(recv)
    partial = lax.all_to_all(partial, ("y", "c"), 0, 0)
    partial = jnp.sum(partial, axis=0)
    partial = lax.all_to_all(jnp.broadcast_to(partial[None], (zs, 16, BLOCK)), "z", 0, 0)
    partial = jnp.sum(partial, axis=0) * scale
    grad_b = jnp.concatenate([partial[8], partial[12]])
    pieces = lax.all_to_all(jnp.broadcast_to(partial[None, 0:8], (2 * ys, 8, BLOCK)), ("y", "c"), 0, 0)
    pieces = pieces.reshape(ys, 2, 8, BLOCK).transpose(0, 2, 1, 3).reshape(8 * ys, 2 * BLOCK)
    grad_w = lax.all_to_all(jnp.broadcast_to(pieces[None], (parts,) + pieces.shape), "x", 0, 0)
    grad_w = grad_w.reshape(parts * 8 * ys, 2 * BLOCK)

    half = jax.ShapeDtypeStruct((feat, nodes), BF16)
    whole = jax.ShapeDtypeStruct((feat, nodes), F32)
    first, far, near, own, last = pl.pallas_call(
        spread_back,
        out_shape=(half, half, half, whole, whole),
        in_specs=[SMEM] * 4 + [ANY] * 2,
        out_specs=(VMEM,) * 5,
        scratch_shapes=[
            pltpu.VMEM((parts, feat, width), BF16),
            pltpu.VMEM((slots, BLOCK, BLOCK), BF16),
            pltpu.VMEM((5 * nblocks + 1, feat, BLOCK), F32),
            pltpu.SemaphoreType.DMA,
            pltpu.SemaphoreType.DMA((slots // CHUNK,)),
        ],
        compiler_params=PARAMS,
        name="spread_back",
    )(blk_dest, blk_src, blk_count, core, recv, adj_values)

    from_first = chip_step(first, -1)
    far = sibling(far)
    near = sibling(near)
    from_last = chip_step((last + far.astype(F32)).astype(BF16), 1)

    grad_x = pl.pallas_call(
        out_of_order,
        out_shape=jax.ShapeDtypeStruct((feat, nodes), BF16),
        in_specs=[VMEM] * 5,
        out_specs=VMEM,
        scratch_shapes=[pltpu.VMEM((feat, nodes), BF16)],
        compiler_params=PARAMS,
        name="out_of_order",
    )(node_order, own, near, from_first, from_last)
    return output, grad_x, grad_w, grad_b


def solution(mesh):
    rows, cols = mesh.devices.shape
    ys = 8 if rows % 16 == 0 else 2
    devices = mesh.devices.reshape(rows // (2 * ys), ys, 2, cols)
    own = Mesh(devices, ("z", "y", "c", "x"))
    in_specs = (
        P("x", ROWS),
        P(ROWS, None),
        P(ROWS, None, None),
        P(ROWS, None),
        P(ROWS, None),
        P(ROWS),
        P(),
        P(),
        P(None, ROWS + ("x",)),
    )
    out_specs = (P(None, ROWS + ("x",)), P("x", ROWS), P(), P())
    return jax.shard_map(
        on_device, mesh=own, in_specs=in_specs, out_specs=out_specs, check_vma=False
    )
```

time: 601 us -> 128 us (0.21)
  waiting for transfers between devices: 331 us -> 8.9 us
  blocking collectives: 106 us -> 28.3 us
  local copies, waits for them, and re-layouts: 59.6 us -> 14.7 us
  matrix products: 19.7 us -> 0 us
  other arithmetic: 20.9 us -> 1.7 us
  Pallas kernels: 0 us -> 15.4 us
  between operations: 14.9 us -> 1.57 us
  starting transfers between devices: 47.8 us -> 56.6 us
    psum x1 -> x0, waiting for transfers between devices: 313 us -> none  [on_device(): total_w, total_b = lax.psum((local_w, local_b), ('rows', 'cols'))]
    psum x1 -> x0, blocking collectives: 106 us -> none  [on_device(): total_w, total_b = lax.psum((local_w, local_b), ('rows', 'cols'))]
    all_to_all x0 -> x2, blocking collectives: none -> 28.3 us  [the longest x1 18.6 us: on_device(): partial = lax.all_to_all(partial, ('y', 'c'), 0, 0)]
    gather x4 -> x0, local copies, waits for them, and re-layouts: 23 us -> none  [the longest x1 8.81 us: on_device(): permuted = jnp.take(features, order, axis=1)]
    dot_general x7 -> x0, matrix products: 19.7 us -> none  [the longest x1 5.03 us: on_device(): jnp.einsum('obj,jfs->ofbs', src_table, back_products, precision=lax.Preci...]
    pallas_call x0 -> x6, Pallas kernels: none -> 15.4 us  [the longest x1 4.59 us: on_device(): pl.pallas_call(aggregate, out_shape=jax.ShapeDtypeStruct((parts, feat, wi...]
    ppermute x8, waiting for transfers between devices: 12.8 us -> 1.55 us  [the longest x4 1.54 us: chip_step(): return lax.ppermute(value, ROWS, pairs)]
    all_to_all x2 -> x4, starting transfers between devices: 8.05 us -> 18.2 us  [the longest x1 5.97 us: on_device(): lax.all_to_all(jnp.broadcast_to(partial[None, 0:8], (2 * ys, 8, BLOCK)),...]
  transfers between devices with their start and end apart: 11 -> 12, of which waited for: 3 -> 4; matrix products, arithmetic and copies ran while one was open for 8% -> 2% of each run, Pallas kernels for 0% -> 6%
where the time goes in v1:
time: 128 us; the launch traced here: 127 us
  starting transfers between devices  56.6 us (44%)
  blocking collectives  28.3 us (22%)
  Pallas kernels  15.4 us (12%)
  local copies, waits for them, and re-layouts  14.7 us (11%)
  waiting for transfers between devices  8.9 us (7%)
  other arithmetic  1.7 us (1%)
  between operations  1.57 us (1%)
    ppermute x4, starting transfers between devices, sibling(): return lax.ppermute(value, 'c', [(0, 1), (1, 0)])  23.1 us
    all_to_all x1, blocking collectives, on_device(): partial = lax.all_to_all(partial, ('y', 'c'), 0, 0)  18.6 us
    ppermute x4, starting transfers between devices, chip_step(): return lax.ppermute(value, ROWS, pairs)  15.4 us
    unnamed x37, local copies, waits for them, and re-layouts  12.6 us
    all_to_all x1, blocking collectives, on_device(): recv = lax.all_to_all(send, 'x', 0, 0)  9.66 us
    all_to_all x1, starting transfers between devices, on_device(): lax.all_to_all(jnp.broadcast_to(partial[None, 0:8], (2 * ys, 8, BLOCK)),...  5.97 us
    all_to_all x1, waiting for transfers between devices, on_device(): hidden_rows = lax.all_to_all(hidden, 'x', 0, 0).reshape(parts * feat, width)  5.39 us
    pallas_call x1, Pallas kernels, on_device(): pl.pallas_call(aggregate, out_shape=jax.ShapeDtypeStruct((parts, feat, wi...  4.59 us
  transfers between devices with their start and end apart: 12, of which 4 were waited for; matrix products, arithmetic and copies ran while one was open for 2% of the time, Pallas kernels for 6%

profile of v1, /device:TPU:1, one launch (start us, length us, event | category | flops | bytes accessed | tf_op | source)
XLA Modules:
  0.0 127.2 jit_solution(8755132073784085216)
XLA Ops:
  0.6 0.9 copy-done.9
  1.6 0.7 copy-done.11
  2.3 1.6 %into_order.1.w2 = bf16[64,2048]{1,0:T(8,128)(2,1)S(1)} custom-call(s32[1,2048]{1,0:T(1,128)S(1)} %copy-done.11, bf16[64,2048]{1,0:T(8,128)(2,1)S(1)} %copy-done.9), custom_call_target="tpu_custom_call" | custom-call | tf_op jit(solution)/shard_map/into_order/pallas_call | solution.py:205
  3.9 4.0 %collective-permute-start.1 = (bf16[64,2048]{1,0:T(8,128)(2,1)S(1)}, bf16[64,2048]{1,0:T(8,128)(2,1)S(1)}, u32[]{:S(2)}, u32[]{:S(2)}) collective-permute-start(bf16[64,2048]{1,0:T(8,128)(2,1)S(1)} %into_order.1.w2), channel_id=1, source_target_pairs={{0,760},{4,12},{8,0},{12,20},{16,8},{20,28},{24,16},{28,36},{32,24... | collective-permute-start | bytes 786440 | tf_op jit(solution)/shard_map/ppermute | solution.py:200
  7.9 16.9 %collective-permute-start.3 = (bf16[64,2048]{1,0:T(8,128)(2,1)S(1)}, bf16[64,2048]{1,0:T(8,128)(2,1)S(1)}, u32[]{:S(2)}, u32[]{:S(2)}) collective-permute-start(bf16[64,2048]{1,0:T(8,128)(2,1)S(1)} %into_order.1.w2), channel_id=1, source_target_pairs={{0,4},{4,0},{1,5},{5,1},{2,6},{6,2},{3,7},{7,3},{8,12},{12,8},{9,1... | collective-permute-start | bytes 786440 | tf_op jit(solution)/shard_map/ppermute | solution.py:203
  24.8 3.0 %collective-permute-start = (bf16[64,2048]{1,0:T(8,128)(2,1)S(1)}, bf16[64,2048]{1,0:T(8,128)(2,1)S(1)}, u32[]{:S(2)}, u32[]{:S(2)}) collective-permute-start(bf16[64,2048]{1,0:T(8,128)(2,1)S(1)} %into_order.1.w2), channel_id=1, source_target_pairs={{0,8},{4,764},{8,16},{12,4},{16,24},{20,12},{24,32},{28,20},{32,40... | collective-permute-start | bytes 786440 | tf_op jit(solution)/shard_map/ppermute | solution.py:200
  27.8 1.9 %collective-permute-start.2 = (bf16[64,2048]{1,0:T(8,128)(2,1)S(1)}, bf16[64,2048]{1,0:T(8,128)(2,1)S(1)}, u32[]{:S(2)}, u32[]{:S(2)}) collective-permute-start(bf16[64,2048]{1,0:T(8,128)(2,1)S(1)} %collective-permute-done.1.w4), channel_id=1, source_target_pairs={{0,4},{4,0},{1,5},{5,1},{2,6},{6,2},{3,7},{7,3},{8,12},{12,8},{9,1... | collective-permute-start | bytes 786440 | tf_op jit(solution)/shard_map/ppermute | solution.py:203
  30.4 0.0 collective-permute-done.3.w3
  30.4 1.5 %collective-permute-done.w0 = bf16[64,2048]{1,0:T(8,128)(2,1)S(1)} collective-permute-done((bf16[64,2048]{1,0:T(8,128)(2,1)S(1)}, bf16[64,2048]{1,0:T(8,128)(2,1)S(1)}, u32[]{:S(2)}, u32[]{:S(2)}) %collective-permute-start) | collective-permute-done | bytes 262176 | tf_op jit(solution)/shard_map/ppermute | solution.py:200
  31.9 0.0 collective-permute-done.2.w1
  31.9 1.9 %copy-done = bf16[96,128,128]{2,1,0:T(8,128)(2,1)S(1)} copy-done((bf16[96,128,128]{2,1,0:T(8,128)(2,1)S(1)}, bf16[96,128,128]{2,1,0:T(8,128)(2,1)}, u32[]{:S(2)}) %copy-start) | copy-done | bytes 3145752
  33.8 0.7 copy-done.13
  34.5 0.7 copy-done.15
  35.1 4.6 %aggregate.1 = bf16[4,64,512]{2,1,0:T(8,128)(2,1)S(1)} custom-call(s32[1,96]{1,0:T(1,128)S(1)} %copy-done.13, s32[1,96]{1,0:T(1,128)S(1)} %copy-done.15, s32[1]{0:T(128)S(6)} %copy.16.count_ref, s32[1]{0:T(128)} %bitcast.core_ref, bf16[64,2048]{1,0:T(8,128)(2,1)S(1)} %collective-permute-done.w0, bf16[64,2048]{1,0:T(8,128)(2,1)S(1)} %collective-permute-done.2.w1, ...), custom_call_target="tpu_custom_call" | custom-call | tf_op jit(solution)/shard_map/aggregate/pallas_call | solution.py:219
  39.7 0.0 copy-start.4
  39.7 0.7 copy-done.4
  40.4 4.3 %all-to-all-start = ((bf16[4,64,512]{2,1,0:T(8,128)(2,1)}), bf16[4,64,512]{2,1,0:T(8,128)(2,1)S(1)}, u32[]{:S(2)}, u32[]{:S(2)}) async-start(bf16[4,64,512]{2,1,0:T(8,128)(2,1)} %copy-done.4), calls=%async_computation | async-start | bytes 524288 | tf_op jit(solution)/shard_map/all_to_all | solution.py:235
  44.7 0.1 copy.14.bias_ref
  44.8 5.4 %all-to-all-done = bf16[4,64,512]{2,1,0:T(8,128)(2,1)S(1)} async-done(((bf16[4,64,512]{2,1,0:T(8,128)(2,1)}), bf16[4,64,512]{2,1,0:T(8,128)(2,1)S(1)}, u32[]{:S(2)}, u32[]{:S(2)}) %all-to-all-start) | async-done | bytes 262176 | tf_op jit(solution)/shard_map/all_to_all | solution.py:235
  50.2 0.9 copy-done.8
  51.2 0.9 copy-done.10
  52.1 1.2 dense.1
  53.3 9.7 %all_to_all.30.recv_ref = bf16[4,144,512]{2,1,0:T(8,128)(2,1)S(1)} all-to-all(bf16[4,144,512]{2,1,0:T(8,128)(2,1)S(1)} %get-tuple-element.12), channel_id=1, replica_groups=mesh['z'=12,'y'=8,'c'=2,'x'=4] {'x'}, dimensions={0} | all-to-all | bytes 1179648 | tf_op jit(solution)/shard_map/all_to_all | solution.py:249
  63.0 0.8 copy-done.2
  63.9 18.6 %all_to_all.31 = f32[16,16,128]{2,1,0:T(8,128)S(1)} all-to-all(f32[16,16,128]{2,1,0:T(8,128)S(1)} %first_sum.1), channel_id=1, replica_groups=mesh['z'=12,'y'=8,'c'=2,'x'=4] {'y','c'}, dimensions={0} | all-to-all | bytes 262144 | tf_op jit(solution)/shard_map/all_to_all | solution.py:259
  82.5 0.0 copy-start.12
  82.5 0.6 broadcast_in_dim.11
  83.1 4.5 %all-to-all-start.3 = ((f32[12,16,128]{2,1,0:T(8,128)}), f32[12,16,128]{2,1,0:T(8,128)S(1)}, u32[]{:S(2)}, u32[]{:S(2)}) async-start(f32[12,16,128]{2,1,0:T(8,128)} %broadcast_in_dim.11), calls=%async_computation.3 | async-start | bytes 196608 | tf_op jit(solution)/shard_map/all_to_all | solution.py:261
  87.7 1.1 copy-done.3
  88.7 4.6 %spread_back.1 = (bf16[64,2048]{1,0:T(8,128)(2,1)S(1)}, bf16[64,2048]{1,0:T(8,128)(2,1)}, bf16[64,2048]{1,0:T(8,128)(2,1)}, f32[64,2048]{1,0:T(8,128)S(1)}, f32[64,2048]{1,0:T(8,128)S(1)}) custom-call(s32[1,96]{1,0:T(1,128)S(1)} %copy-done.14, s32[1,96]{1,0:T(1,128)S(1)} %copy-done.16, s32[1]{0:T(128)S(6)} %copy.16.count_ref, s32[1]{0:T(128)} %bitcast.core_ref, ...), custom_call_target="tpu_custom_call" | custom-call | tf_op jit(solution)/shard_map/spread_back/pallas_call | solution.py:271
  93.3 0.8 copy-done.5
  94.1 0.8 copy-done.7
  94.9 1.9 %collective-permute-start.6 = (bf16[64,2048]{1,0:T(8,128)(2,1)}, bf16[64,2048]{1,0:T(8,128)(2,1)S(1)}, u32[]{:S(2)}, u32[]{:S(2)}) collective-permute-start(bf16[64,2048]{1,0:T(8,128)(2,1)} %get-tuple-element.17), channel_id=1, source_target_pairs={{0,4},{4,0},{1,5},{5,1},{2,6},{6,2},{3,7},{7,3},{8,12},{12,8},{9,1... | collective-permute-start | bytes 786440 | tf_op jit(solution)/shard_map/ppermute | solution.py:203
  96.9 2.4 %collective-permute-start.4 = (bf16[64,2048]{1,0:T(8,128)(2,1)}, bf16[64,2048]{1,0:T(8,128)(2,1)S(1)}, u32[]{:S(2)}, u32[]{:S(2)}) collective-permute-start(bf16[64,2048]{1,0:T(8,128)(2,1)} %get-tuple-element.14), channel_id=1, source_target_pairs={{0,4},{4,0},{1,5},{5,1},{2,6},{6,2},{3,7},{7,3},{8,12},{12,8},{9,1... | collective-permute-start | bytes 786440 | tf_op jit(solution)/shard_map/ppermute | solution.py:203
  99.3 2.0 %collective-permute-start.5 = (bf16[64,2048]{1,0:T(8,128)(2,1)S(1)}, bf16[64,2048]{1,0:T(8,128)(2,1)S(1)}, u32[]{:S(2)}, u32[]{:S(2)}) collective-permute-start(bf16[64,2048]{1,0:T(8,128)(2,1)S(1)} %get-tuple-element.15), channel_id=1, source_target_pairs={{0,760},{4,12},{8,0},{12,20},{16,8},{20,28},{24,16},{28,36},{32,24... | collective-permute-start | bytes 786440 | tf_op jit(solution)/shard_map/ppermute | solution.py:200
  101.2 0.0 all-to-all-done.3
  101.3 0.6 broadcast_in_dim.24
  101.9 6.0 %all-to-all-start.4 = ((f32[16,8,128]{2,1,0:T(8,128)}), f32[16,8,128]{2,1,0:T(8,128)S(1)}, u32[]{:S(2)}, u32[]{:S(2)}) async-start(f32[16,8,128]{2,1,0:T(8,128)} %broadcast_in_dim.24), calls=%async_computation.4 | async-start | bytes 131072 | tf_op jit(solution)/shard_map/all_to_all | solution.py:264
  107.9 1.1 add_convert_fusion
  109.0 6.4 %collective-permute-start.7 = (bf16[64,2048]{1,0:T(8,128)(2,1)S(1)}, bf16[64,2048]{1,0:T(8,128)(2,1)S(1)}, u32[]{:S(2)}, u32[]{:S(2)}) collective-permute-start(bf16[64,2048]{1,0:T(8,128)(2,1)S(1)} %add_convert_fusion), channel_id=1, source_target_pairs={{0,8},{4,764},{8,16},{12,4},{16,24},{20,12},{24,32},{28,20},{32,40... | collective-permute-start | bytes 786440 | tf_op jit(solution)/shard_map/ppermute | solution.py:200
  115.4 0.3 all-to-all-done.4
  115.7 0.7 broadcast_in_dim.26
  116.5 3.4 %all-to-all-start.5 = ((f32[4,64,256]{2,1,0:T(8,128)}), f32[4,64,256]{2,1,0:T(8,128)S(1)}, u32[]{:S(2)}, u32[]{:S(2)}) async-start(f32[4,64,256]{2,1,0:T(8,128)} %broadcast_in_dim.26), calls=%async_computation.5 | async-start | bytes 524288 | tf_op jit(solution)/shard_map/all_to_all | solution.py:266
  119.9 0.6 pad_maximum_fusion
  120.5 1.0 copy-done.6
  121.5 3.3 %out_of_order.1 = bf16[64,2048]{1,0:T(8,128)(2,1)} custom-call(s32[1,2048]{1,0:T(1,128)S(1)} %copy-done.12, f32[64,2048]{1,0:T(8,128)S(1)} %copy-done.6, bf16[64,2048]{1,0:T(8,128)(2,1)S(1)} %collective-permute-done.4.near_ref, bf16[64,2048]{1,0:T(8,128)(2,1)S(1)} %collective-permute-done.5.first_ref, bf16[64,2048]{1,0:T(8,128)(2,1)S(1)} %collective-permute-done.7.second_ref), custom_call_target="tpu_custom_call" | custom-call | tf_op jit(solution)/shard_map/out_of_order/pallas_call | solution.py:292
  124.9 1.6 %all-to-all-done.5 = f32[4,64,256]{2,1,0:T(8,128)S(1)} async-done(((f32[4,64,256]{2,1,0:T(8,128)}), f32[4,64,256]{2,1,0:T(8,128)S(1)}, u32[]{:S(2)}, u32[]{:S(2)}) %all-to-all-start.5) | async-done | bytes 262176 | tf_op jit(solution)/shard_map/all_to_all | solution.py:266
  126.5 0.7 copy.17
  (32 shorter events, 0.1 us)
Async XLA Ops:
  0.6 1.0 copy-start.9
  1.6 0.7 copy-start.11
  2.3 42.4 %copy-start.17 = (f32[256]{0:T(256)S(1)}, f32[256]{0:T(256)}, u32[]{:S(2)}) copy-start(f32[256]{0:T(256)} %param.16) | copy-start | bytes 3076
  3.9 23.9 %collective-permute-start.1 = (bf16[64,2048]{1,0:T(8,128)(2,1)S(1)}, bf16[64,2048]{1,0:T(8,128)(2,1)S(1)}, u32[]{:S(2)}, u32[]{:S(2)}) collective-permute-start(bf16[64,2048]{1,0:T(8,128)(2,1)S(1)} %into_order.1.w2), channel_id=1, source_target_pairs={{0,760},{4,12},{8,0},{12,20},{16,8},{20,28},{24,16},{28,36},{32,24... | collective-permute-start | bytes 786440 | tf_op jit(solution)/shard_map/ppermute | solution.py:200
  7.9 22.5 %collective-permute-start.3 = (bf16[64,2048]{1,0:T(8,128)(2,1)S(1)}, bf16[64,2048]{1,0:T(8,128)(2,1)S(1)}, u32[]{:S(2)}, u32[]{:S(2)}) collective-permute-start(bf16[64,2048]{1,0:T(8,128)(2,1)S(1)} %into_order.1.w2), channel_id=1, source_target_pairs={{0,4},{4,0},{1,5},{5,1},{2,6},{6,2},{3,7},{7,3},{8,12},{12,8},{9,1... | collective-permute-start | bytes 786440 | tf_op jit(solution)/shard_map/ppermute | solution.py:203
  24.8 7.1 %collective-permute-start = (bf16[64,2048]{1,0:T(8,128)(2,1)S(1)}, bf16[64,2048]{1,0:T(8,128)(2,1)S(1)}, u32[]{:S(2)}, u32[]{:S(2)}) collective-permute-start(bf16[64,2048]{1,0:T(8,128)(2,1)S(1)} %into_order.1.w2), channel_id=1, source_target_pairs={{0,8},{4,764},{8,16},{12,4},{16,24},{20,12},{24,32},{28,20},{32,40... | collective-permute-start | bytes 786440 | tf_op jit(solution)/shard_map/ppermute | solution.py:200
  27.8 4.1 %collective-permute-start.2 = (bf16[64,2048]{1,0:T(8,128)(2,1)S(1)}, bf16[64,2048]{1,0:T(8,128)(2,1)S(1)}, u32[]{:S(2)}, u32[]{:S(2)}) collective-permute-start(bf16[64,2048]{1,0:T(8,128)(2,1)S(1)} %collective-permute-done.1.w4), channel_id=1, source_target_pairs={{0,4},{4,0},{1,5},{5,1},{2,6},{6,2},{3,7},{7,3},{8,12},{12,8},{9,1... | collective-permute-start | bytes 786440 | tf_op jit(solution)/shard_map/ppermute | solution.py:203
  31.9 1.9 %copy-start = (bf16[96,128,128]{2,1,0:T(8,128)(2,1)S(1)}, bf16[96,128,128]{2,1,0:T(8,128)(2,1)}, u32[]{:S(2)}) copy-start(bf16[96,128,128]{2,1,0:T(8,128)(2,1)} %adj_ref.3) | copy-start | bytes 9437188
  33.8 0.7 copy-start.13
  34.5 0.7 copy-start.15
  35.1 52.5 %copy-start.14 = (s32[1,96]{1,0:T(1,128)S(1)}, s32[1,96]{1,0:T(1,128)}, u32[]{:S(2)}) copy-start(s32[1,96]{1,0:T(1,128)} %dest_ref.3) | copy-start | bytes 1156
  35.1 52.5 %copy-start.16 = (s32[1,96]{1,0:T(1,128)S(1)}, s32[1,96]{1,0:T(1,128)}, u32[]{:S(2)}) copy-start(s32[1,96]{1,0:T(1,128)} %src_ref.3) | copy-start | bytes 1156
  39.7 0.7 copy-start.4
  40.4 47.2 %copy-start.1 = (bf16[96,128,128]{2,1,0:T(8,128)(2,1)S(1)}, bf16[96,128,128]{2,1,0:T(8,128)(2,1)}, u32[]{:S(2)}) copy-start(bf16[96,128,128]{2,1,0:T(8,128)(2,1)} %adj_ref.3) | copy-start | bytes 9437188
  40.4 9.8 %all-to-all-start = ((bf16[4,64,512]{2,1,0:T(8,128)(2,1)}), bf16[4,64,512]{2,1,0:T(8,128)(2,1)S(1)}, u32[]{:S(2)}, u32[]{:S(2)}) async-start(bf16[4,64,512]{2,1,0:T(8,128)(2,1)} %copy-done.4), calls=%async_computation | async-start | bytes 524288 | tf_op jit(solution)/shard_map/all_to_all | solution.py:235
  50.2 1.0 copy-start.8
  51.2 0.9 copy-start.10
  63.0 0.8 copy-start.2
  82.5 38.0 %copy-start.12 = (s32[1,2048]{1,0:T(1,128)S(1)}, s32[1,2048]{1,0:T(1,128)}, u32[]{:S(2)}) copy-start(s32[1,2048]{1,0:T(1,128)} %order_ref.3) | copy-start | bytes 24580
  83.1 18.1 %all-to-all-start.3 = ((f32[12,16,128]{2,1,0:T(8,128)}), f32[12,16,128]{2,1,0:T(8,128)S(1)}, u32[]{:S(2)}, u32[]{:S(2)}) async-start(f32[12,16,128]{2,1,0:T(8,128)} %broadcast_in_dim.11), calls=%async_computation.3 | async-start | bytes 196608 | tf_op jit(solution)/shard_map/all_to_all | solution.py:261
  87.7 1.1 copy-start.3
  93.3 0.8 copy-start.5
  94.1 0.8 copy-start.7
  94.9 12.9 %collective-permute-start.6 = (bf16[64,2048]{1,0:T(8,128)(2,1)}, bf16[64,2048]{1,0:T(8,128)(2,1)S(1)}, u32[]{:S(2)}, u32[]{:S(2)}) collective-permute-start(bf16[64,2048]{1,0:T(8,128)(2,1)} %get-tuple-element.17), channel_id=1, source_target_pairs={{0,4},{4,0},{1,5},{5,1},{2,6},{6,2},{3,7},{7,3},{8,12},{12,8},{9,1... | collective-permute-start | bytes 786440 | tf_op jit(solution)/shard_map/ppermute | solution.py:203
  96.9 23.6 %collective-permute-start.4 = (bf16[64,2048]{1,0:T(8,128)(2,1)}, bf16[64,2048]{1,0:T(8,128)(2,1)S(1)}, u32[]{:S(2)}, u32[]{:S(2)}) collective-permute-start(bf16[64,2048]{1,0:T(8,128)(2,1)} %get-tuple-element.14), channel_id=1, source_target_pairs={{0,4},{4,0},{1,5},{5,1},{2,6},{6,2},{3,7},{7,3},{8,12},{12,8},{9,1... | collective-permute-start | bytes 786440 | tf_op jit(solution)/shard_map/ppermute | solution.py:203
  99.3 21.2 %collective-permute-start.5 = (bf16[64,2048]{1,0:T(8,128)(2,1)S(1)}, bf16[64,2048]{1,0:T(8,128)(2,1)S(1)}, u32[]{:S(2)}, u32[]{:S(2)}) collective-permute-start(bf16[64,2048]{1,0:T(8,128)(2,1)S(1)} %get-tuple-element.15), channel_id=1, source_target_pairs={{0,760},{4,12},{8,0},{12,20},{16,8},{20,28},{24,16},{28,36},{32,24... | collective-permute-start | bytes 786440 | tf_op jit(solution)/shard_map/ppermute | solution.py:200
  101.9 13.8 %all-to-all-start.4 = ((f32[16,8,128]{2,1,0:T(8,128)}), f32[16,8,128]{2,1,0:T(8,128)S(1)}, u32[]{:S(2)}, u32[]{:S(2)}) async-start(f32[16,8,128]{2,1,0:T(8,128)} %broadcast_in_dim.24), calls=%async_computation.4 | async-start | bytes 131072 | tf_op jit(solution)/shard_map/all_to_all | solution.py:264
  109.0 11.5 %collective-permute-start.7 = (bf16[64,2048]{1,0:T(8,128)(2,1)S(1)}, bf16[64,2048]{1,0:T(8,128)(2,1)S(1)}, u32[]{:S(2)}, u32[]{:S(2)}) collective-permute-start(bf16[64,2048]{1,0:T(8,128)(2,1)S(1)} %add_convert_fusion), channel_id=1, source_target_pairs={{0,8},{4,764},{8,16},{12,4},{16,24},{20,12},{24,32},{28,20},{32,40... | collective-permute-start | bytes 786440 | tf_op jit(solution)/shard_map/ppermute | solution.py:200
  116.5 10.0 %all-to-all-start.5 = ((f32[4,64,256]{2,1,0:T(8,128)}), f32[4,64,256]{2,1,0:T(8,128)S(1)}, u32[]{:S(2)}, u32[]{:S(2)}) async-start(f32[4,64,256]{2,1,0:T(8,128)} %broadcast_in_dim.26), calls=%async_computation.5 | async-start | bytes 524288 | tf_op jit(solution)/shard_map/all_to_all | solution.py:266
  120.5 1.0 copy-start.6

commit v2 on v1

v2 whole, which is shorter than its diff:
```python
import math

import jax
import jax.numpy as jnp
from jax import lax
from jax.experimental import pallas as pl
from jax.experimental.pallas import tpu as pltpu
from jax.sharding import Mesh, PartitionSpec as P

BF16 = jnp.bfloat16
F32 = jnp.float32
BLOCK = 128
TILE = 256
ROWS = ("z", "y", "c")
CHUNK = 8
VMEM = pl.BlockSpec(memory_space=pltpu.VMEM)
SMEM = pl.BlockSpec(memory_space=pltpu.SMEM)
HBM = pl.BlockSpec(memory_space=pltpu.HBM)
ANY = pl.BlockSpec(memory_space=pl.ANY)
PARAMS = pltpu.CompilerParams(vmem_limit_bytes=40 * 1024 * 1024)


def in_hbm(*arrays):
    return tuple(pltpu.with_memory_space_constraint(array, pltpu.HBM) for array in arrays)


def cost(flops, size):
    return pl.CostEstimate(flops=flops, bytes_accessed=size, transcendentals=0)


def started(pairs, sems):
    copies = [pltpu.make_async_copy(a, b, sems.at[i]) for i, (a, b) in enumerate(pairs)]
    for copy in copies:
        copy.start()
    return copies


def into_order(order_hbm, x_hbm, adj_hbm, out_ref, adj_ref, order, x, sems):
    copies = started([(x_hbm, x), (order_hbm, order), (adj_hbm, adj_ref)], sems)
    copies[0].wait()
    copies[1].wait()
    count = x.shape[1]
    for start in range(0, count, TILE):
        rows = lax.broadcasted_iota(jnp.int32, (count, TILE), 0)
        hot = jnp.where(order[:, start : start + TILE] == rows, 1.0, 0.0).astype(BF16)
        moved = jnp.dot(x[...], hot, preferred_element_type=F32)
        out_ref[:, start : start + TILE] = moved.astype(BF16)
    copies[2].wait()


def out_of_order(
    order_hbm, own_hbm, first_hbm, pair_hbm, last_hbm, out_ref, order, own, first, near, last, total, sems
):
    copies = started(
        [
            (last_hbm, last),
            (first_hbm, first),
            (pair_hbm.at[1], near),
            (own_hbm, own),
            (order_hbm, order),
        ],
        sems,
    )
    for copy in copies:
        copy.wait()
    count = own.shape[1]
    sums = own[...] + near[...].astype(F32) + first[...].astype(F32) + last[...].astype(F32)
    total[...] = sums.astype(BF16)
    for start in range(0, count, TILE):
        rows = lax.broadcasted_iota(jnp.int32, (TILE, count), 0) + start
        hot = jnp.where(order[...] == rows, 1.0, 0.0).astype(BF16)
        moved = lax.dot_general(
            total[...], hot, (((1,), (1,)), ((), ())), preferred_element_type=F32
        )
        out_ref[:, start : start + TILE] = moved.astype(BF16)


def mirrored(source, core, nblocks, spread):
    offset = source // nblocks
    return jnp.where(core == 0, offset, spread - 1 - offset), source % nblocks


def aggregate(
    count_ref, dest_hbm, src_hbm, w0, w1, w2, w3, w4, adj, out_ref, dest, src, win, acc, sems
):
    slots = adj.shape[0]
    nblocks = acc.shape[0] - 1
    spread = win.shape[0]
    quarter = out_ref.shape[2] // BLOCK
    windows = [(ref, win.at[i]) for i, ref in enumerate((w0, w1, w2, w3, w4))]
    copies = started([(dest_hbm, dest), (src_hbm, src)] + windows, sems)
    acc[...] = jnp.zeros_like(acc)
    for copy in copies:
        copy.wait()
    core = lax.axis_index("c")
    count = count_ref[0]
    for begin in range(0, slots, CHUNK):
        products = []
        for j in range(begin, begin + CHUNK):
            offset, block = mirrored(src[0, j], core, nblocks, spread)
            picked = win[offset, :, pl.ds(pl.multiple_of(block * BLOCK, BLOCK), BLOCK)]
            products.append(
                lax.dot_general(
                    picked, adj[j], (((1,), (1,)), ((), ())), preferred_element_type=F32
                )
            )
        for j, product in zip(range(begin, begin + CHUNK), products):
            target = jnp.where(j < count, dest[0, j], nblocks)
            acc[target] += product
    for block in range(nblocks):
        lane = (block % quarter) * BLOCK
        out_ref[block // quarter, :, lane : lane + BLOCK] = acc[block].astype(BF16)


def dense(hidden_ref, weight_hbm, bias_hbm, cot_hbm, out_ref, send_ref, weight_v, bias_v, cot, sems):
    copies = started([(weight_hbm, weight_v), (bias_hbm, bias_v), (cot_hbm, cot)], sems)
    feat, width = hidden_ref.shape
    part = send_ref.shape[0]
    rows = feat // part
    hidden = hidden_ref[...]
    copies[0].wait()
    copies[1].wait()
    weight = weight_v[...]
    bias = jnp.broadcast_to(bias_v[...], (BLOCK, bias_v.shape[1])).T
    bias = jnp.concatenate([bias] * (width // BLOCK), axis=1)
    v = (
        lax.dot_general(weight, hidden, (((0,), (0,)), ((), ())), preferred_element_type=F32)
        + bias
    )
    root = math.sqrt(2.0 / math.pi)
    square = v * v
    t = jnp.tanh(root * (v + 0.044715 * (square * v)))
    half = 0.5 * (1.0 + t)
    out_ref[...] = (v * half).astype(BF16)
    slope = half + (0.5 * root) * v * (1.0 - t * t) * (1.0 + (3.0 * 0.044715) * square)
    copies[2].wait()
    grad = (cot[...].astype(F32) * slope).astype(BF16)
    back = jnp.dot(weight, grad, preferred_element_type=F32).astype(BF16)
    grad_w = lax.dot_general(hidden, grad, (((1,), (1,)), ((), ())), preferred_element_type=F32)
    ones = jnp.ones((16, width), BF16)
    grad_b = lax.dot_general(ones, grad, (((1,), (1,)), ((), ())), preferred_element_type=F32)
    high_w = grad_w.astype(BF16)
    low_w = (grad_w - high_w.astype(F32)).astype(BF16)
    high_b = grad_b.astype(BF16)
    low_b = (grad_b - high_b.astype(F32)).astype(BF16)
    half_width = grad_w.shape[1]
    for i in range(part):
        span = slice(i * rows, (i + 1) * rows)
        send_ref[i, 0:rows, :] = back[span]
        send_ref[i, rows : 2 * rows, 0:half_width] = high_w[span]
        send_ref[i, rows : 2 * rows, half_width:] = low_w[span]
        send_ref[i, 2 * rows :, 0:half_width] = high_b
        send_ref[i, 2 * rows :, half_width:] = low_b


def first_sum(recv_hbm, out_hbm, recv, out, sems):
    rows = recv.shape[1] - 16
    half_width = recv.shape[2] // 2
    started([(recv_hbm.at[:, pl.ds(rows, rows + 16), :], recv)], sems)[0].wait()
    total = jnp.zeros((rows + 16, half_width), F32)
    for i in range(recv.shape[0]):
        total = total + recv[i, :, 0:half_width].astype(F32)
        total = total + recv[i, :, half_width:].astype(F32)
    for i in range(out.shape[0] // 2):
        for c in range(2):
            lane = slice(c * BLOCK, (c + 1) * BLOCK)
            out[2 * i + c, 0:8, :] = total[8 * i : 8 * i + 8, lane]
            out[2 * i + c, 8:12, :] = total[rows : rows + 4, 0:BLOCK]
            out[2 * i + c, 12:16, :] = total[rows : rows + 4, BLOCK : 2 * BLOCK]
    started([(out, out_hbm)], sems)[0].wait()


def spread_back(
    count_ref, dest_hbm, src_hbm, recv_hbm, adj_hbm,
    first_hbm, pair_hbm, own_hbm, last_hbm, token_ref,
    dest, src, grad, adj, acc, first, pair, own, last, sems, adj_sems,
):
    slots = adj.shape[0]
    rows = grad.shape[1]
    quarter = grad.shape[2] // BLOCK
    nblocks = grad.shape[0] * quarter
    spread = (acc.shape[0] - 1) // nblocks
    copies = started(
        [(dest_hbm, dest), (src_hbm, src), (recv_hbm.at[:, pl.ds(0, rows), :], grad)], sems
    )
    spans = [pl.ds(begin, CHUNK) for begin in range(0, slots, CHUNK)]
    adj_copies = started([(adj_hbm.at[span], adj.at[span]) for span in spans], adj_sems)
    acc[...] = jnp.zeros_like(acc)
    core = lax.axis_index("c")
    count = count_ref[0]
    for copy in copies:
        copy.wait()
    for index, copy in enumerate(adj_copies):
        copy.wait()
        products = []
        for j in range(index * CHUNK, (index + 1) * CHUNK):
            target = dest[0, j]
            lane = pl.multiple_of((target % quarter) * BLOCK, BLOCK)
            picked = grad[target // quarter, :, pl.ds(lane, BLOCK)]
            products.append(jnp.dot(picked, adj[j], preferred_element_type=F32))
        for j, product in zip(range(index * CHUNK, (index + 1) * CHUNK), products):
            offset, block = mirrored(src[0, j], core, nblocks, spread)
            place = jnp.where(j < count, offset * nblocks + block, spread * nblocks)
            acc[place] += product
    outs = []
    for offset, ref, target in (
        (1, pair.at[0], None),
        (3, pair.at[1], pair_hbm),
        (0, first, first_hbm),
        (4, last, last_hbm),
        (2, own, own_hbm),
    ):
        for block in range(nblocks):
            lane = slice(block * BLOCK, (block + 1) * BLOCK)
            ref[:, lane] = acc[offset * nblocks + block].astype(ref.dtype)
        if target is not None:
            source = pair if target is pair_hbm else ref
            copy = pltpu.make_async_copy(source, target, sems.at[3 + len(outs)])
            copy.start()
            outs.append(copy)
    token_ref[...] = jnp.zeros_like(token_ref)
    for copy in outs:
        copy.wait()


def on_device(
    features, node_order, adj_values, blk_dest, blk_src, blk_count, weight, bias, cotangent
):
    feat, nodes = features.shape
    slots = adj_values.shape[0]
    nblocks = nodes // BLOCK
    parts = lax.axis_size("x")
    out_feat, width = cotangent.shape
    shards = lax.axis_size(ROWS)
    ys, zs = lax.axis_size("y"), lax.axis_size("z")
    scale = 1.0 / math.sqrt(nodes * shards)

    def chip_step(value, sign):
        pairs = [(s, (s + (2 * sign if s % 2 == 0 else -2 * sign)) % shards) for s in range(shards)]
        return lax.ppermute(value, ROWS, pairs)

    def sibling(value):
        return lax.ppermute(value, "c", [(0, 1), (1, 0)])

    slab = jax.ShapeDtypeStruct((feat, nodes), BF16)
    dma = pltpu.SemaphoreType.DMA

    permuted, adj = pl.pallas_call(
        into_order,
        out_shape=(slab, jax.ShapeDtypeStruct(adj_values.shape, BF16)),
        in_specs=[HBM] * 3,
        out_specs=(VMEM, VMEM),
        scratch_shapes=[
            pltpu.VMEM((1, nodes), jnp.int32),
            pltpu.VMEM((feat, nodes), BF16),
            dma((3,)),
        ],
        compiler_params=PARAMS,
        cost_estimate=cost(10**9, 2**20),
        name="into_order",
    )(*in_hbm(node_order, features, adj_values))

    after = chip_step(permuted, -1)
    before = chip_step(permuted, 1)
    beside = sibling(permuted)
    across = sibling(after)

    hidden = pl.pallas_call(
        aggregate,
        out_shape=jax.ShapeDtypeStruct((parts, feat, width), BF16),
        in_specs=[SMEM] + [HBM] * 2 + [VMEM] * 6,
        out_specs=VMEM,
        scratch_shapes=[
            pltpu.SMEM((1, slots), jnp.int32),
            pltpu.SMEM((1, slots), jnp.int32),
            pltpu.VMEM((5, feat, nodes), BF16),
            pltpu.VMEM((nblocks + 1, feat, BLOCK), F32),
            dma((7,)),
        ],
        compiler_params=PARAMS,
        cost_estimate=cost(4 * 10**9, 2**22),
        name="aggregate",
    )(blk_count, *in_hbm(blk_dest, blk_src), before, across, permuted, beside, after, adj)

    hidden_rows = lax.all_to_all(hidden, "x", 0, 0).reshape(parts * feat, width)

    output, send = pl.pallas_call(
        dense,
        out_shape=(
            jax.ShapeDtypeStruct((out_feat, width), BF16),
            jax.ShapeDtypeStruct((parts, 2 * feat + 16, width), BF16),
        ),
        in_specs=[VMEM] + [HBM] * 3,
        out_specs=(VMEM, VMEM),
        scratch_shapes=[
            pltpu.VMEM(weight.shape, BF16),
            pltpu.VMEM((1, out_feat), F32),
            pltpu.VMEM((out_feat, width), BF16),
            dma((3,)),
        ],
        compiler_params=PARAMS,
        cost_estimate=cost(10**9, 2**20),
        name="dense",
    )(hidden_rows, *in_hbm(weight, bias[None, :], cotangent))

    recv = lax.all_to_all(send, "x", 0, 0)

    partial = pl.pallas_call(
        first_sum,
        out_shape=pltpu.HBM((2 * ys, 16, BLOCK), F32),
        in_specs=[HBM],
        out_specs=HBM,
        scratch_shapes=[
            pltpu.VMEM((parts, feat + 16, width), BF16),
            pltpu.VMEM((2 * ys, 16, BLOCK), F32),
            dma((1,)),
        ],
        compiler_params=PARAMS,
        cost_estimate=cost(10**9, 2**20),
        name="first_sum",
    )(*in_hbm(recv))
    partial = lax.all_to_all(partial, ("y", "c"), 0, 0)

    first, pair, own, last, token = pl.pallas_call(
        spread_back,
        out_shape=(
            pltpu.HBM((feat, nodes), BF16),
            pltpu.HBM((2, feat, nodes), BF16),
            pltpu.HBM((feat, nodes), F32),
            pltpu.HBM((feat, nodes), F32),
            jax.ShapeDtypeStruct((8, BLOCK), F32),
        ),
        in_specs=[SMEM] + [HBM] * 4,
        out_specs=(HBM,) * 4 + (VMEM,),
        scratch_shapes=[
            pltpu.SMEM((1, slots), jnp.int32),
            pltpu.SMEM((1, slots), jnp.int32),
            pltpu.VMEM((parts, feat, width), BF16),
            pltpu.VMEM((slots, BLOCK, BLOCK), BF16),
            pltpu.VMEM((5 * nblocks + 1, feat, BLOCK), F32),
            pltpu.VMEM((feat, nodes), BF16),
            pltpu.VMEM((2, feat, nodes), BF16),
            pltpu.VMEM((feat, nodes), F32),
            pltpu.VMEM((feat, nodes), F32),
            dma((7,)),
            dma((slots // CHUNK,)),
        ],
        compiler_params=PARAMS,
        cost_estimate=cost(4 * 10**9, 2**22),
        name="spread_back",
    )(blk_count, *in_hbm(blk_dest, blk_src, recv, adj_values))

    pair = sibling(pair)
    from_first = chip_step(first, -1)
    last = (last + pair[0].astype(F32)).astype(BF16)
    from_last = chip_step(last, 1)

    partial = lax.optimization_barrier((jnp.sum(partial, axis=0), token))[0]
    partial = lax.all_to_all(jnp.broadcast_to(partial[None], (zs, 16, BLOCK)), "z", 0, 0)
    partial = lax.optimization_barrier((jnp.sum(partial, axis=0) * scale, last))[0]
    grad_b = jnp.concatenate([partial[8], partial[12]])
    pieces = lax.all_to_all(jnp.broadcast_to(partial[None, 0:8], (2 * ys, 8, BLOCK)), ("y", "c"), 0, 0)
    pieces = pieces.reshape(ys, 2, 8, BLOCK).transpose(0, 2, 1, 3).reshape(8 * ys, 2 * BLOCK)
    grad_w = lax.all_to_all(jnp.broadcast_to(pieces[None], (parts,) + pieces.shape), "x", 0, 0)
    grad_w = grad_w.reshape(parts * 8 * ys, 2 * BLOCK)

    grad_x = pl.pallas_call(
        out_of_order,
        out_shape=slab,
        in_specs=[HBM] * 2 + [ANY] * 3,
        out_specs=VMEM,
        scratch_shapes=[
            pltpu.VMEM((1, nodes), jnp.int32),
            pltpu.VMEM((feat, nodes), F32),
            pltpu.VMEM((feat, nodes), BF16),
            pltpu.VMEM((feat, nodes), BF16),
            pltpu.VMEM((feat, nodes), BF16),
            pltpu.VMEM((feat, nodes), BF16),
            dma((5,)),
        ],
        compiler_params=PARAMS,
        cost_estimate=cost(3 * 10**9, 2**21),
        name="out_of_order",
    )(*in_hbm(node_order, own), from_first, pair, from_last)
    return output, grad_x, grad_w, grad_b


def solution(mesh):
    rows, cols = mesh.devices.shape
    ys = 8 if rows % 16 == 0 else 2
    devices = mesh.devices.reshape(rows // (2 * ys), ys, 2, cols)
    own = Mesh(devices, ("z", "y", "c", "x"))
    in_specs = (
        P("x", ROWS),
        P(ROWS, None),
        P(ROWS, None, None),
        P(ROWS, None),
        P(ROWS, None),
        P(ROWS),
        P(),
        P(),
        P(None, ROWS + ("x",)),
    )
    out_specs = (P(None, ROWS + ("x",)), P("x", ROWS), P(), P())
    return jax.shard_map(
        on_device, mesh=own, in_specs=in_specs, out_specs=out_specs, check_vma=False
    )
```

time: 128 us -> 125 us (0.977)
  local copies, waits for them, and re-layouts: 14.7 us -> 2.71 us
  waiting for transfers between devices: 8.9 us -> 19.4 us
  blocking collectives: 28.3 us -> 19.7 us
  Pallas kernels: 15.4 us -> 19.9 us
  starting transfers between devices: 56.6 us -> 58.8 us
    unnamed x37 -> x1, local copies, waits for them, and re-layouts: 12.6 us -> 0.7 us
    all_to_all x1, blocking collectives: 18.6 us -> 9.34 us  [on_device(): hidden_rows = lax.all_to_all(hidden, 'x', 0, 0).reshape(parts * feat, width)]
    all_to_all x1, waiting for transfers between devices: 0.01 us -> 7.82 us  [on_device(): lax.all_to_all(jnp.broadcast_to(partial[None], (zs, 16, BLOCK)), 'z', 0, 0)]
    all_to_all x1, waiting for transfers between devices: 0.33 us -> 7.23 us  [on_device(): lax.all_to_all(jnp.broadcast_to(partial[None, 0:8], (2 * ys, 8, BLOCK)),...]
    all_to_all x1, starting transfers between devices: 4.27 us -> 10.4 us  [on_device(): partial = lax.all_to_all(partial, ('y', 'c'), 0, 0)]
    pallas_call x4, Pallas kernels: 9.55 us -> 15.1 us  [the longest x1 6.37 us: on_device(): pl.pallas_call(spread_back, out_shape=(pltpu.HBM((feat, nodes), BF16), pl...]
    all_to_all x1, waiting for transfers between devices: 5.39 us -> 0.67 us  [on_device(): partial = lax.all_to_all(partial, ('y', 'c'), 0, 0)]
    ppermute x4 -> x3, starting transfers between devices: 23.1 us -> 20.9 us  [sibling(): return lax.ppermute(value, 'c', [(0, 1), (1, 0)])]
  transfers between devices with their start and end apart: 12 -> 11, of which waited for: 4 -> 5; matrix products, arithmetic and copies ran while one was open for 2% -> 3% of each run, Pallas kernels for 6% -> 9%
where the time goes in v2:
time: 125 us; the launch traced here: 124 us
  starting transfers between devices  58.8 us (47%)
  Pallas kernels  19.9 us (16%)
  blocking collectives  19.7 us (16%)
  waiting for transfers between devices  19.4 us (16%)
  local copies, waits for them, and re-layouts  2.71 us (2%)
  other arithmetic  1.7 us (1%)
  between operations  1.47 us (1%)
    ppermute x3, starting transfers between devices, sibling(): return lax.ppermute(value, 'c', [(0, 1), (1, 0)])  20.9 us
    ppermute x4, starting transfers between devices, chip_step(): return lax.ppermute(value, ROWS, pairs)  13.3 us
    all_to_all x1, starting transfers between devices, on_device(): partial = lax.all_to_all(partial, ('y', 'c'), 0, 0)  10.4 us
    all_to_all x1, blocking collectives, on_device(): recv = lax.all_to_all(send, 'x', 0, 0)  10.4 us
    all_to_all x1, blocking collectives, on_device(): hidden_rows = lax.all_to_all(hidden, 'x', 0, 0).reshape(parts * feat, width)  9.34 us
    all_to_all x1, waiting for transfers between devices, on_device(): lax.all_to_all(jnp.broadcast_to(partial[None], (zs, 16, BLOCK)), 'z', 0, 0)  7.82 us
    all_to_all x1, waiting for transfers between devices, on_device(): lax.all_to_all(jnp.broadcast_to(partial[None, 0:8], (2 * ys, 8, BLOCK)),...  7.23 us
    all_to_all x1, starting transfers between devices, on_device(): lax.all_to_all(jnp.broadcast_to(partial[None, 0:8], (2 * ys, 8, BLOCK)),...  7.04 us
  transfers between devices with their start and end apart: 11, of which 5 were waited for; matrix products, arithmetic and copies ran while one was open for 3% of the time, Pallas kernels for 9%

profile of v2, /device:TPU:1, one launch (start us, length us, event | category | flops | bytes accessed | tf_op | source)
XLA Modules:
  0.0 123.7 jit_solution(7333783180926741070)
XLA Ops:
  0.6 2.6 %into_order.1 = (bf16[64,2048]{1,0:T(8,128)(2,1)S(1)}, bf16[96,128,128]{2,1,0:T(8,128)(2,1)S(1)}) custom-call(s32[1,2048]{1,0:T(1,128)} %order_hbm.3, bf16[64,2048]{1,0:T(8,128)(2,1)} %x_hbm.1, bf16[96,128,128]{2,1,0:T(8,128)(2,1)} %adj_hbm.3), custom_call_target="tpu_custom_call" | custom-call | flops 1000000000 | bytes 1048576 | tf_op jit(solution)/shard_map/into_order/pallas_call | solution.py:248
  3.2 4.0 %collective-permute-start.1 = (bf16[64,2048]{1,0:T(8,128)(2,1)S(1)}, bf16[64,2048]{1,0:T(8,128)(2,1)S(1)}, u32[]{:S(2)}, u32[]{:S(2)}) collective-permute-start(bf16[64,2048]{1,0:T(8,128)(2,1)S(1)} %get-tuple-element.13.w2), channel_id=1, source_target_pairs={{0,760},{4,12},{8,0},{12,20},{16,8},{20,28},{24,16},{28,36},{32,24... | collective-permute-start | bytes 786440 | tf_op jit(solution)/shard_map/ppermute | solution.py:240
  7.3 16.9 %collective-permute-start.3 = (bf16[64,2048]{1,0:T(8,128)(2,1)S(1)}, bf16[64,2048]{1,0:T(8,128)(2,1)S(1)}, u32[]{:S(2)}, u32[]{:S(2)}) collective-permute-start(bf16[64,2048]{1,0:T(8,128)(2,1)S(1)} %get-tuple-element.13.w2), channel_id=1, source_target_pairs={{0,4},{4,0},{1,5},{5,1},{2,6},{6,2},{3,7},{7,3},{8,12},{12,8},{9,1... | collective-permute-start | bytes 786440 | tf_op jit(solution)/shard_map/ppermute | solution.py:243
  24.1 3.0 %collective-permute-start = (bf16[64,2048]{1,0:T(8,128)(2,1)S(1)}, bf16[64,2048]{1,0:T(8,128)(2,1)S(1)}, u32[]{:S(2)}, u32[]{:S(2)}) collective-permute-start(bf16[64,2048]{1,0:T(8,128)(2,1)S(1)} %get-tuple-element.13.w2), channel_id=1, source_target_pairs={{0,8},{4,764},{8,16},{12,4},{16,24},{20,12},{24,32},{28,20},{32,40... | collective-permute-start | bytes 786440 | tf_op jit(solution)/shard_map/ppermute | solution.py:240
  27.1 0.0 collective-permute-done.1.w4
  27.1 1.9 %collective-permute-start.2 = (bf16[64,2048]{1,0:T(8,128)(2,1)S(1)}, bf16[64,2048]{1,0:T(8,128)(2,1)S(1)}, u32[]{:S(2)}, u32[]{:S(2)}) collective-permute-start(bf16[64,2048]{1,0:T(8,128)(2,1)S(1)} %collective-permute-done.1.w4), channel_id=1, source_target_pairs={{0,4},{4,0},{1,5},{5,1},{2,6},{6,2},{3,7},{7,3},{8,12},{12,8},{9,1... | collective-permute-start | bytes 786440 | tf_op jit(solution)/shard_map/ppermute | solution.py:243
  29.7 0.0 collective-permute-done.3.w3
  29.7 1.5 %collective-permute-done.w0 = bf16[64,2048]{1,0:T(8,128)(2,1)S(1)} collective-permute-done((bf16[64,2048]{1,0:T(8,128)(2,1)S(1)}, bf16[64,2048]{1,0:T(8,128)(2,1)S(1)}, u32[]{:S(2)}, u32[]{:S(2)}) %collective-permute-start) | collective-permute-done | bytes 262176 | tf_op jit(solution)/shard_map/ppermute | solution.py:240
  31.3 0.0 collective-permute-done.2.w1
  31.3 2.7 %aggregate.1 = bf16[4,64,512]{2,1,0:T(8,128)(2,1)S(1)} custom-call(s32[1]{0:T(128)S(6)} %copy.14.count_ref, s32[1,96]{1,0:T(1,128)} %dest_hbm.3, s32[1,96]{1,0:T(1,128)} %src_hbm.3, bf16[64,2048]{1,0:T(8,128)(2,1)S(1)} %collective-permute-done.w0, bf16[64,2048]{1,0:T(8,128)(2,1)S(1)} %collective-permute-done.2.w1, ...), custom_call_target="tpu_custom_call" | custom-call | flops 4000000000 | bytes 4194304 | tf_op jit(solution)/shard_map/aggregate/pallas_call | solution.py:268
  33.9 9.3 %all_to_all.30 = bf16[4,64,512]{2,1,0:T(8,128)(2,1)S(1)} all-to-all(bf16[4,64,512]{2,1,0:T(8,128)(2,1)S(1)} %aggregate.1), channel_id=1, replica_groups=mesh['z'=12,'y'=8,'c'=2,'x'=4] {'x'}, dimensions={0} | all-to-all | bytes 524288 | tf_op jit(solution)/shard_map/all_to_all | solution.py:285
  43.3 2.1 %dense.1 = (bf16[256,512]{1,0:T(8,128)(2,1)}, bf16[4,144,512]{2,1,0:T(8,128)(2,1)S(1)}) custom-call(bf16[256,512]{1,0:T(8,128)(2,1)S(1)} %bitcast.17, bf16[256,256]{1,0:T(8,128)(2,1)} %weight_hbm.1, f32[1,256]{1,0:T(1,128)} %bitcast.20, bf16[256,512]{1,0:T(8,128)(2,1)} %cot_hbm.1), custom_call_target="tpu_custom_call" | custom-call | flops 1000000000 | bytes 1048576 | tf_op jit(solution)/shard_map/dense/pallas_call | solution.py:287
  45.4 10.4 %all_to_all.31.recv_hbm = bf16[4,144,512]{2,1,0:T(8,128)(2,1)} all-to-all(bf16[4,144,512]{2,1,0:T(8,128)(2,1)S(1)} %get-tuple-element.16), channel_id=1, replica_groups=mesh['z'=12,'y'=8,'c'=2,'x'=4] {'x'}, dimensions={0} | all-to-all | bytes 1179648 | tf_op jit(solution)/shard_map/all_to_all | solution.py:306
  55.8 1.7 %first_sum.1 = f32[16,16,128]{2,1,0:T(8,128)} custom-call(bf16[4,144,512]{2,1,0:T(8,128)(2,1)} %all_to_all.31.recv_hbm), custom_call_target="tpu_custom_call" | custom-call | flops 1000000000 | bytes 1048576 | tf_op jit(solution)/shard_map/first_sum/pallas_call | solution.py:308
  57.5 10.4 %all-to-all-start.2 = ((f32[16,16,128]{2,1,0:T(8,128)}), f32[16,16,128]{2,1,0:T(8,128)S(1)}, u32[]{:S(2)}, u32[]{:S(2)}) async-start(f32[16,16,128]{2,1,0:T(8,128)} %first_sum.1), calls=%async_computation.2 | async-start | bytes 262144 | tf_op jit(solution)/shard_map/all_to_all | solution.py:322
  67.9 6.4 %spread_back.1 = (bf16[64,2048]{1,0:T(8,128)(2,1)}, bf16[2,64,2048]{2,1,0:T(8,128)(2,1)}, f32[64,2048]{1,0:T(8,128)}, f32[64,2048]{1,0:T(8,128)}, f32[8,128]{1,0:T(8,128)}) custom-call(s32[1]{0:T(128)S(6)} %copy.14.count_ref, s32[1,96]{1,0:T(1,128)} %dest_hbm.3, s32[1,96]{1,0:T(1,128)} %src_hbm.3, bf16[4,144,512]{2,1,0:T(8,128)(2,1)} %all_to_all.31.recv_hbm, ...), custom_call_target="tpu_custom_call" | custom-call | flops 4000000000 | bytes 4194304 | tf_op jit(solution)/shard_map/spread_back/pallas_call | solution.py:324
  74.3 2.2 %collective-permute-start.5 = (bf16[2,64,2048]{2,1,0:T(8,128)(2,1)}, bf16[2,64,2048]{2,1,0:T(8,128)(2,1)S(1)}, u32[]{:S(2)}, u32[]{:S(2)}) collective-permute-start(bf16[2,64,2048]{2,1,0:T(8,128)(2,1)} %get-tuple-element.19), channel_id=1, source_target_pairs={{0,4},{4,0},{1,5},{5,1},{2,6},{6,2},{3,7},{7,3},{8,12},{12,8},{9,1... | collective-permute-start | bytes 1572872 | tf_op jit(solution)/shard_map/ppermute | solution.py:243
  76.4 0.7 all-to-all-done.2
  77.1 0.6 broadcast_in_dim.11
  77.8 3.8 %all-to-all-start.3 = ((f32[12,16,128]{2,1,0:T(8,128)}), f32[12,16,128]{2,1,0:T(8,128)S(1)}, u32[]{:S(2)}, u32[]{:S(2)}) async-start(f32[12,16,128]{2,1,0:T(8,128)} %broadcast_in_dim.11), calls=%async_computation.3 | async-start | bytes 196608 | tf_op jit(solution)/shard_map/all_to_all | solution.py:359
  81.5 2.9 %collective-permute-start.4 = (bf16[64,2048]{1,0:T(8,128)(2,1)}, bf16[64,2048]{1,0:T(8,128)(2,1)S(1)}, u32[]{:S(2)}, u32[]{:S(2)}) collective-permute-start(bf16[64,2048]{1,0:T(8,128)(2,1)} %get-tuple-element.18), channel_id=1, source_target_pairs={{0,760},{4,12},{8,0},{12,20},{16,8},{20,28},{24,16},{28,36},{32,24... | collective-permute-start | bytes 786440 | tf_op jit(solution)/shard_map/ppermute | solution.py:240
  84.4 7.8 %all-to-all-done.3 = f32[12,16,128]{2,1,0:T(8,128)S(1)} async-done(((f32[12,16,128]{2,1,0:T(8,128)}), f32[12,16,128]{2,1,0:T(8,128)S(1)}, u32[]{:S(2)}, u32[]{:S(2)}) %all-to-all-start.3) | async-done | bytes 98336 | tf_op jit(solution)/shard_map/all_to_all | solution.py:359
  92.3 0.0 collective-permute-done.5.pair_hbm
  92.3 1.1 fusion
  93.4 3.4 %collective-permute-start.6 = (bf16[64,2048]{1,0:T(8,128)(2,1)S(1)}, bf16[64,2048]{1,0:T(8,128)(2,1)S(1)}, u32[]{:S(2)}, u32[]{:S(2)}) collective-permute-start(bf16[64,2048]{1,0:T(8,128)(2,1)S(1)} %fusion), channel_id=1, source_target_pairs={{0,8},{4,764},{8,16},{12,4},{16,24},{20,12},{24,32},{28,20},{32,40... | collective-permute-start | bytes 786440 | tf_op jit(solution)/shard_map/ppermute | solution.py:240
  96.8 0.6 broadcast_in_dim.24
  97.4 7.0 %all-to-all-start.4 = ((f32[16,8,128]{2,1,0:T(8,128)}), f32[16,8,128]{2,1,0:T(8,128)S(1)}, u32[]{:S(2)}, u32[]{:S(2)}) async-start(f32[16,8,128]{2,1,0:T(8,128)} %broadcast_in_dim.24), calls=%async_computation.4 | async-start | bytes 131072 | tf_op jit(solution)/shard_map/all_to_all | solution.py:362
  104.5 0.6 pad_maximum_fusion
  105.1 7.2 %all-to-all-done.4 = f32[16,8,128]{2,1,0:T(8,128)S(1)} async-done(((f32[16,8,128]{2,1,0:T(8,128)}), f32[16,8,128]{2,1,0:T(8,128)S(1)}, u32[]{:S(2)}, u32[]{:S(2)}) %all-to-all-start.4) | async-done | bytes 65568 | tf_op jit(solution)/shard_map/all_to_all | solution.py:362
  112.3 0.7 broadcast_in_dim.26
  113.0 3.4 %all-to-all-start.5 = ((f32[4,64,256]{2,1,0:T(8,128)}), f32[4,64,256]{2,1,0:T(8,128)S(1)}, u32[]{:S(2)}, u32[]{:S(2)}) async-start(f32[4,64,256]{2,1,0:T(8,128)} %broadcast_in_dim.26), calls=%async_computation.5 | async-start | bytes 524288 | tf_op jit(solution)/shard_map/all_to_all | solution.py:364
  116.4 0.0 collective-permute-done.4.first_hbm
  116.4 0.0 collective-permute-done.6.last_hbm
  116.4 4.5 %out_of_order.1 = bf16[64,2048]{1,0:T(8,128)(2,1)} custom-call(s32[1,2048]{1,0:T(1,128)} %order_hbm.3, f32[64,2048]{1,0:T(8,128)} %get-tuple-element.17.own_hbm, bf16[64,2048]{1,0:T(8,128)(2,1)S(1)} %collective-permute-done.4.first_hbm, bf16[2,64,2048]{2,1,0:T(8,128)(2,1)S(1)} %collective-permute-done.5.pair_hbm, ...), custom_call_target="tpu_custom_call" | custom-call | flops 3000000000 | bytes 2097152 | tf_op jit(solution)/shard_map/out_of_order/pallas_call | solution.py:367
  120.9 2.1 %all-to-all-done.5 = f32[4,64,256]{2,1,0:T(8,128)S(1)} async-done(((f32[4,64,256]{2,1,0:T(8,128)}), f32[4,64,256]{2,1,0:T(8,128)S(1)}, u32[]{:S(2)}, u32[]{:S(2)}) %all-to-all-start.5) | async-done | bytes 262176 | tf_op jit(solution)/shard_map/all_to_all | solution.py:364
  123.0 0.7 copy.15
  (5 shorter events, 0.0 us)
Async XLA Ops:
  3.2 23.9 %collective-permute-start.1 = (bf16[64,2048]{1,0:T(8,128)(2,1)S(1)}, bf16[64,2048]{1,0:T(8,128)(2,1)S(1)}, u32[]{:S(2)}, u32[]{:S(2)}) collective-permute-start(bf16[64,2048]{1,0:T(8,128)(2,1)S(1)} %get-tuple-element.13.w2), channel_id=1, source_target_pairs={{0,760},{4,12},{8,0},{12,20},{16,8},{20,28},{24,16},{28,36},{32,24... | collective-permute-start | bytes 786440 | tf_op jit(solution)/shard_map/ppermute | solution.py:240
  7.3 22.5 %collective-permute-start.3 = (bf16[64,2048]{1,0:T(8,128)(2,1)S(1)}, bf16[64,2048]{1,0:T(8,128)(2,1)S(1)}, u32[]{:S(2)}, u32[]{:S(2)}) collective-permute-start(bf16[64,2048]{1,0:T(8,128)(2,1)S(1)} %get-tuple-element.13.w2), channel_id=1, source_target_pairs={{0,4},{4,0},{1,5},{5,1},{2,6},{6,2},{3,7},{7,3},{8,12},{12,8},{9,1... | collective-permute-start | bytes 786440 | tf_op jit(solution)/shard_map/ppermute | solution.py:243
  24.1 7.1 %collective-permute-start = (bf16[64,2048]{1,0:T(8,128)(2,1)S(1)}, bf16[64,2048]{1,0:T(8,128)(2,1)S(1)}, u32[]{:S(2)}, u32[]{:S(2)}) collective-permute-start(bf16[64,2048]{1,0:T(8,128)(2,1)S(1)} %get-tuple-element.13.w2), channel_id=1, source_target_pairs={{0,8},{4,764},{8,16},{12,4},{16,24},{20,12},{24,32},{28,20},{32,40... | collective-permute-start | bytes 786440 | tf_op jit(solution)/shard_map/ppermute | solution.py:240
  27.1 4.1 %collective-permute-start.2 = (bf16[64,2048]{1,0:T(8,128)(2,1)S(1)}, bf16[64,2048]{1,0:T(8,128)(2,1)S(1)}, u32[]{:S(2)}, u32[]{:S(2)}) collective-permute-start(bf16[64,2048]{1,0:T(8,128)(2,1)S(1)} %collective-permute-done.1.w4), channel_id=1, source_target_pairs={{0,4},{4,0},{1,5},{5,1},{2,6},{6,2},{3,7},{7,3},{8,12},{12,8},{9,1... | collective-permute-start | bytes 786440 | tf_op jit(solution)/shard_map/ppermute | solution.py:243
  57.5 19.6 %all-to-all-start.2 = ((f32[16,16,128]{2,1,0:T(8,128)}), f32[16,16,128]{2,1,0:T(8,128)S(1)}, u32[]{:S(2)}, u32[]{:S(2)}) async-start(f32[16,16,128]{2,1,0:T(8,128)} %first_sum.1), calls=%async_computation.2 | async-start | bytes 262144 | tf_op jit(solution)/shard_map/all_to_all | solution.py:322
  74.3 18.0 %collective-permute-start.5 = (bf16[2,64,2048]{2,1,0:T(8,128)(2,1)}, bf16[2,64,2048]{2,1,0:T(8,128)(2,1)S(1)}, u32[]{:S(2)}, u32[]{:S(2)}) collective-permute-start(bf16[2,64,2048]{2,1,0:T(8,128)(2,1)} %get-tuple-element.19), channel_id=1, source_target_pairs={{0,4},{4,0},{1,5},{5,1},{2,6},{6,2},{3,7},{7,3},{8,12},{12,8},{9,1... | collective-permute-start | bytes 1572872 | tf_op jit(solution)/shard_map/ppermute | solution.py:243
  77.8 14.5 %all-to-all-start.3 = ((f32[12,16,128]{2,1,0:T(8,128)}), f32[12,16,128]{2,1,0:T(8,128)S(1)}, u32[]{:S(2)}, u32[]{:S(2)}) async-start(f32[12,16,128]{2,1,0:T(8,128)} %broadcast_in_dim.11), calls=%async_computation.3 | async-start | bytes 196608 | tf_op jit(solution)/shard_map/all_to_all | solution.py:359
  81.5 34.9 %collective-permute-start.4 = (bf16[64,2048]{1,0:T(8,128)(2,1)}, bf16[64,2048]{1,0:T(8,128)(2,1)S(1)}, u32[]{:S(2)}, u32[]{:S(2)}) collective-permute-start(bf16[64,2048]{1,0:T(8,128)(2,1)} %get-tuple-element.18), channel_id=1, source_target_pairs={{0,760},{4,12},{8,0},{12,20},{16,8},{20,28},{24,16},{28,36},{32,24... | collective-permute-start | bytes 786440 | tf_op jit(solution)/shard_map/ppermute | solution.py:240
  93.4 23.1 %collective-permute-start.6 = (bf16[64,2048]{1,0:T(8,128)(2,1)S(1)}, bf16[64,2048]{1,0:T(8,128)(2,1)S(1)}, u32[]{:S(2)}, u32[]{:S(2)}) collective-permute-start(bf16[64,2048]{1,0:T(8,128)(2,1)S(1)} %fusion), channel_id=1, source_target_pairs={{0,8},{4,764},{8,16},{12,4},{16,24},{20,12},{24,32},{28,20},{32,40... | collective-permute-start | bytes 786440 | tf_op jit(solution)/shard_map/ppermute | solution.py:240
  97.4 14.8 %all-to-all-start.4 = ((f32[16,8,128]{2,1,0:T(8,128)}), f32[16,8,128]{2,1,0:T(8,128)S(1)}, u32[]{:S(2)}, u32[]{:S(2)}) async-start(f32[16,8,128]{2,1,0:T(8,128)} %broadcast_in_dim.24), calls=%async_computation.4 | async-start | bytes 131072 | tf_op jit(solution)/shard_map/all_to_all | solution.py:362
  113.0 10.0 %all-to-all-start.5 = ((f32[4,64,256]{2,1,0:T(8,128)}), f32[4,64,256]{2,1,0:T(8,128)S(1)}, u32[]{:S(2)}, u32[]{:S(2)}) async-start(f32[4,64,256]{2,1,0:T(8,128)} %broadcast_in_dim.26), calls=%async_computation.5 | async-start | bytes 524288 | tf_op jit(solution)/shard_map/all_to_all | solution.py:364

commit v3 on v2

--- a/solution.py
+++ b/solution.py
@@ -1,3 +1,4 @@
+import functools
 import math
 
 import jax
@@ -49,7 +50,7 @@
 
 
 def out_of_order(
-    order_hbm, own_hbm, first_hbm, pair_hbm, last_hbm, out_ref, order, own, first, near, last, total, sems
+    order_hbm, own_hbm, first_hbm, pair_hbm, last_hbm, out_ref, token_ref, order, own, first, near, last, total, sems
 ):
     copies = started(
         [
@@ -61,11 +62,14 @@
         ],
         sems,
     )
+    token_ref[...] = jnp.zeros_like(token_ref)
     for copy in copies:
         copy.wait()
-    count = own.shape[1]
-    sums = own[...] + near[...].astype(F32) + first[...].astype(F32) + last[...].astype(F32)
-    total[...] = sums.astype(BF16)
+    for block in range(own.shape[0]):
+        sums = own[block] + near[block].astype(F32)
+        sums = sums + first[block].astype(F32) + last[block].astype(F32)
+        total[:, block * BLOCK : (block + 1) * BLOCK] = sums.astype(BF16)
+    count = total.shape[1]
     for start in range(0, count, TILE):
         rows = lax.broadcasted_iota(jnp.int32, (TILE, count), 0) + start
         hot = jnp.where(order[...] == rows, 1.0, 0.0).astype(BF16)
@@ -75,33 +79,67 @@
         out_ref[:, start : start + TILE] = moved.astype(BF16)
 
 
+def sum_to_all(recv, first_hbm, token, out_hbm, kept_hbm, out, sems):
+    total = jnp.sum(recv[...], axis=0)
+    for i in range(out.shape[0]):
+        out[i] = total
+    started([(out, out_hbm)], sems)[0].wait()
+
+
+def last_sum(scale, recv, own_hbm, token, out_hbm, kept_hbm, bias_ref, out, sems):
+    total = jnp.sum(recv[...], axis=0) * scale
+    for i in range(out.shape[0]):
+        out[i] = total[0:8]
+    copies = started([(out, out_hbm)], sems)
+    bias_ref[:, 0:BLOCK] = total[8:9]
+    bias_ref[:, BLOCK:] = total[12:13]
+    copies[0].wait()
+
+
+def put_together(recv, token, out_hbm, out, sems):
+    for i in range(recv.shape[0] // 2):
+        for c in range(2):
+            out[8 * i : 8 * i + 8, c * BLOCK : (c + 1) * BLOCK] = recv[2 * i + c]
+    pairs = [(out, out_hbm.at[i]) for i in range(out_hbm.shape[0])]
+    for copy in started(pairs, sems):
+        copy.wait()
+
+
 def mirrored(source, core, nblocks, spread):
     offset = source // nblocks
     return jnp.where(core == 0, offset, spread - 1 - offset), source % nblocks
 
 
 def aggregate(
-    count_ref, dest_hbm, src_hbm, w0, w1, w2, w3, w4, adj, out_ref, dest, src, win, acc, sems
+    count_ref, dest_hbm, src_hbm, before, across, permuted, beside, after, adj, out_ref, dest, src, win, acc, sems
 ):
     slots = adj.shape[0]
     nblocks = acc.shape[0] - 1
-    spread = win.shape[0]
+    spread = win.shape[0] // nblocks
     quarter = out_ref.shape[2] // BLOCK
-    windows = [(ref, win.at[i]) for i, ref in enumerate((w0, w1, w2, w3, w4))]
-    copies = started([(dest_hbm, dest), (src_hbm, src)] + windows, sems)
+    copies = started([(dest_hbm, dest), (src_hbm, src)], sems)
     acc[...] = jnp.zeros_like(acc)
-    for copy in copies:
-        copy.wait()
+    for block in range(nblocks):
+        lane = slice(block * BLOCK, (block + 1) * BLOCK)
+        win[block] = before[:, lane]
+        win[nblocks + block] = across[:, lane]
+        win[2 * nblocks + block] = permuted[:, lane]
+        win[3 * nblocks + block] = beside[:, lane]
+        win[4 * nblocks + block] = after[:, lane]
     core = lax.axis_index("c")
     count = count_ref[0]
+    for copy in copies:
+        copy.wait()
     for begin in range(0, slots, CHUNK):
         products = []
         for j in range(begin, begin + CHUNK):
             offset, block = mirrored(src[0, j], core, nblocks, spread)
-            picked = win[offset, :, pl.ds(pl.multiple_of(block * BLOCK, BLOCK), BLOCK)]
             products.append(
                 lax.dot_general(
-                    picked, adj[j], (((1,), (1,)), ((), ())), preferred_element_type=F32
+                    win[offset * nblocks + block],
+                    adj[j],
+                    (((1,), (1,)), ((), ())),
+                    preferred_element_type=F32,
                 )
             )
         for j, product in zip(range(begin, begin + CHUNK), products):
@@ -153,35 +191,37 @@
         send_ref[i, 2 * rows :, half_width:] = low_b
 
 
-def first_sum(recv_hbm, out_hbm, recv, out, sems):
-    rows = recv.shape[1] - 16
+def first_sum(recv, out_hbm, grad_hbm, out, sems):
+    rows = grad_hbm.shape[1]
     half_width = recv.shape[2] // 2
-    started([(recv_hbm.at[:, pl.ds(rows, rows + 16), :], recv)], sems)[0].wait()
+    copies = started([(recv.at[:, pl.ds(0, rows), :], grad_hbm)], sems)
     total = jnp.zeros((rows + 16, half_width), F32)
     for i in range(recv.shape[0]):
-        total = total + recv[i, :, 0:half_width].astype(F32)
-        total = total + recv[i, :, half_width:].astype(F32)
+        total = total + recv[i, rows:, 0:half_width].astype(F32)
+        total = total + recv[i, rows:, half_width:].astype(F32)
     for i in range(out.shape[0] // 2):
         for c in range(2):
             lane = slice(c * BLOCK, (c + 1) * BLOCK)
             out[2 * i + c, 0:8, :] = total[8 * i : 8 * i + 8, lane]
             out[2 * i + c, 8:12, :] = total[rows : rows + 4, 0:BLOCK]
             out[2 * i + c, 12:16, :] = total[rows : rows + 4, BLOCK : 2 * BLOCK]
-    started([(out, out_hbm)], sems)[0].wait()
+    last = pltpu.make_async_copy(out, out_hbm, sems.at[1])
+    last.start()
+    copies[0].wait()
+    last.wait()
 
 
 def spread_back(
-    count_ref, dest_hbm, src_hbm, recv_hbm, adj_hbm,
+    count_ref, dest_hbm, src_hbm, grad_hbm, adj_hbm,
     first_hbm, pair_hbm, own_hbm, last_hbm, token_ref,
-    dest, src, grad, adj, acc, first, pair, own, last, sems, adj_sems,
+    dest, src, grad, adj, acc, first, pair, sems, adj_sems,
 ):
     slots = adj.shape[0]
-    rows = grad.shape[1]
     quarter = grad.shape[2] // BLOCK
     nblocks = grad.shape[0] * quarter
     spread = (acc.shape[0] - 1) // nblocks
     copies = started(
-        [(dest_hbm, dest), (src_hbm, src), (recv_hbm.at[:, pl.ds(0, rows), :], grad)], sems
+        [(dest_hbm, dest), (src_hbm, src), (grad_hbm, grad)], sems
     )
     spans = [pl.ds(begin, CHUNK) for begin in range(0, slots, CHUNK)]
     adj_copies = started([(adj_hbm.at[span], adj.at[span]) for span in spans], adj_sems)
@@ -202,22 +242,20 @@
             offset, block = mirrored(src[0, j], core, nblocks, spread)
             place = jnp.where(j < count, offset * nblocks + block, spread * nblocks)
             acc[place] += product
-    outs = []
-    for offset, ref, target in (
-        (1, pair.at[0], None),
-        (3, pair.at[1], pair_hbm),
-        (0, first, first_hbm),
-        (4, last, last_hbm),
-        (2, own, own_hbm),
-    ):
-        for block in range(nblocks):
-            lane = slice(block * BLOCK, (block + 1) * BLOCK)
-            ref[:, lane] = acc[offset * nblocks + block].astype(ref.dtype)
-        if target is not None:
-            source = pair if target is pair_hbm else ref
-            copy = pltpu.make_async_copy(source, target, sems.at[3 + len(outs)])
-            copy.start()
-            outs.append(copy)
+    outs = started(
+        [
+            (acc.at[pl.ds(2 * nblocks, nblocks)], own_hbm),
+            (acc.at[pl.ds(4 * nblocks, nblocks)], last_hbm),
+        ],
+        sems,
+    )
+    pair[0] = acc[nblocks : 2 * nblocks].astype(BF16)
+    pair[1] = acc[3 * nblocks : 4 * nblocks].astype(BF16)
+    outs.append(pltpu.make_async_copy(pair, pair_hbm, sems.at[3]))
+    outs[-1].start()
+    first[...] = acc[0:nblocks].astype(BF16)
+    outs.append(pltpu.make_async_copy(first, first_hbm, sems.at[4]))
+    outs[-1].start()
     token_ref[...] = jnp.zeros_like(token_ref)
     for copy in outs:
         copy.wait()
@@ -273,9 +311,9 @@
         scratch_shapes=[
             pltpu.SMEM((1, slots), jnp.int32),
             pltpu.SMEM((1, slots), jnp.int32),
-            pltpu.VMEM((5, feat, nodes), BF16),
+            pltpu.VMEM((5 * nblocks, feat, BLOCK), BF16),
             pltpu.VMEM((nblocks + 1, feat, BLOCK), F32),
-            dma((7,)),
+            dma((2,)),
         ],
         compiler_params=PARAMS,
         cost_estimate=cost(4 * 10**9, 2**22),
@@ -305,29 +343,28 @@
 
     recv = lax.all_to_all(send, "x", 0, 0)
 
-    partial = pl.pallas_call(
+    partial, grads = pl.pallas_call(
         first_sum,
-        out_shape=pltpu.HBM((2 * ys, 16, BLOCK), F32),
-        in_specs=[HBM],
-        out_specs=HBM,
-        scratch_shapes=[
-            pltpu.VMEM((parts, feat + 16, width), BF16),
-            pltpu.VMEM((2 * ys, 16, BLOCK), F32),
-            dma((1,)),
-        ],
+        out_shape=(
+            pltpu.HBM((2 * ys, 16, BLOCK), F32),
+            pltpu.HBM((parts, feat, width), BF16),
+        ),
+        in_specs=[VMEM],
+        out_specs=(HBM, HBM),
+        scratch_shapes=[pltpu.VMEM((2 * ys, 16, BLOCK), F32), dma((2,))],
         compiler_params=PARAMS,
         cost_estimate=cost(10**9, 2**20),
         name="first_sum",
-    )(*in_hbm(recv))
+    )(recv)
     partial = lax.all_to_all(partial, ("y", "c"), 0, 0)
 
     first, pair, own, last, token = pl.pallas_call(
         spread_back,
         out_shape=(
-            pltpu.HBM((feat, nodes), BF16),
-            pltpu.HBM((2, feat, nodes), BF16),
-            pltpu.HBM((feat, nodes), F32),
-            pltpu.HBM((feat, nodes), F32),
+            pltpu.HBM((nblocks, feat, BLOCK), BF16),
+            pltpu.HBM((2, nblocks, feat, BLOCK), BF16),
+            pltpu.HBM((nblocks, feat, BLOCK), F32),
+            pltpu.HBM((nblocks, feat, BLOCK), F32),
             jax.ShapeDtypeStruct((8, BLOCK), F32),
         ),
         in_specs=[SMEM] + [HBM] * 4,
@@ -338,43 +375,61 @@
             pltpu.VMEM((parts, feat, width), BF16),
             pltpu.VMEM((slots, BLOCK, BLOCK), BF16),
             pltpu.VMEM((5 * nblocks + 1, feat, BLOCK), F32),
-            pltpu.VMEM((feat, nodes), BF16),
-            pltpu.VMEM((2, feat, nodes), BF16),
-            pltpu.VMEM((feat, nodes), F32),
-            pltpu.VMEM((feat, nodes), F32),
-            dma((7,)),
+            pltpu.VMEM((nblocks, feat, BLOCK), BF16),
+            pltpu.VMEM((2, nblocks, feat, BLOCK), BF16),
+            dma((5,)),
             dma((slots // CHUNK,)),
         ],
         compiler_params=PARAMS,
         cost_estimate=cost(4 * 10**9, 2**22),
         name="spread_back",
-    )(blk_count, *in_hbm(blk_dest, blk_src, recv, adj_values))
+    )(blk_count, *in_hbm(blk_dest, blk_src, grads, adj_values))
+
+    partial, first = pl.pallas_call(
+        sum_to_all,
+        out_shape=(pltpu.HBM((zs, 16, BLOCK), F32), pltpu.HBM(first.shape, BF16)),
+        in_specs=[VMEM, HBM, ANY],
+        out_specs=(HBM, HBM),
+        scratch_shapes=[pltpu.VMEM((zs, 16, BLOCK), F32), dma((1,))],
+        input_output_aliases={1: 1},
+        compiler_params=PARAMS,
+        cost_estimate=cost(3 * 10**10, 2**20),
+        name="sum_to_all",
+    )(partial, *in_hbm(first), token)
+    partial = lax.all_to_all(partial, "z", 0, 0)
 
     pair = sibling(pair)
     from_first = chip_step(first, -1)
     last = (last + pair[0].astype(F32)).astype(BF16)
     from_last = chip_step(last, 1)
 
-    partial = lax.optimization_barrier((jnp.sum(partial, axis=0), token))[0]
-    partial = lax.all_to_all(jnp.broadcast_to(partial[None], (zs, 16, BLOCK)), "z", 0, 0)
-    partial = lax.optimization_barrier((jnp.sum(partial, axis=0) * scale, last))[0]
-    grad_b = jnp.concatenate([partial[8], partial[12]])
-    pieces = lax.all_to_all(jnp.broadcast_to(partial[None, 0:8], (2 * ys, 8, BLOCK)), ("y", "c"), 0, 0)
-    pieces = pieces.reshape(ys, 2, 8, BLOCK).transpose(0, 2, 1, 3).reshape(8 * ys, 2 * BLOCK)
-    grad_w = lax.all_to_all(jnp.broadcast_to(pieces[None], (parts,) + pieces.shape), "x", 0, 0)
-    grad_w = grad_w.reshape(parts * 8 * ys, 2 * BLOCK)
-
-    grad_x = pl.pallas_call(
+    pieces, own, grad_b = pl.pallas_call(
+        functools.partial(last_sum, scale),
+        out_shape=(
+            pltpu.HBM((2 * ys, 8, BLOCK), F32),
+            pltpu.HBM(own.shape, F32),
+            jax.ShapeDtypeStruct((1, out_feat), F32),
+        ),
+        in_specs=[VMEM, HBM, ANY],
+        out_specs=(HBM, HBM, VMEM),
+        scratch_shapes=[pltpu.VMEM((2 * ys, 8, BLOCK), F32), dma((1,))],
+        input_output_aliases={1: 1},
+        compiler_params=PARAMS,
+        name="last_sum",
+    )(partial, *in_hbm(own), last)
+    pieces = lax.all_to_all(pieces, ("y", "c"), 0, 0)
+
+    grad_x, token = pl.pallas_call(
         out_of_order,
-        out_shape=slab,
+        out_shape=(slab, jax.ShapeDtypeStruct((8, BLOCK), F32)),
         in_specs=[HBM] * 2 + [ANY] * 3,
-        out_specs=VMEM,
+        out_specs=(VMEM, VMEM),
         scratch_shapes=[
             pltpu.VMEM((1, nodes), jnp.int32),
-            pltpu.VMEM((feat, nodes), F32),
-            pltpu.VMEM((feat, nodes), BF16),
-            pltpu.VMEM((feat, nodes), BF16),
-            pltpu.VMEM((feat, nodes), BF16),
+            pltpu.VMEM((nblocks, feat, BLOCK), F32),
+            pltpu.VMEM((nblocks, feat, BLOCK), BF16),
+            pltpu.VMEM((nblocks, feat, BLOCK), BF16),
+            pltpu.VMEM((nblocks, feat, BLOCK), BF16),
             pltpu.VMEM((feat, nodes), BF16),
             dma((5,)),
         ],
@@ -382,7 +437,18 @@
         cost_estimate=cost(3 * 10**9, 2**21),
         name="out_of_order",
     )(*in_hbm(node_order, own), from_first, pair, from_last)
-    return output, grad_x, grad_w, grad_b
+
+    whole = pl.pallas_call(
+        put_together,
+        out_shape=pltpu.HBM((parts, 8 * ys, 2 * BLOCK), F32),
+        in_specs=[VMEM, ANY],
+        out_specs=HBM,
+        scratch_shapes=[pltpu.VMEM((8 * ys, 2 * BLOCK), F32), dma((parts,))],
+        compiler_params=PARAMS,
+        name="put_together",
+    )(pieces, token)
+    grad_w = lax.all_to_all(whole, "x", 0, 0).reshape(parts * 8 * ys, 2 * BLOCK)
+    return output, grad_x, grad_w, grad_b.reshape(out_feat)
 
 
 def solution(mesh):

time: 125 us -> 119 us (0.952)
  waiting for transfers between devices: 19.4 us -> 8.18 us
  blocking collectives: 19.7 us -> 28.8 us
  local copies, waits for them, and re-layouts: 2.71 us -> 0.71 us
  other arithmetic: 1.7 us -> 0.06 us
  Pallas kernels: 19.9 us -> 21.3 us
    all_to_all x3 -> x2, waiting for transfers between devices: 17.2 us -> 5.24 us  [the longest x1 3.25 us: on_device(): pieces = lax.all_to_all(pieces, ('y', 'c'), 0, 0)]
    all_to_all x0 -> x1, blocking collectives: none -> 9.77 us  [on_device(): grad_w = lax.all_to_all(whole, 'x', 0, 0).reshape(parts * 8 * ys, 2 * BLOCK)]
    all_to_all x3 -> x2, starting transfers between devices: 14.2 us -> 11.1 us  [the longest x1 7.31 us: on_device(): pieces = lax.all_to_all(pieces, ('y', 'c'), 0, 0)]
    ppermute x4, starting transfers between devices: 13.3 us -> 15.6 us  [chip_step(): return lax.ppermute(value, ROWS, pairs)]
    broadcast_in_dim x3 -> x0, local copies, waits for them, and re-layouts: 2 us -> none  [the longest x1 0.72 us: on_device(): jnp.broadcast_to(pieces[None], (parts,) + pieces.shape)]
    pallas_call x3 -> x6, Pallas kernels: 12.5 us -> 13.6 us  [the longest x1 5.72 us: on_device(): pl.pallas_call(spread_back, out_shape=(pltpu.HBM((nblocks, feat, BLOCK),...]
  transfers between devices with their start and end apart: 11 -> 10, of which waited for: 5 -> 4; matrix products, arithmetic and copies ran while one was open for 3% -> 0% of each run, Pallas kernels for 9% -> 10%
where the time goes in v3:
time: 119 us; the launch traced here: 118 us
  starting transfers between devices  57.9 us (49%)
  blocking collectives  28.8 us (24%)
  Pallas kernels  21.3 us (18%)
  waiting for transfers between devices  8.18 us (7%)
  between operations  1.47 us (1%)
    ppermute x3, starting transfers between devices, sibling(): return lax.ppermute(value, 'c', [(0, 1), (1, 0)])  20.9 us
    ppermute x4, starting transfers between devices, chip_step(): return lax.ppermute(value, ROWS, pairs)  15.6 us
    all_to_all x1, starting transfers between devices, on_device(): partial = lax.all_to_all(partial, ('y', 'c'), 0, 0)  10.3 us
    all_to_all x1, blocking collectives, on_device(): grad_w = lax.all_to_all(whole, 'x', 0, 0).reshape(parts * 8 * ys, 2 * BLOCK)  9.77 us
    all_to_all x1, blocking collectives, on_device(): recv = lax.all_to_all(send, 'x', 0, 0)  9.67 us
    all_to_all x1, blocking collectives, on_device(): hidden_rows = lax.all_to_all(hidden, 'x', 0, 0).reshape(parts * feat, width)  9.34 us
    all_to_all x1, starting transfers between devices, on_device(): pieces = lax.all_to_all(pieces, ('y', 'c'), 0, 0)  7.31 us
    pallas_call x1, Pallas kernels, on_device(): pl.pallas_call(spread_back, out_shape=(pltpu.HBM((nblocks, feat, BLOCK),...  5.72 us
  transfers between devices with their start and end apart: 10, of which 4 were waited for; matrix products, arithmetic and copies ran while one was open for 0% of the time, Pallas kernels for 10%

profile of v3, /device:TPU:1, one launch (start us, length us, event | category | flops | bytes accessed | tf_op | source)
XLA Modules:
  0.0 118.5 jit_solution(17665610427959136885)
XLA Ops:
  0.6 2.6 %into_order.1 = (bf16[64,2048]{1,0:T(8,128)(2,1)S(1)}, bf16[96,128,128]{2,1,0:T(8,128)(2,1)S(1)}) custom-call(s32[1,2048]{1,0:T(1,128)} %order_hbm.3, bf16[64,2048]{1,0:T(8,128)(2,1)} %x_hbm.1, bf16[96,128,128]{2,1,0:T(8,128)(2,1)} %adj_hbm.3), custom_call_target="tpu_custom_call" | custom-call | flops 1000000000 | bytes 1048576 | tf_op jit(solution)/shard_map/into_order/pallas_call | solution.py:286
  3.2 4.0 %collective-permute-start.1 = (bf16[64,2048]{1,0:T(8,128)(2,1)S(1)}, bf16[64,2048]{1,0:T(8,128)(2,1)S(1)}, u32[]{:S(2)}, u32[]{:S(2)}) collective-permute-start(bf16[64,2048]{1,0:T(8,128)(2,1)S(1)} %get-tuple-element.22.permuted), channel_id=1, source_target_pairs={{0,760},{4,12},{8,0},{12,20},{16,8},{20,28},{24,16},{28,36},{32,24... | collective-permute-start | bytes 786440 | tf_op jit(solution)/shard_map/ppermute | solution.py:278
  7.3 16.9 %collective-permute-start.3 = (bf16[64,2048]{1,0:T(8,128)(2,1)S(1)}, bf16[64,2048]{1,0:T(8,128)(2,1)S(1)}, u32[]{:S(2)}, u32[]{:S(2)}) collective-permute-start(bf16[64,2048]{1,0:T(8,128)(2,1)S(1)} %get-tuple-element.22.permuted), channel_id=1, source_target_pairs={{0,4},{4,0},{1,5},{5,1},{2,6},{6,2},{3,7},{7,3},{8,12},{12,8},{9,1... | collective-permute-start | bytes 786440 | tf_op jit(solution)/shard_map/ppermute | solution.py:281
  24.1 3.0 %collective-permute-start = (bf16[64,2048]{1,0:T(8,128)(2,1)S(1)}, bf16[64,2048]{1,0:T(8,128)(2,1)S(1)}, u32[]{:S(2)}, u32[]{:S(2)}) collective-permute-start(bf16[64,2048]{1,0:T(8,128)(2,1)S(1)} %get-tuple-element.22.permuted), channel_id=1, source_target_pairs={{0,8},{4,764},{8,16},{12,4},{16,24},{20,12},{24,32},{28,20},{32,40... | collective-permute-start | bytes 786440 | tf_op jit(solution)/shard_map/ppermute | solution.py:278
  27.1 0.0 collective-permute-done.1.after
  27.1 1.9 %collective-permute-start.2 = (bf16[64,2048]{1,0:T(8,128)(2,1)S(1)}, bf16[64,2048]{1,0:T(8,128)(2,1)S(1)}, u32[]{:S(2)}, u32[]{:S(2)}) collective-permute-start(bf16[64,2048]{1,0:T(8,128)(2,1)S(1)} %collective-permute-done.1.after), channel_id=1, source_target_pairs={{0,4},{4,0},{1,5},{5,1},{2,6},{6,2},{3,7},{7,3},{8,12},{12,8},{9,1... | collective-permute-start | bytes 786440 | tf_op jit(solution)/shard_map/ppermute | solution.py:281
  29.7 0.0 collective-permute-done.3.beside
  29.7 1.5 %collective-permute-done.before = bf16[64,2048]{1,0:T(8,128)(2,1)S(1)} collective-permute-done((bf16[64,2048]{1,0:T(8,128)(2,1)S(1)}, bf16[64,2048]{1,0:T(8,128)(2,1)S(1)}, u32[]{:S(2)}, u32[]{:S(2)}) %collective-permute-start) | collective-permute-done | bytes 262176 | tf_op jit(solution)/shard_map/ppermute | solution.py:278
  31.3 0.0 collective-permute-done.2.across
  31.3 3.0 %aggregate.1 = bf16[4,64,512]{2,1,0:T(8,128)(2,1)S(1)} custom-call(s32[1]{0:T(128)S(6)} %copy.18.count_ref, s32[1,96]{1,0:T(1,128)} %dest_hbm.3, s32[1,96]{1,0:T(1,128)} %src_hbm.3, bf16[64,2048]{1,0:T(8,128)(2,1)S(1)} %collective-permute-done.before, bf16[64,2048]{1,0:T(8,128)(2,1)S(1)} %collective-permute-done.2.across, ...), custom_call_target="tpu_custom_call" | custom-call | flops 4000000000 | bytes 4194304 | tf_op jit(solution)/shard_map/aggregate/pallas_call | solution.py:306
  34.3 9.3 %all_to_all.30 = bf16[4,64,512]{2,1,0:T(8,128)(2,1)S(1)} all-to-all(bf16[4,64,512]{2,1,0:T(8,128)(2,1)S(1)} %aggregate.1), channel_id=1, replica_groups=mesh['z'=12,'y'=8,'c'=2,'x'=4] {'x'}, dimensions={0} | all-to-all | bytes 524288 | tf_op jit(solution)/shard_map/all_to_all | solution.py:323
  43.6 2.1 %dense.1 = (bf16[256,512]{1,0:T(8,128)(2,1)}, bf16[4,144,512]{2,1,0:T(8,128)(2,1)S(1)}) custom-call(bf16[256,512]{1,0:T(8,128)(2,1)S(1)} %bitcast.9, bf16[256,256]{1,0:T(8,128)(2,1)} %weight_hbm.1, f32[1,256]{1,0:T(1,128)} %bitcast.11, bf16[256,512]{1,0:T(8,128)(2,1)} %cot_hbm.1), custom_call_target="tpu_custom_call" | custom-call | flops 1000000000 | bytes 1048576 | tf_op jit(solution)/shard_map/dense/pallas_call | solution.py:325
  45.7 9.7 %all_to_all.31.recv = bf16[4,144,512]{2,1,0:T(8,128)(2,1)S(1)} all-to-all(bf16[4,144,512]{2,1,0:T(8,128)(2,1)S(1)} %get-tuple-element.25), channel_id=1, replica_groups=mesh['z'=12,'y'=8,'c'=2,'x'=4] {'x'}, dimensions={0} | all-to-all | bytes 1179648 | tf_op jit(solution)/shard_map/all_to_all | solution.py:344
  55.4 0.8 first_sum.1
  56.2 10.3 %all-to-all-start.2 = ((f32[16,16,128]{2,1,0:T(8,128)}), f32[16,16,128]{2,1,0:T(8,128)S(1)}, u32[]{:S(2)}, u32[]{:S(2)}) async-start(f32[16,16,128]{2,1,0:T(8,128)} %get-tuple-element.26), calls=%async_computation.2 | async-start | bytes 262144 | tf_op jit(solution)/shard_map/all_to_all | solution.py:359
  66.5 5.7 %spread_back.1 = (bf16[16,64,128]{2,1,0:T(8,128)(2,1)}, bf16[2,16,64,128]{3,2,1,0:T(8,128)(2,1)}, f32[16,64,128]{2,1,0:T(8,128)}, f32[16,64,128]{2,1,0:T(8,128)}, f32[8,128]{1,0:T(8,128)S(1)}) custom-call(s32[1]{0:T(128)S(6)} %copy.18.count_ref, s32[1,96]{1,0:T(1,128)} %dest_hbm.3, s32[1,96]{1,0:T(1,128)} %src_hbm.3, ...), custom_call_target="tpu_custom_call" | custom-call | flops 4000000000 | bytes 4194304 | tf_op jit(solution)/shard_map/spread_back/pallas_call | solution.py:361
  72.3 2.1 %collective-permute-start.4 = (bf16[2,16,64,128]{3,2,1,0:T(8,128)(2,1)}, bf16[2,16,64,128]{3,2,1,0:T(8,128)(2,1)S(1)}, u32[]{:S(2)}, u32[]{:S(2)}) collective-permute-start(bf16[2,16,64,128]{3,2,1,0:T(8,128)(2,1)} %get-tuple-element.33), channel_id=1, source_target_pairs={{0,4},{4,0},{1,5},{5,1},{2,6},{6,2},{3,7},{7,3},{8,12},{12,8},{9,1... | collective-permute-start | bytes 1572872 | tf_op jit(solution)/shard_map/ppermute | solution.py:281
  74.4 1.4 %all-to-all-done.2.recv = f32[16,16,128]{2,1,0:T(8,128)S(1)} async-done(((f32[16,16,128]{2,1,0:T(8,128)}), f32[16,16,128]{2,1,0:T(8,128)S(1)}, u32[]{:S(2)}, u32[]{:S(2)}) %all-to-all-start.2) | async-done | bytes 131104 | tf_op jit(solution)/shard_map/all_to_all | solution.py:359
  75.7 0.0 copy-start
  75.7 0.7 sum_to_all.1
  76.4 3.8 %all-to-all-start.3 = ((f32[12,16,128]{2,1,0:T(8,128)}), f32[12,16,128]{2,1,0:T(8,128)S(1)}, u32[]{:S(2)}, u32[]{:S(2)}) async-start(f32[12,16,128]{2,1,0:T(8,128)} %get-tuple-element.30), calls=%async_computation.3 | async-start | bytes 196608 | tf_op jit(solution)/shard_map/all_to_all | solution.py:399
  80.2 2.1 %collective-permute-start.5 = (bf16[16,64,128]{2,1,0:T(8,128)(2,1)}, bf16[16,64,128]{2,1,0:T(8,128)(2,1)S(1)}, u32[]{:S(2)}, u32[]{:S(2)}) collective-permute-start(bf16[16,64,128]{2,1,0:T(8,128)(2,1)} %get-tuple-element.35), channel_id=1, source_target_pairs={{0,760},{4,12},{8,0},{12,20},{16,8},{20,28},{24,16},{28,36},{32,24... | collective-permute-start | bytes 786440 | tf_op jit(solution)/shard_map/ppermute | solution.py:278
  82.4 0.0 collective-permute-done.4.pair_hbm
  82.4 0.0 copy-done
  82.4 0.1 fusion.token
  82.5 6.5 %collective-permute-start.6 = (bf16[16,64,128]{2,1,0:T(8,128)(2,1)S(1)}, bf16[16,64,128]{2,1,0:T(8,128)(2,1)S(1)}, u32[]{:S(2)}, u32[]{:S(2)}) collective-permute-start(bf16[16,64,128]{2,1,0:T(8,128)(2,1)S(1)} %fusion.token), channel_id=1, source_target_pairs={{0,8},{4,764},{8,16},{12,4},{16,24},{20,12},{24,32},{28,20},{32,40... | collective-permute-start | bytes 786440 | tf_op jit(solution)/shard_map/ppermute | solution.py:278
  88.9 2.0 %all-to-all-done.3.recv = f32[12,16,128]{2,1,0:T(8,128)S(1)} async-done(((f32[12,16,128]{2,1,0:T(8,128)}), f32[12,16,128]{2,1,0:T(8,128)S(1)}, u32[]{:S(2)}, u32[]{:S(2)}) %all-to-all-start.3) | async-done | bytes 98336 | tf_op jit(solution)/shard_map/all_to_all | solution.py:399
  90.9 1.2 %last_sum.1 = (f32[16,8,128]{2,1,0:T(8,128)}, f32[16,64,128]{2,1,0:T(8,128)}, f32[1,256]{1,0:T(1,128)}) custom-call(f32[12,16,128]{2,1,0:T(8,128)S(1)} %all-to-all-done.3.recv, f32[16,64,128]{2,1,0:T(8,128)} %get-tuple-element.31.own_hbm, bf16[16,64,128]{2,1,0:T(8,128)(2,1)S(1)} %fusion.token), custom_call_target="tpu_custom_call", output_to_operand_aliasing={{1}: (1, {})} | custom-call | tf_op jit(solution)/shard_map/last_sum/pallas_call | solution.py:406
  92.1 7.3 %all-to-all-start.4 = ((f32[16,8,128]{2,1,0:T(8,128)}), f32[16,8,128]{2,1,0:T(8,128)S(1)}, u32[]{:S(2)}, u32[]{:S(2)}) async-start(f32[16,8,128]{2,1,0:T(8,128)} %get-tuple-element.37), calls=%async_computation.4 | async-start | bytes 131072 | tf_op jit(solution)/shard_map/all_to_all | solution.py:420
  99.5 0.0 collective-permute-done.5.first_hbm
  99.5 0.0 collective-permute-done.6.last_hbm
  99.5 4.5 %out_of_order.1 = (bf16[64,2048]{1,0:T(8,128)(2,1)}, f32[8,128]{1,0:T(8,128)S(1)}) custom-call(s32[1,2048]{1,0:T(1,128)} %order_hbm.3, f32[16,64,128]{2,1,0:T(8,128)} %get-tuple-element.34.own_hbm, bf16[16,64,128]{2,1,0:T(8,128)(2,1)S(1)} %collective-permute-done.5.first_hbm, bf16[2,16,64,128]{3,2,1,0:T(8,128)(2,1)S(1)} %collective-permute-done.4.pair_hbm, ...), custom_call_target="tpu_custom_call" | custom-call | flops 3000000000 | bytes 2097152 | tf_op jit(solution)/shard_map/out_of_order/pallas_call | solution.py:422
  104.0 3.3 %all-to-all-done.4.recv = f32[16,8,128]{2,1,0:T(8,128)S(1)} async-done(((f32[16,8,128]{2,1,0:T(8,128)}), f32[16,8,128]{2,1,0:T(8,128)S(1)}, u32[]{:S(2)}, u32[]{:S(2)}) %all-to-all-start.4) | async-done | bytes 65568 | tf_op jit(solution)/shard_map/all_to_all | solution.py:420
  107.3 0.7 put_together.1
  108.0 9.8 %all_to_all.32 = f32[4,64,256]{2,1,0:T(8,128)S(1)} all-to-all(f32[4,64,256]{2,1,0:T(8,128)} %put_together.1), channel_id=1, replica_groups=mesh['z'=12,'y'=8,'c'=2,'x'=4] {'x'}, dimensions={0} | all-to-all | bytes 524288 | tf_op jit(solution)/shard_map/all_to_all | solution.py:450
  117.8 0.7 copy.19
Async XLA Ops:
  3.2 23.9 %collective-permute-start.1 = (bf16[64,2048]{1,0:T(8,128)(2,1)S(1)}, bf16[64,2048]{1,0:T(8,128)(2,1)S(1)}, u32[]{:S(2)}, u32[]{:S(2)}) collective-permute-start(bf16[64,2048]{1,0:T(8,128)(2,1)S(1)} %get-tuple-element.22.permuted), channel_id=1, source_target_pairs={{0,760},{4,12},{8,0},{12,20},{16,8},{20,28},{24,16},{28,36},{32,24... | collective-permute-start | bytes 786440 | tf_op jit(solution)/shard_map/ppermute | solution.py:278
  7.3 22.5 %collective-permute-start.3 = (bf16[64,2048]{1,0:T(8,128)(2,1)S(1)}, bf16[64,2048]{1,0:T(8,128)(2,1)S(1)}, u32[]{:S(2)}, u32[]{:S(2)}) collective-permute-start(bf16[64,2048]{1,0:T(8,128)(2,1)S(1)} %get-tuple-element.22.permuted), channel_id=1, source_target_pairs={{0,4},{4,0},{1,5},{5,1},{2,6},{6,2},{3,7},{7,3},{8,12},{12,8},{9,1... | collective-permute-start | bytes 786440 | tf_op jit(solution)/shard_map/ppermute | solution.py:281
  24.1 7.1 %collective-permute-start = (bf16[64,2048]{1,0:T(8,128)(2,1)S(1)}, bf16[64,2048]{1,0:T(8,128)(2,1)S(1)}, u32[]{:S(2)}, u32[]{:S(2)}) collective-permute-start(bf16[64,2048]{1,0:T(8,128)(2,1)S(1)} %get-tuple-element.22.permuted), channel_id=1, source_target_pairs={{0,8},{4,764},{8,16},{12,4},{16,24},{20,12},{24,32},{28,20},{32,40... | collective-permute-start | bytes 786440 | tf_op jit(solution)/shard_map/ppermute | solution.py:278
  27.1 4.1 %collective-permute-start.2 = (bf16[64,2048]{1,0:T(8,128)(2,1)S(1)}, bf16[64,2048]{1,0:T(8,128)(2,1)S(1)}, u32[]{:S(2)}, u32[]{:S(2)}) collective-permute-start(bf16[64,2048]{1,0:T(8,128)(2,1)S(1)} %collective-permute-done.1.after), channel_id=1, source_target_pairs={{0,4},{4,0},{1,5},{5,1},{2,6},{6,2},{3,7},{7,3},{8,12},{12,8},{9,1... | collective-permute-start | bytes 786440 | tf_op jit(solution)/shard_map/ppermute | solution.py:281
  56.2 19.6 %all-to-all-start.2 = ((f32[16,16,128]{2,1,0:T(8,128)}), f32[16,16,128]{2,1,0:T(8,128)S(1)}, u32[]{:S(2)}, u32[]{:S(2)}) async-start(f32[16,16,128]{2,1,0:T(8,128)} %get-tuple-element.26), calls=%async_computation.2 | async-start | bytes 262144 | tf_op jit(solution)/shard_map/all_to_all | solution.py:359
  72.3 10.1 %collective-permute-start.4 = (bf16[2,16,64,128]{3,2,1,0:T(8,128)(2,1)}, bf16[2,16,64,128]{3,2,1,0:T(8,128)(2,1)S(1)}, u32[]{:S(2)}, u32[]{:S(2)}) collective-permute-start(bf16[2,16,64,128]{3,2,1,0:T(8,128)(2,1)} %get-tuple-element.33), channel_id=1, source_target_pairs={{0,4},{4,0},{1,5},{5,1},{2,6},{6,2},{3,7},{7,3},{8,12},{12,8},{9,1... | collective-permute-start | bytes 1572872 | tf_op jit(solution)/shard_map/ppermute | solution.py:281
  75.7 6.6 %copy-start = (f32[16,64,128]{2,1,0:T(8,128)S(1)}, f32[16,64,128]{2,1,0:T(8,128)}, u32[]{:S(2)}) copy-start(f32[16,64,128]{2,1,0:T(8,128)} %get-tuple-element.32) | copy-start | bytes 1572868
  76.4 14.5 %all-to-all-start.3 = ((f32[12,16,128]{2,1,0:T(8,128)}), f32[12,16,128]{2,1,0:T(8,128)S(1)}, u32[]{:S(2)}, u32[]{:S(2)}) async-start(f32[12,16,128]{2,1,0:T(8,128)} %get-tuple-element.30), calls=%async_computation.3 | async-start | bytes 196608 | tf_op jit(solution)/shard_map/all_to_all | solution.py:399
  80.2 19.2 %collective-permute-start.5 = (bf16[16,64,128]{2,1,0:T(8,128)(2,1)}, bf16[16,64,128]{2,1,0:T(8,128)(2,1)S(1)}, u32[]{:S(2)}, u32[]{:S(2)}) collective-permute-start(bf16[16,64,128]{2,1,0:T(8,128)(2,1)} %get-tuple-element.35), channel_id=1, source_target_pairs={{0,760},{4,12},{8,0},{12,20},{16,8},{20,28},{24,16},{28,36},{32,24... | collective-permute-start | bytes 786440 | tf_op jit(solution)/shard_map/ppermute | solution.py:278
  82.5 17.0 %collective-permute-start.6 = (bf16[16,64,128]{2,1,0:T(8,128)(2,1)S(1)}, bf16[16,64,128]{2,1,0:T(8,128)(2,1)S(1)}, u32[]{:S(2)}, u32[]{:S(2)}) collective-permute-start(bf16[16,64,128]{2,1,0:T(8,128)(2,1)S(1)} %fusion.token), channel_id=1, source_target_pairs={{0,8},{4,764},{8,16},{12,4},{16,24},{20,12},{24,32},{28,20},{32,40... | collective-permute-start | bytes 786440 | tf_op jit(solution)/shard_map/ppermute | solution.py:278
  92.1 15.1 %all-to-all-start.4 = ((f32[16,8,128]{2,1,0:T(8,128)}), f32[16,8,128]{2,1,0:T(8,128)S(1)}, u32[]{:S(2)}, u32[]{:S(2)}) async-start(f32[16,8,128]{2,1,0:T(8,128)} %get-tuple-element.37), calls=%async_computation.4 | async-start | bytes 131072 | tf_op jit(solution)/shard_map/all_to_all | solution.py:420

commit v4 on v3

--- a/solution.py
+++ b/solution.py
@@ -14,6 +14,7 @@
 TILE = 256
 ROWS = ("z", "y", "c")
 CHUNK = 8
+SPAN = 48
 VMEM = pl.BlockSpec(memory_space=pltpu.VMEM)
 SMEM = pl.BlockSpec(memory_space=pltpu.SMEM)
 HBM = pl.BlockSpec(memory_space=pltpu.HBM)
@@ -25,6 +26,10 @@
     return tuple(pltpu.with_memory_space_constraint(array, pltpu.HBM) for array in arrays)
 
 
+def in_smem(*arrays):
+    return tuple(pltpu.with_memory_space_constraint(array, pltpu.SMEM) for array in arrays)
+
+
 def cost(flops, size):
     return pl.CostEstimate(flops=flops, bytes_accessed=size, transcendentals=0)
 
@@ -34,6 +39,10 @@
     for copy in copies:
         copy.start()
     return copies
+
+
+def split(index, size):
+    return index >> (size.bit_length() - 1), index & (size - 1)
 
 
 def into_order(order_hbm, x_hbm, adj_hbm, out_ref, adj_ref, order, x, sems):
@@ -42,9 +51,13 @@
     copies[1].wait()
     count = x.shape[1]
     for start in range(0, count, TILE):
-        rows = lax.broadcasted_iota(jnp.int32, (count, TILE), 0)
-        hot = jnp.where(order[:, start : start + TILE] == rows, 1.0, 0.0).astype(BF16)
-        moved = jnp.dot(x[...], hot, preferred_element_type=F32)
+        group, lane = split(order[:, start : start + TILE], BLOCK)
+        rows = lax.broadcasted_iota(jnp.int32, (BLOCK, TILE), 0)
+        hot = jnp.where(lane == rows, 1.0, 0.0).astype(BF16)
+        moved = jnp.zeros((x.shape[0], TILE), F32)
+        for g in range(count // BLOCK):
+            part = jnp.dot(x[:, g * BLOCK : (g + 1) * BLOCK], hot, preferred_element_type=F32)
+            moved = jnp.where(group == g, part, moved)
         out_ref[:, start : start + TILE] = moved.astype(BF16)
     copies[2].wait()
 
@@ -96,28 +109,31 @@
     copies[0].wait()
 
 
-def put_together(recv, token, out_hbm, out, sems):
-    for i in range(recv.shape[0] // 2):
-        for c in range(2):
-            out[8 * i : 8 * i + 8, c * BLOCK : (c + 1) * BLOCK] = recv[2 * i + c]
-    pairs = [(out, out_hbm.at[i]) for i in range(out_hbm.shape[0])]
-    for copy in started(pairs, sems):
-        copy.wait()
+def put_together(parts, recv, token, out_ref):
+    rows = out_ref.shape[0] // parts
+    for i in range(recv.shape[0]):
+        y, c, x = i // (2 * parts), i // parts % 2, i % parts
+        row, lane = x * rows + 8 * y, c * BLOCK
+        out_ref[row : row + 8, lane : lane + BLOCK] = recv[i]
 
 
 def mirrored(source, core, nblocks, spread):
-    offset = source // nblocks
-    return jnp.where(core == 0, offset, spread - 1 - offset), source % nblocks
+    offset, block = split(source, nblocks)
+    return jnp.where(core == 0, offset, spread - 1 - offset) * nblocks + block
+
+
+def turned(adj, out_ref):
+    for j in range(adj.shape[0]):
+        out_ref[j] = adj[j].T
 
 
 def aggregate(
-    count_ref, dest_hbm, src_hbm, before, across, permuted, beside, after, adj, out_ref, dest, src, win, acc, sems
+    count_ref, dest, src, before, across, permuted, beside, after, adj, out_ref, win, acc
 ):
     slots = adj.shape[0]
     nblocks = acc.shape[0] - 1
     spread = win.shape[0] // nblocks
     quarter = out_ref.shape[2] // BLOCK
-    copies = started([(dest_hbm, dest), (src_hbm, src)], sems)
     acc[...] = jnp.zeros_like(acc)
     for block in range(nblocks):
         lane = slice(block * BLOCK, (block + 1) * BLOCK)
@@ -128,19 +144,12 @@
         win[4 * nblocks + block] = after[:, lane]
     core = lax.axis_index("c")
     count = count_ref[0]
-    for copy in copies:
-        copy.wait()
     for begin in range(0, slots, CHUNK):
         products = []
         for j in range(begin, begin + CHUNK):
-            offset, block = mirrored(src[0, j], core, nblocks, spread)
+            place = mirrored(src[0, j], core, nblocks, spread)
             products.append(
-                lax.dot_general(
-                    win[offset * nblocks + block],
-                    adj[j],
-                    (((1,), (1,)), ((), ())),
-                    preferred_element_type=F32,
-                )
+                jnp.dot(win[place], adj[j], preferred_element_type=F32)
             )
         for j, product in zip(range(begin, begin + CHUNK), products):
             target = jnp.where(j < count, dest[0, j], nblocks)
@@ -223,7 +232,7 @@
     copies = started(
         [(dest_hbm, dest), (src_hbm, src), (grad_hbm, grad)], sems
     )
-    spans = [pl.ds(begin, CHUNK) for begin in range(0, slots, CHUNK)]
+    spans = [pl.ds(begin, SPAN) for begin in range(0, slots, SPAN)]
     adj_copies = started([(adj_hbm.at[span], adj.at[span]) for span in spans], adj_sems)
     acc[...] = jnp.zeros_like(acc)
     core = lax.axis_index("c")
@@ -233,14 +242,13 @@
     for index, copy in enumerate(adj_copies):
         copy.wait()
         products = []
-        for j in range(index * CHUNK, (index + 1) * CHUNK):
-            target = dest[0, j]
-            lane = pl.multiple_of((target % quarter) * BLOCK, BLOCK)
-            picked = grad[target // quarter, :, pl.ds(lane, BLOCK)]
+        for j in range(index * SPAN, (index + 1) * SPAN):
+            part, place = split(dest[0, j], quarter)
+            picked = grad[part, :, pl.ds(pl.multiple_of(place * BLOCK, BLOCK), BLOCK)]
             products.append(jnp.dot(picked, adj[j], preferred_element_type=F32))
-        for j, product in zip(range(index * CHUNK, (index + 1) * CHUNK), products):
-            offset, block = mirrored(src[0, j], core, nblocks, spread)
-            place = jnp.where(j < count, offset * nblocks + block, spread * nblocks)
+        for j, product in zip(range(index * SPAN, (index + 1) * SPAN), products):
+            place = mirrored(src[0, j], core, nblocks, spread)
+            place = jnp.where(j < count, place, spread * nblocks)
             acc[place] += product
     outs = started(
         [
@@ -298,6 +306,15 @@
         name="into_order",
     )(*in_hbm(node_order, features, adj_values))
 
+    across_adj = pl.pallas_call(
+        turned,
+        out_shape=jax.ShapeDtypeStruct(adj_values.shape, BF16),
+        in_specs=[VMEM],
+        out_specs=VMEM,
+        compiler_params=PARAMS,
+        cost_estimate=cost(2 * 10**9, 2**20),
+        name="turned",
+    )(adj)
     after = chip_step(permuted, -1)
     before = chip_step(permuted, 1)
     beside = sibling(permuted)
@@ -306,19 +323,16 @@
     hidden = pl.pallas_call(
         aggregate,
         out_shape=jax.ShapeDtypeStruct((parts, feat, width), BF16),
-        in_specs=[SMEM] + [HBM] * 2 + [VMEM] * 6,
+        in_specs=[SMEM] * 3 + [VMEM] * 6,
         out_specs=VMEM,
         scratch_shapes=[
-            pltpu.SMEM((1, slots), jnp.int32),
-            pltpu.SMEM((1, slots), jnp.int32),
             pltpu.VMEM((5 * nblocks, feat, BLOCK), BF16),
             pltpu.VMEM((nblocks + 1, feat, BLOCK), F32),
-            dma((2,)),
         ],
         compiler_params=PARAMS,
         cost_estimate=cost(4 * 10**9, 2**22),
         name="aggregate",
-    )(blk_count, *in_hbm(blk_dest, blk_src), before, across, permuted, beside, after, adj)
+    )(blk_count, *in_smem(blk_dest, blk_src), before, across, permuted, beside, after, across_adj)
 
     hidden_rows = lax.all_to_all(hidden, "x", 0, 0).reshape(parts * feat, width)
 
@@ -378,7 +392,7 @@
             pltpu.VMEM((nblocks, feat, BLOCK), BF16),
             pltpu.VMEM((2, nblocks, feat, BLOCK), BF16),
             dma((5,)),
-            dma((slots // CHUNK,)),
+            dma((slots // SPAN,)),
         ],
         compiler_params=PARAMS,
         cost_estimate=cost(4 * 10**9, 2**22),
@@ -406,18 +420,18 @@
     pieces, own, grad_b = pl.pallas_call(
         functools.partial(last_sum, scale),
         out_shape=(
-            pltpu.HBM((2 * ys, 8, BLOCK), F32),
+            pltpu.HBM((2 * ys * parts, 8, BLOCK), F32),
             pltpu.HBM(own.shape, F32),
             jax.ShapeDtypeStruct((1, out_feat), F32),
         ),
         in_specs=[VMEM, HBM, ANY],
         out_specs=(HBM, HBM, VMEM),
-        scratch_shapes=[pltpu.VMEM((2 * ys, 8, BLOCK), F32), dma((1,))],
+        scratch_shapes=[pltpu.VMEM((2 * ys * parts, 8, BLOCK), F32), dma((1,))],
         input_output_aliases={1: 1},
         compiler_params=PARAMS,
         name="last_sum",
     )(partial, *in_hbm(own), last)
-    pieces = lax.all_to_all(pieces, ("y", "c"), 0, 0)
+    pieces = lax.all_to_all(pieces, ("y", "c", "x"), 0, 0)
 
     grad_x, token = pl.pallas_call(
         out_of_order,
@@ -438,16 +452,14 @@
         name="out_of_order",
     )(*in_hbm(node_order, own), from_first, pair, from_last)
 
-    whole = pl.pallas_call(
-        put_together,
-        out_shape=pltpu.HBM((parts, 8 * ys, 2 * BLOCK), F32),
+    grad_w = pl.pallas_call(
+        functools.partial(put_together, parts),
+        out_shape=jax.ShapeDtypeStruct((parts * 8 * ys, 2 * BLOCK), F32),
         in_specs=[VMEM, ANY],
-        out_specs=HBM,
-        scratch_shapes=[pltpu.VMEM((8 * ys, 2 * BLOCK), F32), dma((parts,))],
+        out_specs=VMEM,
         compiler_params=PARAMS,
         name="put_together",
     )(pieces, token)
-    grad_w = lax.all_to_all(whole, "x", 0, 0).reshape(parts * 8 * ys, 2 * BLOCK)
     return output, grad_x, grad_w, grad_b.reshape(out_feat)
 
 

time: 119 us -> 111 us (0.933)
  blocking collectives: 28.8 us -> 19 us
  waiting for transfers between devices: 8.18 us -> 13.5 us
  Pallas kernels: 21.3 us -> 18.9 us
    all_to_all x1 -> x0, blocking collectives: 9.77 us -> none  [on_device(): grad_w = lax.all_to_all(whole, 'x', 0, 0).reshape(parts * 8 * ys, 2 * BLOCK)]
    all_to_all x1, waiting for transfers between devices: 3.25 us -> 7.73 us  [on_device(): pieces = lax.all_to_all(pieces, ('y', 'c', 'x'), 0, 0)]
    pallas_call x1, Pallas kernels: 5.72 us -> 3.93 us  [on_device(): pl.pallas_call(spread_back, out_shape=(pltpu.HBM((nblocks, feat, BLOCK),...]
    all_to_all x1, waiting for transfers between devices: 1.39 us -> 3.12 us  [on_device(): partial = lax.all_to_all(partial, ('y', 'c'), 0, 0)]
    pallas_call x1, Pallas kernels: 2.99 us -> 1.78 us  [on_device(): pl.pallas_call(aggregate, out_shape=jax.ShapeDtypeStruct((parts, feat, wi...]
where the time goes in v4:
time: 111 us; the launch traced here: 110 us
  starting transfers between devices  57.3 us (52%)
  blocking collectives  19 us (17%)
  Pallas kernels  18.9 us (17%)
  waiting for transfers between devices  13.5 us (12%)
  between operations  1.5 us (1%)
    ppermute x3, starting transfers between devices, sibling(): return lax.ppermute(value, 'c', [(0, 1), (1, 0)])  20.9 us
    ppermute x4, starting transfers between devices, chip_step(): return lax.ppermute(value, ROWS, pairs)  15.6 us
    all_to_all x1, starting transfers between devices, on_device(): partial = lax.all_to_all(partial, ('y', 'c'), 0, 0)  10.4 us
    all_to_all x1, blocking collectives, on_device(): recv = lax.all_to_all(send, 'x', 0, 0)  9.67 us
    all_to_all x1, blocking collectives, on_device(): hidden_rows = lax.all_to_all(hidden, 'x', 0, 0).reshape(parts * feat, width)  9.34 us
    all_to_all x1, waiting for transfers between devices, on_device(): pieces = lax.all_to_all(pieces, ('y', 'c', 'x'), 0, 0)  7.73 us
    all_to_all x1, starting transfers between devices, on_device(): pieces = lax.all_to_all(pieces, ('y', 'c', 'x'), 0, 0)  6.67 us
    pallas_call x1, Pallas kernels, on_device(): pl.pallas_call(out_of_order, out_shape=(slab, jax.ShapeDtypeStruct((8, BL...  4.53 us
  transfers between devices with their start and end apart: 10, of which 4 were waited for; matrix products, arithmetic and copies ran while one was open for 0% of the time, Pallas kernels for 10%

profile of v4, /device:TPU:1, one launch (start us, length us, event | category | flops | bytes accessed | tf_op | source)
XLA Modules:
  0.0 110.3 jit_solution(16973976069848512131)
XLA Ops:
  0.6 2.2 %into_order.1 = (bf16[64,2048]{1,0:T(8,128)(2,1)S(1)}, bf16[96,128,128]{2,1,0:T(8,128)(2,1)S(1)}) custom-call(s32[1,2048]{1,0:T(1,128)} %order_hbm.3, bf16[64,2048]{1,0:T(8,128)(2,1)} %x_hbm.1, bf16[96,128,128]{2,1,0:T(8,128)(2,1)} %adj_hbm.3), custom_call_target="tpu_custom_call" | custom-call | flops 1000000000 | bytes 1048576 | tf_op jit(solution)/shard_map/into_order/pallas_call | solution.py:294
  2.9 4.0 %collective-permute-start.1 = (bf16[64,2048]{1,0:T(8,128)(2,1)S(1)}, bf16[64,2048]{1,0:T(8,128)(2,1)S(1)}, u32[]{:S(2)}, u32[]{:S(2)}) collective-permute-start(bf16[64,2048]{1,0:T(8,128)(2,1)S(1)} %get-tuple-element.22.permuted), channel_id=1, source_target_pairs={{0,760},{4,12},{8,0},{12,20},{16,8},{20,28},{24,16},{28,36},{32,24... | collective-permute-start | bytes 786440 | tf_op jit(solution)/shard_map/ppermute | solution.py:286
  6.9 16.9 %collective-permute-start.3 = (bf16[64,2048]{1,0:T(8,128)(2,1)S(1)}, bf16[64,2048]{1,0:T(8,128)(2,1)S(1)}, u32[]{:S(2)}, u32[]{:S(2)}) collective-permute-start(bf16[64,2048]{1,0:T(8,128)(2,1)S(1)} %get-tuple-element.22.permuted), channel_id=1, source_target_pairs={{0,4},{4,0},{1,5},{5,1},{2,6},{6,2},{3,7},{7,3},{8,12},{12,8},{9,1... | collective-permute-start | bytes 786440 | tf_op jit(solution)/shard_map/ppermute | solution.py:289
  23.8 3.0 %collective-permute-start = (bf16[64,2048]{1,0:T(8,128)(2,1)S(1)}, bf16[64,2048]{1,0:T(8,128)(2,1)S(1)}, u32[]{:S(2)}, u32[]{:S(2)}) collective-permute-start(bf16[64,2048]{1,0:T(8,128)(2,1)S(1)} %get-tuple-element.22.permuted), channel_id=1, source_target_pairs={{0,8},{4,764},{8,16},{12,4},{16,24},{20,12},{24,32},{28,20},{32,40... | collective-permute-start | bytes 786440 | tf_op jit(solution)/shard_map/ppermute | solution.py:286
  26.8 0.0 collective-permute-done.1.after
  26.8 1.9 %collective-permute-start.2 = (bf16[64,2048]{1,0:T(8,128)(2,1)S(1)}, bf16[64,2048]{1,0:T(8,128)(2,1)S(1)}, u32[]{:S(2)}, u32[]{:S(2)}) collective-permute-start(bf16[64,2048]{1,0:T(8,128)(2,1)S(1)} %collective-permute-done.1.after), channel_id=1, source_target_pairs={{0,4},{4,0},{1,5},{5,1},{2,6},{6,2},{3,7},{7,3},{8,12},{12,8},{9,1... | collective-permute-start | bytes 786440 | tf_op jit(solution)/shard_map/ppermute | solution.py:289
  29.4 0.0 copy-start
  29.4 0.0 copy-start.1
  29.4 0.9 turned.1.adj
  30.3 0.0 collective-permute-done.3.beside
  30.3 0.6 collective-permute-done.before
  30.9 0.0 collective-permute-done.2.across
  30.9 0.0 copy-done
  30.9 0.0 copy-done.1
  30.9 1.8 %aggregate.1 = bf16[4,64,512]{2,1,0:T(8,128)(2,1)S(1)} custom-call(s32[1]{0:T(128)S(6)} %copy.17.count_ref, s32[1,96]{1,0:T(1,128)S(1)} %copy-done, s32[1,96]{1,0:T(1,128)S(1)} %copy-done.1, bf16[64,2048]{1,0:T(8,128)(2,1)S(1)} %collective-permute-done.before, bf16[64,2048]{1,0:T(8,128)(2,1)S(1)} %collective-permute-done.2.across, ...), custom_call_target="tpu_custom_call" | custom-call | flops 4000000000 | bytes 4194304 | tf_op jit(solution)/shard_map/aggregate/pallas_call | solution.py:323
  32.7 9.3 %all_to_all.25 = bf16[4,64,512]{2,1,0:T(8,128)(2,1)S(1)} all-to-all(bf16[4,64,512]{2,1,0:T(8,128)(2,1)S(1)} %aggregate.1), channel_id=1, replica_groups=mesh['z'=12,'y'=8,'c'=2,'x'=4] {'x'}, dimensions={0} | all-to-all | bytes 524288 | tf_op jit(solution)/shard_map/all_to_all | solution.py:337
  42.0 2.1 %dense.1 = (bf16[256,512]{1,0:T(8,128)(2,1)}, bf16[4,144,512]{2,1,0:T(8,128)(2,1)S(1)}) custom-call(bf16[256,512]{1,0:T(8,128)(2,1)S(1)} %bitcast.8, bf16[256,256]{1,0:T(8,128)(2,1)} %weight_hbm.1, f32[1,256]{1,0:T(1,128)} %bitcast.9, bf16[256,512]{1,0:T(8,128)(2,1)} %cot_hbm.1), custom_call_target="tpu_custom_call" | custom-call | flops 1000000000 | bytes 1048576 | tf_op jit(solution)/shard_map/dense/pallas_call | solution.py:339
  44.2 9.7 %all_to_all.26.recv = bf16[4,144,512]{2,1,0:T(8,128)(2,1)S(1)} all-to-all(bf16[4,144,512]{2,1,0:T(8,128)(2,1)S(1)} %get-tuple-element.25), channel_id=1, replica_groups=mesh['z'=12,'y'=8,'c'=2,'x'=4] {'x'}, dimensions={0} | all-to-all | bytes 1179648 | tf_op jit(solution)/shard_map/all_to_all | solution.py:358
  53.9 0.8 first_sum.1
  54.6 10.4 %all-to-all-start.2 = ((f32[16,16,128]{2,1,0:T(8,128)}), f32[16,16,128]{2,1,0:T(8,128)S(1)}, u32[]{:S(2)}, u32[]{:S(2)}) async-start(f32[16,16,128]{2,1,0:T(8,128)} %get-tuple-element.26), calls=%async_computation.2 | async-start | bytes 262144 | tf_op jit(solution)/shard_map/all_to_all | solution.py:373
  65.0 3.9 %spread_back.1 = (bf16[16,64,128]{2,1,0:T(8,128)(2,1)}, bf16[2,16,64,128]{3,2,1,0:T(8,128)(2,1)}, f32[16,64,128]{2,1,0:T(8,128)}, f32[16,64,128]{2,1,0:T(8,128)}, f32[8,128]{1,0:T(8,128)S(1)}) custom-call(s32[1]{0:T(128)S(6)} %copy.17.count_ref, s32[1,96]{1,0:T(1,128)} %dest_hbm.1, s32[1,96]{1,0:T(1,128)} %src_hbm.1, ...), custom_call_target="tpu_custom_call" | custom-call | flops 4000000000 | bytes 4194304 | tf_op jit(solution)/shard_map/spread_back/pallas_call | solution.py:375
  69.0 2.1 %collective-permute-start.4 = (bf16[2,16,64,128]{3,2,1,0:T(8,128)(2,1)}, bf16[2,16,64,128]{3,2,1,0:T(8,128)(2,1)S(1)}, u32[]{:S(2)}, u32[]{:S(2)}) collective-permute-start(bf16[2,16,64,128]{3,2,1,0:T(8,128)(2,1)} %get-tuple-element.33), channel_id=1, source_target_pairs={{0,4},{4,0},{1,5},{5,1},{2,6},{6,2},{3,7},{7,3},{8,12},{12,8},{9,1... | collective-permute-start | bytes 1572872 | tf_op jit(solution)/shard_map/ppermute | solution.py:289
  71.1 3.1 %all-to-all-done.2.recv = f32[16,16,128]{2,1,0:T(8,128)S(1)} async-done(((f32[16,16,128]{2,1,0:T(8,128)}), f32[16,16,128]{2,1,0:T(8,128)S(1)}, u32[]{:S(2)}, u32[]{:S(2)}) %all-to-all-start.2) | async-done | bytes 131104 | tf_op jit(solution)/shard_map/all_to_all | solution.py:373
  74.2 0.0 copy-start.2
  74.2 0.7 sum_to_all.1
  74.9 3.7 %all-to-all-start.3 = ((f32[12,16,128]{2,1,0:T(8,128)}), f32[12,16,128]{2,1,0:T(8,128)S(1)}, u32[]{:S(2)}, u32[]{:S(2)}) async-start(f32[12,16,128]{2,1,0:T(8,128)} %get-tuple-element.30), calls=%async_computation.3 | async-start | bytes 196608 | tf_op jit(solution)/shard_map/all_to_all | solution.py:413
  78.6 2.0 %collective-permute-start.5 = (bf16[16,64,128]{2,1,0:T(8,128)(2,1)}, bf16[16,64,128]{2,1,0:T(8,128)(2,1)S(1)}, u32[]{:S(2)}, u32[]{:S(2)}) collective-permute-start(bf16[16,64,128]{2,1,0:T(8,128)(2,1)} %get-tuple-element.35), channel_id=1, source_target_pairs={{0,760},{4,12},{8,0},{12,20},{16,8},{20,28},{24,16},{28,36},{32,24... | collective-permute-start | bytes 786440 | tf_op jit(solution)/shard_map/ppermute | solution.py:286
  80.6 0.0 collective-permute-done.4.pair_hbm
  80.6 0.0 copy-done.2
  80.6 0.1 fusion.token
  80.7 6.6 %collective-permute-start.6 = (bf16[16,64,128]{2,1,0:T(8,128)(2,1)S(1)}, bf16[16,64,128]{2,1,0:T(8,128)(2,1)S(1)}, u32[]{:S(2)}, u32[]{:S(2)}) collective-permute-start(bf16[16,64,128]{2,1,0:T(8,128)(2,1)S(1)} %fusion.token), channel_id=1, source_target_pairs={{0,8},{4,764},{8,16},{12,4},{16,24},{20,12},{24,32},{28,20},{32,40... | collective-permute-start | bytes 786440 | tf_op jit(solution)/shard_map/ppermute | solution.py:286
  87.3 2.0 %all-to-all-done.3.recv = f32[12,16,128]{2,1,0:T(8,128)S(1)} async-done(((f32[12,16,128]{2,1,0:T(8,128)}), f32[12,16,128]{2,1,0:T(8,128)S(1)}, u32[]{:S(2)}, u32[]{:S(2)}) %all-to-all-start.3) | async-done | bytes 98336 | tf_op jit(solution)/shard_map/all_to_all | solution.py:413
  89.3 1.3 %last_sum.1 = (f32[64,8,128]{2,1,0:T(8,128)}, f32[16,64,128]{2,1,0:T(8,128)}, f32[1,256]{1,0:T(1,128)}) custom-call(f32[12,16,128]{2,1,0:T(8,128)S(1)} %all-to-all-done.3.recv, f32[16,64,128]{2,1,0:T(8,128)} %get-tuple-element.31.own_hbm, bf16[16,64,128]{2,1,0:T(8,128)(2,1)S(1)} %fusion.token), custom_call_target="tpu_custom_call", output_to_operand_aliasing={{1}: (1, {})} | custom-call | tf_op jit(solution)/shard_map/last_sum/pallas_call | solution.py:420
  90.6 6.7 %all-to-all-start.4 = ((f32[64,8,128]{2,1,0:T(8,128)}), f32[64,8,128]{2,1,0:T(8,128)S(1)}, u32[]{:S(2)}, u32[]{:S(2)}) async-start(f32[64,8,128]{2,1,0:T(8,128)} %get-tuple-element.37), calls=%async_computation.4 | async-start | bytes 524288 | tf_op jit(solution)/shard_map/all_to_all | solution.py:434
  97.3 0.0 collective-permute-done.5.first_hbm
  97.3 0.0 collective-permute-done.6.last_hbm
  97.3 4.5 %out_of_order.1 = (bf16[64,2048]{1,0:T(8,128)(2,1)}, f32[8,128]{1,0:T(8,128)S(1)}) custom-call(s32[1,2048]{1,0:T(1,128)} %order_hbm.3, f32[16,64,128]{2,1,0:T(8,128)} %get-tuple-element.34.own_hbm, bf16[16,64,128]{2,1,0:T(8,128)(2,1)S(1)} %collective-permute-done.5.first_hbm, bf16[2,16,64,128]{3,2,1,0:T(8,128)(2,1)S(1)} %collective-permute-done.4.pair_hbm, ...), custom_call_target="tpu_custom_call" | custom-call | flops 3000000000 | bytes 2097152 | tf_op jit(solution)/shard_map/out_of_order/pallas_call | solution.py:436
  101.8 7.7 %all-to-all-done.4.recv = f32[64,8,128]{2,1,0:T(8,128)S(1)} async-done(((f32[64,8,128]{2,1,0:T(8,128)}), f32[64,8,128]{2,1,0:T(8,128)S(1)}, u32[]{:S(2)}, u32[]{:S(2)}) %all-to-all-start.4) | async-done | bytes 262176 | tf_op jit(solution)/shard_map/all_to_all | solution.py:434
  109.6 0.7 put_together.1
Async XLA Ops:
  2.9 23.9 %collective-permute-start.1 = (bf16[64,2048]{1,0:T(8,128)(2,1)S(1)}, bf16[64,2048]{1,0:T(8,128)(2,1)S(1)}, u32[]{:S(2)}, u32[]{:S(2)}) collective-permute-start(bf16[64,2048]{1,0:T(8,128)(2,1)S(1)} %get-tuple-element.22.permuted), channel_id=1, source_target_pairs={{0,760},{4,12},{8,0},{12,20},{16,8},{20,28},{24,16},{28,36},{32,24... | collective-permute-start | bytes 786440 | tf_op jit(solution)/shard_map/ppermute | solution.py:286
  6.9 23.3 %collective-permute-start.3 = (bf16[64,2048]{1,0:T(8,128)(2,1)S(1)}, bf16[64,2048]{1,0:T(8,128)(2,1)S(1)}, u32[]{:S(2)}, u32[]{:S(2)}) collective-permute-start(bf16[64,2048]{1,0:T(8,128)(2,1)S(1)} %get-tuple-element.22.permuted), channel_id=1, source_target_pairs={{0,4},{4,0},{1,5},{5,1},{2,6},{6,2},{3,7},{7,3},{8,12},{12,8},{9,1... | collective-permute-start | bytes 786440 | tf_op jit(solution)/shard_map/ppermute | solution.py:289
  23.8 7.1 %collective-permute-start = (bf16[64,2048]{1,0:T(8,128)(2,1)S(1)}, bf16[64,2048]{1,0:T(8,128)(2,1)S(1)}, u32[]{:S(2)}, u32[]{:S(2)}) collective-permute-start(bf16[64,2048]{1,0:T(8,128)(2,1)S(1)} %get-tuple-element.22.permuted), channel_id=1, source_target_pairs={{0,8},{4,764},{8,16},{12,4},{16,24},{20,12},{24,32},{28,20},{32,40... | collective-permute-start | bytes 786440 | tf_op jit(solution)/shard_map/ppermute | solution.py:286
  26.8 4.1 %collective-permute-start.2 = (bf16[64,2048]{1,0:T(8,128)(2,1)S(1)}, bf16[64,2048]{1,0:T(8,128)(2,1)S(1)}, u32[]{:S(2)}, u32[]{:S(2)}) collective-permute-start(bf16[64,2048]{1,0:T(8,128)(2,1)S(1)} %collective-permute-done.1.after), channel_id=1, source_target_pairs={{0,4},{4,0},{1,5},{5,1},{2,6},{6,2},{3,7},{7,3},{8,12},{12,8},{9,1... | collective-permute-start | bytes 786440 | tf_op jit(solution)/shard_map/ppermute | solution.py:289
  29.4 1.5 %copy-start = (s32[1,96]{1,0:T(1,128)S(1)}, s32[1,96]{1,0:T(1,128)}, u32[]{:S(2)}) copy-start(s32[1,96]{1,0:T(1,128)} %dest_hbm.1) | copy-start | bytes 1156
  29.4 1.5 %copy-start.1 = (s32[1,96]{1,0:T(1,128)S(1)}, s32[1,96]{1,0:T(1,128)}, u32[]{:S(2)}) copy-start(s32[1,96]{1,0:T(1,128)} %src_hbm.1) | copy-start | bytes 1156
  54.6 19.6 %all-to-all-start.2 = ((f32[16,16,128]{2,1,0:T(8,128)}), f32[16,16,128]{2,1,0:T(8,128)S(1)}, u32[]{:S(2)}, u32[]{:S(2)}) async-start(f32[16,16,128]{2,1,0:T(8,128)} %get-tuple-element.26), calls=%async_computation.2 | async-start | bytes 262144 | tf_op jit(solution)/shard_map/all_to_all | solution.py:373
  69.0 11.6 %collective-permute-start.4 = (bf16[2,16,64,128]{3,2,1,0:T(8,128)(2,1)}, bf16[2,16,64,128]{3,2,1,0:T(8,128)(2,1)S(1)}, u32[]{:S(2)}, u32[]{:S(2)}) collective-permute-start(bf16[2,16,64,128]{3,2,1,0:T(8,128)(2,1)} %get-tuple-element.33), channel_id=1, source_target_pairs={{0,4},{4,0},{1,5},{5,1},{2,6},{6,2},{3,7},{7,3},{8,12},{12,8},{9,1... | collective-permute-start | bytes 1572872 | tf_op jit(solution)/shard_map/ppermute | solution.py:289
  74.2 6.4 %copy-start.2 = (f32[16,64,128]{2,1,0:T(8,128)S(1)}, f32[16,64,128]{2,1,0:T(8,128)}, u32[]{:S(2)}) copy-start(f32[16,64,128]{2,1,0:T(8,128)} %get-tuple-element.32) | copy-start | bytes 1572868
  74.9 14.4 %all-to-all-start.3 = ((f32[12,16,128]{2,1,0:T(8,128)}), f32[12,16,128]{2,1,0:T(8,128)S(1)}, u32[]{:S(2)}, u32[]{:S(2)}) async-start(f32[12,16,128]{2,1,0:T(8,128)} %get-tuple-element.30), calls=%async_computation.3 | async-start | bytes 196608 | tf_op jit(solution)/shard_map/all_to_all | solution.py:413
  78.6 18.7 %collective-permute-start.5 = (bf16[16,64,128]{2,1,0:T(8,128)(2,1)}, bf16[16,64,128]{2,1,0:T(8,128)(2,1)S(1)}, u32[]{:S(2)}, u32[]{:S(2)}) collective-permute-start(bf16[16,64,128]{2,1,0:T(8,128)(2,1)} %get-tuple-element.35), channel_id=1, source_target_pairs={{0,760},{4,12},{8,0},{12,20},{16,8},{20,28},{24,16},{28,36},{32,24... | collective-permute-start | bytes 786440 | tf_op jit(solution)/shard_map/ppermute | solution.py:286
  80.7 16.6 %collective-permute-start.6 = (bf16[16,64,128]{2,1,0:T(8,128)(2,1)S(1)}, bf16[16,64,128]{2,1,0:T(8,128)(2,1)S(1)}, u32[]{:S(2)}, u32[]{:S(2)}) collective-permute-start(bf16[16,64,128]{2,1,0:T(8,128)(2,1)S(1)} %fusion.token), channel_id=1, source_target_pairs={{0,8},{4,764},{8,16},{12,4},{16,24},{20,12},{24,32},{28,20},{32,40... | collective-permute-start | bytes 786440 | tf_op jit(solution)/shard_map/ppermute | solution.py:286
  90.6 19.0 %all-to-all-start.4 = ((f32[64,8,128]{2,1,0:T(8,128)}), f32[64,8,128]{2,1,0:T(8,128)S(1)}, u32[]{:S(2)}, u32[]{:S(2)}) async-start(f32[64,8,128]{2,1,0:T(8,128)} %get-tuple-element.37), calls=%async_computation.4 | async-start | bytes 524288 | tf_op jit(solution)/shard_map/all_to_all | solution.py:434

commit v5 on v4

--- a/solution.py
+++ b/solution.py
@@ -92,14 +92,14 @@
         out_ref[:, start : start + TILE] = moved.astype(BF16)
 
 
-def sum_to_all(recv, first_hbm, token, out_hbm, kept_hbm, out, sems):
+def sum_to_all(recv, token, out_hbm, out, sems):
     total = jnp.sum(recv[...], axis=0)
     for i in range(out.shape[0]):
         out[i] = total
     started([(out, out_hbm)], sems)[0].wait()
 
 
-def last_sum(scale, recv, own_hbm, token, out_hbm, kept_hbm, bias_ref, out, sems):
+def last_sum(scale, recv, own_hbm, token, returned, out_hbm, kept_hbm, bias_ref, out, sems):
     total = jnp.sum(recv[...], axis=0) * scale
     for i in range(out.shape[0]):
         out[i] = total[0:8]
@@ -128,7 +128,7 @@
 
 
 def aggregate(
-    count_ref, dest, src, before, across, permuted, beside, after, adj, out_ref, win, acc
+    count_ref, dest, src, beside, across, permuted, before, after, adj, out_ref, win, acc
 ):
     slots = adj.shape[0]
     nblocks = acc.shape[0] - 1
@@ -306,7 +306,7 @@
         name="into_order",
     )(*in_hbm(node_order, features, adj_values))
 
-    across_adj = pl.pallas_call(
+    adj_turned = pl.pallas_call(
         turned,
         out_shape=jax.ShapeDtypeStruct(adj_values.shape, BF16),
         in_specs=[VMEM],
@@ -332,7 +332,7 @@
         compiler_params=PARAMS,
         cost_estimate=cost(4 * 10**9, 2**22),
         name="aggregate",
-    )(blk_count, *in_smem(blk_dest, blk_src), before, across, permuted, beside, after, across_adj)
+    )(blk_count, *in_smem(blk_dest, blk_src), beside, across, permuted, before, after, adj_turned)
 
     hidden_rows = lax.all_to_all(hidden, "x", 0, 0).reshape(parts * feat, width)
 
@@ -399,17 +399,16 @@
         name="spread_back",
     )(blk_count, *in_hbm(blk_dest, blk_src, grads, adj_values))
 
-    partial, first = pl.pallas_call(
+    partial = pl.pallas_call(
         sum_to_all,
-        out_shape=(pltpu.HBM((zs, 16, BLOCK), F32), pltpu.HBM(first.shape, BF16)),
-        in_specs=[VMEM, HBM, ANY],
-        out_specs=(HBM, HBM),
+        out_shape=pltpu.HBM((zs, 16, BLOCK), F32),
+        in_specs=[VMEM, ANY],
+        out_specs=HBM,
         scratch_shapes=[pltpu.VMEM((zs, 16, BLOCK), F32), dma((1,))],
-        input_output_aliases={1: 1},
         compiler_params=PARAMS,
         cost_estimate=cost(3 * 10**10, 2**20),
         name="sum_to_all",
-    )(partial, *in_hbm(first), token)
+    )(partial, token)
     partial = lax.all_to_all(partial, "z", 0, 0)
 
     pair = sibling(pair)
@@ -424,13 +423,13 @@
             pltpu.HBM(own.shape, F32),
             jax.ShapeDtypeStruct((1, out_feat), F32),
         ),
-        in_specs=[VMEM, HBM, ANY],
+        in_specs=[VMEM, HBM, ANY, ANY],
         out_specs=(HBM, HBM, VMEM),
         scratch_shapes=[pltpu.VMEM((2 * ys * parts, 8, BLOCK), F32), dma((1,))],
         input_output_aliases={1: 1},
         compiler_params=PARAMS,
         name="last_sum",
-    )(partial, *in_hbm(own), last)
+    )(partial, *in_hbm(own), last, from_first)
     pieces = lax.all_to_all(pieces, ("y", "c", "x"), 0, 0)
 
     grad_x, token = pl.pallas_call(

time: 111 us -> 114 us (1.027)
  starting transfers between devices: 57.3 us -> 59.9 us
    ppermute x4, starting transfers between devices: 15.6 us -> 27.6 us  [chip_step(): return lax.ppermute(value, ROWS, pairs)]
    ppermute x3, starting transfers between devices: 20.9 us -> 14.4 us  [sibling(): return lax.ppermute(value, 'c', [(0, 1), (1, 0)])]
    all_to_all x1, waiting for transfers between devices: 1.99 us -> 6.19 us  [on_device(): partial = lax.all_to_all(partial, 'z', 0, 0)]
    all_to_all x1, waiting for transfers between devices: 3.12 us -> 0.01 us  [on_device(): partial = lax.all_to_all(partial, ('y', 'c'), 0, 0)]
    all_to_all x1, starting transfers between devices: 10.4 us -> 8.12 us  [on_device(): partial = lax.all_to_all(partial, ('y', 'c'), 0, 0)]
  transfers between devices with their start and end apart: 10 -> 10, of which waited for: 4 -> 2; matrix products, arithmetic and copies ran while one was open for 0% -> 0% of each run, Pallas kernels for 10% -> 10%
where the time goes in v5:
time: 114 us; the launch traced here: 113 us
  starting transfers between devices  59.9 us (53%)
  blocking collectives  19 us (17%)
  Pallas kernels  18.9 us (17%)
  waiting for transfers between devices  13.9 us (12%)
  between operations  1.54 us (1%)
    ppermute x4, starting transfers between devices, chip_step(): return lax.ppermute(value, ROWS, pairs)  27.6 us
    ppermute x3, starting transfers between devices, sibling(): return lax.ppermute(value, 'c', [(0, 1), (1, 0)])  14.4 us
    all_to_all x1, blocking collectives, on_device(): recv = lax.all_to_all(send, 'x', 0, 0)  9.67 us
    all_to_all x1, blocking collectives, on_device(): hidden_rows = lax.all_to_all(hidden, 'x', 0, 0).reshape(parts * feat, width)  9.35 us
    all_to_all x1, starting transfers between devices, on_device(): partial = lax.all_to_all(partial, ('y', 'c'), 0, 0)  8.12 us
    all_to_all x1, waiting for transfers between devices, on_device(): pieces = lax.all_to_all(pieces, ('y', 'c', 'x'), 0, 0)  7.74 us
    all_to_all x1, starting transfers between devices, on_device(): pieces = lax.all_to_all(pieces, ('y', 'c', 'x'), 0, 0)  6.26 us
    all_to_all x1, waiting for transfers between devices, on_device(): partial = lax.all_to_all(partial, 'z', 0, 0)  6.19 us
  transfers between devices with their start and end apart: 10, of which 2 were waited for; matrix products, arithmetic and copies ran while one was open for 0% of the time, Pallas kernels for 10%

profile of v5, /device:TPU:1, one launch (start us, length us, event | category | flops | bytes accessed | tf_op | source)
XLA Modules:
  0.0 113.3 jit_solution(9939918350821108877)
XLA Ops:
  0.6 2.2 %into_order.1 = (bf16[64,2048]{1,0:T(8,128)(2,1)S(1)}, bf16[96,128,128]{2,1,0:T(8,128)(2,1)S(1)}) custom-call(s32[1,2048]{1,0:T(1,128)} %order_hbm.3, bf16[64,2048]{1,0:T(8,128)(2,1)} %x_hbm.1, bf16[96,128,128]{2,1,0:T(8,128)(2,1)} %adj_hbm.3), custom_call_target="tpu_custom_call" | custom-call | flops 1000000000 | bytes 1048576 | tf_op jit(solution)/shard_map/into_order/pallas_call | solution.py:294
  2.9 4.0 %collective-permute-start.1 = (bf16[64,2048]{1,0:T(8,128)(2,1)S(1)}, bf16[64,2048]{1,0:T(8,128)(2,1)S(1)}, u32[]{:S(2)}, u32[]{:S(2)}) collective-permute-start(bf16[64,2048]{1,0:T(8,128)(2,1)S(1)} %get-tuple-element.20.permuted), channel_id=1, source_target_pairs={{0,760},{4,12},{8,0},{12,20},{16,8},{20,28},{24,16},{28,36},{32,24... | collective-permute-start | bytes 786440 | tf_op jit(solution)/shard_map/ppermute | solution.py:286
  6.9 15.9 %collective-permute-start.3 = (bf16[64,2048]{1,0:T(8,128)(2,1)S(1)}, bf16[64,2048]{1,0:T(8,128)(2,1)S(1)}, u32[]{:S(2)}, u32[]{:S(2)}) collective-permute-start(bf16[64,2048]{1,0:T(8,128)(2,1)S(1)} %get-tuple-element.20.permuted), channel_id=1, source_target_pairs={{0,8},{4,764},{8,16},{12,4},{16,24},{20,12},{24,32},{28,20},{32,40... | collective-permute-start | bytes 786440 | tf_op jit(solution)/shard_map/ppermute | solution.py:286
  22.9 2.9 %collective-permute-start = (bf16[64,2048]{1,0:T(8,128)(2,1)S(1)}, bf16[64,2048]{1,0:T(8,128)(2,1)S(1)}, u32[]{:S(2)}, u32[]{:S(2)}) collective-permute-start(bf16[64,2048]{1,0:T(8,128)(2,1)S(1)} %get-tuple-element.20.permuted), channel_id=1, source_target_pairs={{0,4},{4,0},{1,5},{5,1},{2,6},{6,2},{3,7},{7,3},{8,12},{12,8},{9,1... | collective-permute-start | bytes 786440 | tf_op jit(solution)/shard_map/ppermute | solution.py:289
  25.7 0.0 collective-permute-done.1.after
  25.7 4.0 %collective-permute-start.2 = (bf16[64,2048]{1,0:T(8,128)(2,1)S(1)}, bf16[64,2048]{1,0:T(8,128)(2,1)S(1)}, u32[]{:S(2)}, u32[]{:S(2)}) collective-permute-start(bf16[64,2048]{1,0:T(8,128)(2,1)S(1)} %collective-permute-done.1.after), channel_id=1, source_target_pairs={{0,4},{4,0},{1,5},{5,1},{2,6},{6,2},{3,7},{7,3},{8,12},{12,8},{9,1... | collective-permute-start | bytes 786440 | tf_op jit(solution)/shard_map/ppermute | solution.py:289
  30.3 0.0 copy-start
  30.3 0.0 copy-start.1
  30.4 0.9 turned.1.adj
  31.2 0.0 collective-permute-done.3.before
  31.2 0.0 collective-permute-done.beside
  31.2 0.0 collective-permute-done.2.across
  31.3 0.0 copy-done
  31.3 0.0 copy-done.1
  31.3 1.8 %aggregate.1 = bf16[4,64,512]{2,1,0:T(8,128)(2,1)S(1)} custom-call(s32[1]{0:T(128)S(6)} %copy.15.count_ref, s32[1,96]{1,0:T(1,128)S(1)} %copy-done, s32[1,96]{1,0:T(1,128)S(1)} %copy-done.1, bf16[64,2048]{1,0:T(8,128)(2,1)S(1)} %collective-permute-done.beside, bf16[64,2048]{1,0:T(8,128)(2,1)S(1)} %collective-permute-done.2.across, ...), custom_call_target="tpu_custom_call" | custom-call | flops 4000000000 | bytes 4194304 | tf_op jit(solution)/shard_map/aggregate/pallas_call | solution.py:323
  33.1 9.3 %all_to_all.25 = bf16[4,64,512]{2,1,0:T(8,128)(2,1)S(1)} all-to-all(bf16[4,64,512]{2,1,0:T(8,128)(2,1)S(1)} %aggregate.1), channel_id=1, replica_groups=mesh['z'=12,'y'=8,'c'=2,'x'=4] {'x'}, dimensions={0} | all-to-all | bytes 524288 | tf_op jit(solution)/shard_map/all_to_all | solution.py:337
  42.4 2.1 %dense.1 = (bf16[256,512]{1,0:T(8,128)(2,1)}, bf16[4,144,512]{2,1,0:T(8,128)(2,1)S(1)}) custom-call(bf16[256,512]{1,0:T(8,128)(2,1)S(1)} %bitcast.8, bf16[256,256]{1,0:T(8,128)(2,1)} %weight_hbm.1, f32[1,256]{1,0:T(1,128)} %bitcast.9, bf16[256,512]{1,0:T(8,128)(2,1)} %cot_hbm.1), custom_call_target="tpu_custom_call" | custom-call | flops 1000000000 | bytes 1048576 | tf_op jit(solution)/shard_map/dense/pallas_call | solution.py:339
  44.5 9.7 %all_to_all.26.recv = bf16[4,144,512]{2,1,0:T(8,128)(2,1)S(1)} all-to-all(bf16[4,144,512]{2,1,0:T(8,128)(2,1)S(1)} %get-tuple-element.23), channel_id=1, replica_groups=mesh['z'=12,'y'=8,'c'=2,'x'=4] {'x'}, dimensions={0} | all-to-all | bytes 1179648 | tf_op jit(solution)/shard_map/all_to_all | solution.py:358
  54.2 0.8 first_sum.1
  55.0 8.1 %all-to-all-start.2 = ((f32[16,16,128]{2,1,0:T(8,128)}), f32[16,16,128]{2,1,0:T(8,128)S(1)}, u32[]{:S(2)}, u32[]{:S(2)}) async-start(f32[16,16,128]{2,1,0:T(8,128)} %get-tuple-element.24), calls=%async_computation.2 | async-start | bytes 262144 | tf_op jit(solution)/shard_map/all_to_all | solution.py:373
  63.1 3.9 %spread_back.1 = (bf16[16,64,128]{2,1,0:T(8,128)(2,1)}, bf16[2,16,64,128]{3,2,1,0:T(8,128)(2,1)}, f32[16,64,128]{2,1,0:T(8,128)}, f32[16,64,128]{2,1,0:T(8,128)}, f32[8,128]{1,0:T(8,128)S(1)}) custom-call(s32[1]{0:T(128)S(6)} %copy.15.count_ref, s32[1,96]{1,0:T(1,128)} %dest_hbm.1, s32[1,96]{1,0:T(1,128)} %src_hbm.1, ...), custom_call_target="tpu_custom_call" | custom-call | flops 4000000000 | bytes 4194304 | tf_op jit(solution)/shard_map/spread_back/pallas_call | solution.py:375
  67.0 3.3 %collective-permute-start.5 = (bf16[16,64,128]{2,1,0:T(8,128)(2,1)}, bf16[16,64,128]{2,1,0:T(8,128)(2,1)S(1)}, u32[]{:S(2)}, u32[]{:S(2)}) collective-permute-start(bf16[16,64,128]{2,1,0:T(8,128)(2,1)} %get-tuple-element.30), channel_id=1, source_target_pairs={{0,760},{4,12},{8,0},{12,20},{16,8},{20,28},{24,16},{28,36},{32,24... | collective-permute-start | bytes 786440 | tf_op jit(solution)/shard_map/ppermute | solution.py:286
  70.4 7.6 %collective-permute-start.4 = (bf16[2,16,64,128]{3,2,1,0:T(8,128)(2,1)}, bf16[2,16,64,128]{3,2,1,0:T(8,128)(2,1)S(1)}, u32[]{:S(2)}, u32[]{:S(2)}) collective-permute-start(bf16[2,16,64,128]{3,2,1,0:T(8,128)(2,1)} %get-tuple-element.29), channel_id=1, source_target_pairs={{0,4},{4,0},{1,5},{5,1},{2,6},{6,2},{3,7},{7,3},{8,12},{12,8},{9,1... | collective-permute-start | bytes 1572872 | tf_op jit(solution)/shard_map/ppermute | solution.py:289
  77.9 0.0 all-to-all-done.2.recv
  77.9 0.0 copy-start.2
  77.9 0.7 sum_to_all.1
  78.6 3.5 %all-to-all-start.3 = ((f32[12,16,128]{2,1,0:T(8,128)}), f32[12,16,128]{2,1,0:T(8,128)S(1)}, u32[]{:S(2)}, u32[]{:S(2)}) async-start(f32[12,16,128]{2,1,0:T(8,128)} %sum_to_all.1), calls=%async_computation.3 | async-start | bytes 196608 | tf_op jit(solution)/shard_map/all_to_all | solution.py:412
  82.1 0.0 collective-permute-done.4.pair_hbm
  82.2 0.0 copy-done.2
  82.2 0.1 fusion.token
  82.2 4.3 %collective-permute-start.6 = (bf16[16,64,128]{2,1,0:T(8,128)(2,1)S(1)}, bf16[16,64,128]{2,1,0:T(8,128)(2,1)S(1)}, u32[]{:S(2)}, u32[]{:S(2)}) collective-permute-start(bf16[16,64,128]{2,1,0:T(8,128)(2,1)S(1)} %fusion.token), channel_id=1, source_target_pairs={{0,8},{4,764},{8,16},{12,4},{16,24},{20,12},{24,32},{28,20},{32,40... | collective-permute-start | bytes 786440 | tf_op jit(solution)/shard_map/ppermute | solution.py:286
  86.6 0.0 collective-permute-done.5.returned.first_hbm
  86.6 6.2 %all-to-all-done.3.recv = f32[12,16,128]{2,1,0:T(8,128)S(1)} async-done(((f32[12,16,128]{2,1,0:T(8,128)}), f32[12,16,128]{2,1,0:T(8,128)S(1)}, u32[]{:S(2)}, u32[]{:S(2)}) %all-to-all-start.3) | async-done | bytes 98336 | tf_op jit(solution)/shard_map/all_to_all | solution.py:412
  92.8 1.3 %last_sum.1 = (f32[64,8,128]{2,1,0:T(8,128)}, f32[16,64,128]{2,1,0:T(8,128)}, f32[1,256]{1,0:T(1,128)}) custom-call(f32[12,16,128]{2,1,0:T(8,128)S(1)} %all-to-all-done.3.recv, f32[16,64,128]{2,1,0:T(8,128)} %get-tuple-element.27.own_hbm, bf16[16,64,128]{2,1,0:T(8,128)(2,1)S(1)} %fusion.token, ...), custom_call_target="tpu_custom_call", output_to_operand_aliasing={{1}: (1, {})} | custom-call | tf_op jit(solution)/shard_map/last_sum/pallas_call | solution.py:419
  94.1 6.3 %all-to-all-start.4 = ((f32[64,8,128]{2,1,0:T(8,128)}), f32[64,8,128]{2,1,0:T(8,128)S(1)}, u32[]{:S(2)}, u32[]{:S(2)}) async-start(f32[64,8,128]{2,1,0:T(8,128)} %get-tuple-element.33), calls=%async_computation.4 | async-start | bytes 524288 | tf_op jit(solution)/shard_map/all_to_all | solution.py:433
  100.3 0.0 collective-permute-done.6.last_hbm
  100.3 4.5 %out_of_order.1 = (bf16[64,2048]{1,0:T(8,128)(2,1)}, f32[8,128]{1,0:T(8,128)S(1)}) custom-call(s32[1,2048]{1,0:T(1,128)} %order_hbm.3, f32[16,64,128]{2,1,0:T(8,128)} %get-tuple-element.31.own_hbm, bf16[16,64,128]{2,1,0:T(8,128)(2,1)S(1)} %collective-permute-done.5.returned.first_hbm, bf16[2,16,64,128]{3,2,1,0:T(8,128)(2,1)S(1)} %collective-permute-done.4.pair_hbm, ...), custom_call_target="tpu_custom_call" | custom-call | flops 3000000000 | bytes 2097152 | tf_op jit(solution)/shard_map/out_of_order/pallas_call | solution.py:435
  104.9 7.7 %all-to-all-done.4.recv = f32[64,8,128]{2,1,0:T(8,128)S(1)} async-done(((f32[64,8,128]{2,1,0:T(8,128)}), f32[64,8,128]{2,1,0:T(8,128)S(1)}, u32[]{:S(2)}, u32[]{:S(2)}) %all-to-all-start.4) | async-done | bytes 262176 | tf_op jit(solution)/shard_map/all_to_all | solution.py:433
  112.6 0.7 put_together.1
Async XLA Ops:
  2.9 22.9 %collective-permute-start.1 = (bf16[64,2048]{1,0:T(8,128)(2,1)S(1)}, bf16[64,2048]{1,0:T(8,128)(2,1)S(1)}, u32[]{:S(2)}, u32[]{:S(2)}) collective-permute-start(bf16[64,2048]{1,0:T(8,128)(2,1)S(1)} %get-tuple-element.20.permuted), channel_id=1, source_target_pairs={{0,760},{4,12},{8,0},{12,20},{16,8},{20,28},{24,16},{28,36},{32,24... | collective-permute-start | bytes 786440 | tf_op jit(solution)/shard_map/ppermute | solution.py:286
  6.9 24.3 %collective-permute-start.3 = (bf16[64,2048]{1,0:T(8,128)(2,1)S(1)}, bf16[64,2048]{1,0:T(8,128)(2,1)S(1)}, u32[]{:S(2)}, u32[]{:S(2)}) collective-permute-start(bf16[64,2048]{1,0:T(8,128)(2,1)S(1)} %get-tuple-element.20.permuted), channel_id=1, source_target_pairs={{0,8},{4,764},{8,16},{12,4},{16,24},{20,12},{24,32},{28,20},{32,40... | collective-permute-start | bytes 786440 | tf_op jit(solution)/shard_map/ppermute | solution.py:286
  22.9 8.4 %collective-permute-start = (bf16[64,2048]{1,0:T(8,128)(2,1)S(1)}, bf16[64,2048]{1,0:T(8,128)(2,1)S(1)}, u32[]{:S(2)}, u32[]{:S(2)}) collective-permute-start(bf16[64,2048]{1,0:T(8,128)(2,1)S(1)} %get-tuple-element.20.permuted), channel_id=1, source_target_pairs={{0,4},{4,0},{1,5},{5,1},{2,6},{6,2},{3,7},{7,3},{8,12},{12,8},{9,1... | collective-permute-start | bytes 786440 | tf_op jit(solution)/shard_map/ppermute | solution.py:289
  25.7 5.5 %collective-permute-start.2 = (bf16[64,2048]{1,0:T(8,128)(2,1)S(1)}, bf16[64,2048]{1,0:T(8,128)(2,1)S(1)}, u32[]{:S(2)}, u32[]{:S(2)}) collective-permute-start(bf16[64,2048]{1,0:T(8,128)(2,1)S(1)} %collective-permute-done.1.after), channel_id=1, source_target_pairs={{0,4},{4,0},{1,5},{5,1},{2,6},{6,2},{3,7},{7,3},{8,12},{12,8},{9,1... | collective-permute-start | bytes 786440 | tf_op jit(solution)/shard_map/ppermute | solution.py:289
  30.3 0.9 copy-start
  30.3 0.9 copy-start.1
  55.0 22.9 %all-to-all-start.2 = ((f32[16,16,128]{2,1,0:T(8,128)}), f32[16,16,128]{2,1,0:T(8,128)S(1)}, u32[]{:S(2)}, u32[]{:S(2)}) async-start(f32[16,16,128]{2,1,0:T(8,128)} %get-tuple-element.24), calls=%async_computation.2 | async-start | bytes 262144 | tf_op jit(solution)/shard_map/all_to_all | solution.py:373
  67.0 19.6 %collective-permute-start.5 = (bf16[16,64,128]{2,1,0:T(8,128)(2,1)}, bf16[16,64,128]{2,1,0:T(8,128)(2,1)S(1)}, u32[]{:S(2)}, u32[]{:S(2)}) collective-permute-start(bf16[16,64,128]{2,1,0:T(8,128)(2,1)} %get-tuple-element.30), channel_id=1, source_target_pairs={{0,760},{4,12},{8,0},{12,20},{16,8},{20,28},{24,16},{28,36},{32,24... | collective-permute-start | bytes 786440 | tf_op jit(solution)/shard_map/ppermute | solution.py:286
  70.4 11.8 %collective-permute-start.4 = (bf16[2,16,64,128]{3,2,1,0:T(8,128)(2,1)}, bf16[2,16,64,128]{3,2,1,0:T(8,128)(2,1)S(1)}, u32[]{:S(2)}, u32[]{:S(2)}) collective-permute-start(bf16[2,16,64,128]{3,2,1,0:T(8,128)(2,1)} %get-tuple-element.29), channel_id=1, source_target_pairs={{0,4},{4,0},{1,5},{5,1},{2,6},{6,2},{3,7},{7,3},{8,12},{12,8},{9,1... | collective-permute-start | bytes 1572872 | tf_op jit(solution)/shard_map/ppermute | solution.py:289
  77.9 4.2 %copy-start.2 = (f32[16,64,128]{2,1,0:T(8,128)S(1)}, f32[16,64,128]{2,1,0:T(8,128)}, u32[]{:S(2)}) copy-start(f32[16,64,128]{2,1,0:T(8,128)} %get-tuple-element.28) | copy-start | bytes 1572868
  78.6 14.1 %all-to-all-start.3 = ((f32[12,16,128]{2,1,0:T(8,128)}), f32[12,16,128]{2,1,0:T(8,128)S(1)}, u32[]{:S(2)}, u32[]{:S(2)}) async-start(f32[12,16,128]{2,1,0:T(8,128)} %sum_to_all.1), calls=%async_computation.3 | async-start | bytes 196608 | tf_op jit(solution)/shard_map/all_to_all | solution.py:412
  82.2 18.1 %collective-permute-start.6 = (bf16[16,64,128]{2,1,0:T(8,128)(2,1)S(1)}, bf16[16,64,128]{2,1,0:T(8,128)(2,1)S(1)}, u32[]{:S(2)}, u32[]{:S(2)}) collective-permute-start(bf16[16,64,128]{2,1,0:T(8,128)(2,1)S(1)} %fusion.token), channel_id=1, source_target_pairs={{0,8},{4,764},{8,16},{12,4},{16,24},{20,12},{24,32},{28,20},{32,40... | collective-permute-start | bytes 786440 | tf_op jit(solution)/shard_map/ppermute | solution.py:286
  94.1 18.6 %all-to-all-start.4 = ((f32[64,8,128]{2,1,0:T(8,128)}), f32[64,8,128]{2,1,0:T(8,128)S(1)}, u32[]{:S(2)}, u32[]{:S(2)}) async-start(f32[64,8,128]{2,1,0:T(8,128)} %get-tuple-element.33), calls=%async_computation.4 | async-start | bytes 524288 | tf_op jit(solution)/shard_map/all_to_all | solution.py:433

commit v6 on v4

--- a/solution.py
+++ b/solution.py
@@ -63,7 +63,7 @@
 
 
 def out_of_order(
-    order_hbm, own_hbm, first_hbm, pair_hbm, last_hbm, out_ref, token_ref, order, own, first, near, last, total, sems
+    order_hbm, own_hbm, first_hbm, pair_hbm, last_hbm, out_ref, token_ref, order, own, first, near, last, total, stacked, sems
 ):
     copies = started(
         [
@@ -82,14 +82,20 @@
         sums = own[block] + near[block].astype(F32)
         sums = sums + first[block].astype(F32) + last[block].astype(F32)
         total[:, block * BLOCK : (block + 1) * BLOCK] = sums.astype(BF16)
-    count = total.shape[1]
-    for start in range(0, count, TILE):
-        rows = lax.broadcasted_iota(jnp.int32, (TILE, count), 0) + start
-        hot = jnp.where(order[...] == rows, 1.0, 0.0).astype(BF16)
-        moved = lax.dot_general(
-            total[...], hot, (((1,), (1,)), ((), ())), preferred_element_type=F32
-        )
-        out_ref[:, start : start + TILE] = moved.astype(BF16)
+    rows, count = total.shape
+    group, lane = split(order[...], BLOCK)
+    ids = lax.broadcasted_iota(jnp.int32, (BLOCK, count), 0)
+    hot = jnp.where(lane == ids, 1.0, 0.0).astype(BF16)
+    group = jnp.broadcast_to(group.astype(F32).astype(BF16), (rows, count))
+    values = total[...]
+    for g in range(count // BLOCK):
+        chosen = jnp.where(group == jnp.asarray(g, BF16), values, jnp.zeros_like(values))
+        stacked[g * rows : (g + 1) * rows, :] = chosen
+    moved = lax.dot_general(
+        stacked[...], hot, (((1,), (1,)), ((), ())), preferred_element_type=F32
+    ).astype(BF16)
+    for g in range(count // BLOCK):
+        out_ref[:, g * BLOCK : (g + 1) * BLOCK] = moved[g * rows : (g + 1) * rows]
 
 
 def sum_to_all(recv, first_hbm, token, out_hbm, kept_hbm, out, sems):
@@ -109,12 +115,16 @@
     copies[0].wait()
 
 
-def put_together(parts, recv, token, out_ref):
+def kept(recv, token, out_ref):
+    out_ref[...] = recv[...]
+
+
+def put_together(parts, recv, out_ref):
     rows = out_ref.shape[0] // parts
-    for i in range(recv.shape[0]):
-        y, c, x = i // (2 * parts), i // parts % 2, i % parts
-        row, lane = x * rows + 8 * y, c * BLOCK
-        out_ref[row : row + 8, lane : lane + BLOCK] = recv[i]
+    for c in range(recv.shape[0]):
+        for i in range(recv.shape[1]):
+            row, lane = i % parts * rows + 8 * (i // parts), c * BLOCK
+            out_ref[row : row + 8, lane : lane + BLOCK] = recv[c, i]
 
 
 def mirrored(source, core, nblocks, spread):
@@ -128,7 +138,7 @@
 
 
 def aggregate(
-    count_ref, dest, src, before, across, permuted, beside, after, adj, out_ref, win, acc
+    count_ref, dest, src, beside, across, permuted, before, after, adj, out_ref, win, acc
 ):
     slots = adj.shape[0]
     nblocks = acc.shape[0] - 1
@@ -306,7 +316,7 @@
         name="into_order",
     )(*in_hbm(node_order, features, adj_values))
 
-    across_adj = pl.pallas_call(
+    adj_turned = pl.pallas_call(
         turned,
         out_shape=jax.ShapeDtypeStruct(adj_values.shape, BF16),
         in_specs=[VMEM],
@@ -332,7 +342,7 @@
         compiler_params=PARAMS,
         cost_estimate=cost(4 * 10**9, 2**22),
         name="aggregate",
-    )(blk_count, *in_smem(blk_dest, blk_src), before, across, permuted, beside, after, across_adj)
+    )(blk_count, *in_smem(blk_dest, blk_src), beside, across, permuted, before, after, adj_turned)
 
     hidden_rows = lax.all_to_all(hidden, "x", 0, 0).reshape(parts * feat, width)
 
@@ -420,18 +430,18 @@
     pieces, own, grad_b = pl.pallas_call(
         functools.partial(last_sum, scale),
         out_shape=(
-            pltpu.HBM((2 * ys * parts, 8, BLOCK), F32),
+            pltpu.HBM((ys * parts, 8, BLOCK), F32),
             pltpu.HBM(own.shape, F32),
             jax.ShapeDtypeStruct((1, out_feat), F32),
         ),
         in_specs=[VMEM, HBM, ANY],
         out_specs=(HBM, HBM, VMEM),
-        scratch_shapes=[pltpu.VMEM((2 * ys * parts, 8, BLOCK), F32), dma((1,))],
+        scratch_shapes=[pltpu.VMEM((ys * parts, 8, BLOCK), F32), dma((1,))],
         input_output_aliases={1: 1},
         compiler_params=PARAMS,
         name="last_sum",
     )(partial, *in_hbm(own), last)
-    pieces = lax.all_to_all(pieces, ("y", "c", "x"), 0, 0)
+    pieces = lax.all_to_all(pieces, ("y", "x"), 0, 0)
 
     grad_x, token = pl.pallas_call(
         out_of_order,
@@ -445,6 +455,7 @@
             pltpu.VMEM((nblocks, feat, BLOCK), BF16),
             pltpu.VMEM((nblocks, feat, BLOCK), BF16),
             pltpu.VMEM((feat, nodes), BF16),
+            pltpu.VMEM((nblocks * feat, nodes), BF16),
             dma((5,)),
         ],
         compiler_params=PARAMS,
@@ -452,14 +463,22 @@
         name="out_of_order",
     )(*in_hbm(node_order, own), from_first, pair, from_last)
 
+    pieces = pl.pallas_call(
+        kept,
+        out_shape=jax.ShapeDtypeStruct(pieces.shape, F32),
+        in_specs=[VMEM, ANY],
+        out_specs=VMEM,
+        compiler_params=PARAMS,
+        name="kept",
+    )(pieces, token)
     grad_w = pl.pallas_call(
         functools.partial(put_together, parts),
         out_shape=jax.ShapeDtypeStruct((parts * 8 * ys, 2 * BLOCK), F32),
-        in_specs=[VMEM, ANY],
+        in_specs=[VMEM],
         out_specs=VMEM,
         compiler_params=PARAMS,
         name="put_together",
-    )(pieces, token)
+    )(lax.all_gather(pieces, "c"))
     return output, grad_x, grad_w, grad_b.reshape(out_feat)
 
 

time: 111 us -> 111 us (level)
  blocking collectives: 19 us -> 24.2 us
  waiting for transfers between devices: 13.5 us -> 11.3 us
  Pallas kernels: 18.9 us -> 17.5 us
  starting transfers between devices: 57.3 us -> 55.9 us
    ppermute x4, starting transfers between devices: 15.6 us -> 28.6 us  [chip_step(): return lax.ppermute(value, ROWS, pairs)]
    ppermute x3, starting transfers between devices: 20.9 us -> 8.96 us  [sibling(): return lax.ppermute(value, 'c', [(0, 1), (1, 0)])]
    all_gather x0 -> x1, blocking collectives: none -> 5.14 us  [on_device(): lax.all_gather(pieces, 'c')]
    all_to_all x1, starting transfers between devices: 6.67 us -> 4.2 us  [on_device(): pieces = lax.all_to_all(pieces, ('y', 'x'), 0, 0)]
    all_to_all x1, starting transfers between devices: 3.66 us -> 6.09 us  [on_device(): partial = lax.all_to_all(partial, 'z', 0, 0)]
    all_to_all x1, starting transfers between devices: 10.4 us -> 8.1 us  [on_device(): partial = lax.all_to_all(partial, ('y', 'c'), 0, 0)]
    all_to_all x1, waiting for transfers between devices: 7.73 us -> 6.19 us  [on_device(): pieces = lax.all_to_all(pieces, ('y', 'x'), 0, 0)]
    pallas_call x1, Pallas kernels: 4.53 us -> 3.12 us  [on_device(): pl.pallas_call(out_of_order, out_shape=(slab, jax.ShapeDtypeStruct((8, BL...]
  transfers between devices with their start and end apart: 10 -> 10, of which waited for: 4 -> 3; matrix products, arithmetic and copies ran while one was open for 0% -> 0% of each run, Pallas kernels for 10% -> 9%
where the time goes in v6:
time: 111 us; the launch traced here: 110 us
  starting transfers between devices  55.9 us (50%)
  blocking collectives  24.2 us (22%)
  Pallas kernels  17.5 us (16%)
  waiting for transfers between devices  11.3 us (10%)
  between operations  1.53 us (1%)
    ppermute x4, starting transfers between devices, chip_step(): return lax.ppermute(value, ROWS, pairs)  28.6 us
    all_to_all x1, blocking collectives, on_device(): recv = lax.all_to_all(send, 'x', 0, 0)  9.67 us
    all_to_all x1, blocking collectives, on_device(): hidden_rows = lax.all_to_all(hidden, 'x', 0, 0).reshape(parts * feat, width)  9.35 us
    ppermute x3, starting transfers between devices, sibling(): return lax.ppermute(value, 'c', [(0, 1), (1, 0)])  8.96 us
    all_to_all x1, starting transfers between devices, on_device(): partial = lax.all_to_all(partial, ('y', 'c'), 0, 0)  8.1 us
    all_to_all x1, waiting for transfers between devices, on_device(): pieces = lax.all_to_all(pieces, ('y', 'x'), 0, 0)  6.19 us
    all_to_all x1, starting transfers between devices, on_device(): partial = lax.all_to_all(partial, 'z', 0, 0)  6.09 us
    all_gather x1, blocking collectives, on_device(): lax.all_gather(pieces, 'c')  5.14 us
  transfers between devices with their start and end apart: 10, of which 3 were waited for; matrix products, arithmetic and copies ran while one was open for 0% of the time, Pallas kernels for 9%

profile of v6, /device:TPU:1, one launch (start us, length us, event | category | flops | bytes accessed | tf_op | source)
XLA Modules:
  0.0 110.5 jit_solution(14702137821118944242)
XLA Ops:
  0.6 2.2 %into_order.1 = (bf16[64,2048]{1,0:T(8,128)(2,1)S(1)}, bf16[96,128,128]{2,1,0:T(8,128)(2,1)S(1)}) custom-call(s32[1,2048]{1,0:T(1,128)} %order_hbm.3, bf16[64,2048]{1,0:T(8,128)(2,1)} %x_hbm.1, bf16[96,128,128]{2,1,0:T(8,128)(2,1)} %adj_hbm.3), custom_call_target="tpu_custom_call" | custom-call | flops 1000000000 | bytes 1048576 | tf_op jit(solution)/shard_map/into_order/pallas_call | solution.py:304
  2.9 4.0 %collective-permute-start.1 = (bf16[64,2048]{1,0:T(8,128)(2,1)S(1)}, bf16[64,2048]{1,0:T(8,128)(2,1)S(1)}, u32[]{:S(2)}, u32[]{:S(2)}) collective-permute-start(bf16[64,2048]{1,0:T(8,128)(2,1)S(1)} %get-tuple-element.22.permuted), channel_id=1, source_target_pairs={{0,760},{4,12},{8,0},{12,20},{16,8},{20,28},{24,16},{28,36},{32,24... | collective-permute-start | bytes 786440 | tf_op jit(solution)/shard_map/ppermute | solution.py:296
  6.9 15.9 %collective-permute-start.3 = (bf16[64,2048]{1,0:T(8,128)(2,1)S(1)}, bf16[64,2048]{1,0:T(8,128)(2,1)S(1)}, u32[]{:S(2)}, u32[]{:S(2)}) collective-permute-start(bf16[64,2048]{1,0:T(8,128)(2,1)S(1)} %get-tuple-element.22.permuted), channel_id=1, source_target_pairs={{0,8},{4,764},{8,16},{12,4},{16,24},{20,12},{24,32},{28,20},{32,40... | collective-permute-start | bytes 786440 | tf_op jit(solution)/shard_map/ppermute | solution.py:296
  22.9 2.9 %collective-permute-start = (bf16[64,2048]{1,0:T(8,128)(2,1)S(1)}, bf16[64,2048]{1,0:T(8,128)(2,1)S(1)}, u32[]{:S(2)}, u32[]{:S(2)}) collective-permute-start(bf16[64,2048]{1,0:T(8,128)(2,1)S(1)} %get-tuple-element.22.permuted), channel_id=1, source_target_pairs={{0,4},{4,0},{1,5},{5,1},{2,6},{6,2},{3,7},{7,3},{8,12},{12,8},{9,1... | collective-permute-start | bytes 786440 | tf_op jit(solution)/shard_map/ppermute | solution.py:299
  25.7 0.0 collective-permute-done.1.after
  25.7 4.0 %collective-permute-start.2 = (bf16[64,2048]{1,0:T(8,128)(2,1)S(1)}, bf16[64,2048]{1,0:T(8,128)(2,1)S(1)}, u32[]{:S(2)}, u32[]{:S(2)}) collective-permute-start(bf16[64,2048]{1,0:T(8,128)(2,1)S(1)} %collective-permute-done.1.after), channel_id=1, source_target_pairs={{0,4},{4,0},{1,5},{5,1},{2,6},{6,2},{3,7},{7,3},{8,12},{12,8},{9,1... | collective-permute-start | bytes 786440 | tf_op jit(solution)/shard_map/ppermute | solution.py:299
  30.3 0.0 copy-start
  30.3 0.0 copy-start.1
  30.4 0.9 turned.1.adj
  31.2 0.0 collective-permute-done.3.before
  31.2 0.0 collective-permute-done.beside
  31.2 0.0 collective-permute-done.2.across
  31.3 0.0 copy-done
  31.3 0.0 copy-done.1
  31.3 1.8 %aggregate.1 = bf16[4,64,512]{2,1,0:T(8,128)(2,1)S(1)} custom-call(s32[1]{0:T(128)S(6)} %copy.17.count_ref, s32[1,96]{1,0:T(1,128)S(1)} %copy-done, s32[1,96]{1,0:T(1,128)S(1)} %copy-done.1, bf16[64,2048]{1,0:T(8,128)(2,1)S(1)} %collective-permute-done.beside, bf16[64,2048]{1,0:T(8,128)(2,1)S(1)} %collective-permute-done.2.across, ...), custom_call_target="tpu_custom_call" | custom-call | flops 4000000000 | bytes 4194304 | tf_op jit(solution)/shard_map/aggregate/pallas_call | solution.py:333
  33.1 9.3 %all_to_all.25 = bf16[4,64,512]{2,1,0:T(8,128)(2,1)S(1)} all-to-all(bf16[4,64,512]{2,1,0:T(8,128)(2,1)S(1)} %aggregate.1), channel_id=1, replica_groups=mesh['z'=12,'y'=8,'c'=2,'x'=4] {'x'}, dimensions={0} | all-to-all | bytes 524288 | tf_op jit(solution)/shard_map/all_to_all | solution.py:347
  42.4 2.1 %dense.1 = (bf16[256,512]{1,0:T(8,128)(2,1)}, bf16[4,144,512]{2,1,0:T(8,128)(2,1)S(1)}) custom-call(bf16[256,512]{1,0:T(8,128)(2,1)S(1)} %bitcast.10, bf16[256,256]{1,0:T(8,128)(2,1)} %weight_hbm.1, f32[1,256]{1,0:T(1,128)} %bitcast.11, bf16[256,512]{1,0:T(8,128)(2,1)} %cot_hbm.1), custom_call_target="tpu_custom_call" | custom-call | flops 1000000000 | bytes 1048576 | tf_op jit(solution)/shard_map/dense/pallas_call | solution.py:349
  44.6 9.7 %all_to_all.26.recv = bf16[4,144,512]{2,1,0:T(8,128)(2,1)S(1)} all-to-all(bf16[4,144,512]{2,1,0:T(8,128)(2,1)S(1)} %get-tuple-element.25), channel_id=1, replica_groups=mesh['z'=12,'y'=8,'c'=2,'x'=4] {'x'}, dimensions={0} | all-to-all | bytes 1179648 | tf_op jit(solution)/shard_map/all_to_all | solution.py:368
  54.2 0.8 first_sum.1
  55.0 8.1 %all-to-all-start.2 = ((f32[16,16,128]{2,1,0:T(8,128)}), f32[16,16,128]{2,1,0:T(8,128)S(1)}, u32[]{:S(2)}, u32[]{:S(2)}) async-start(f32[16,16,128]{2,1,0:T(8,128)} %get-tuple-element.26), calls=%async_computation.2 | async-start | bytes 262144 | tf_op jit(solution)/shard_map/all_to_all | solution.py:383
  63.1 3.9 %spread_back.1 = (bf16[16,64,128]{2,1,0:T(8,128)(2,1)}, bf16[2,16,64,128]{3,2,1,0:T(8,128)(2,1)}, f32[16,64,128]{2,1,0:T(8,128)}, f32[16,64,128]{2,1,0:T(8,128)}, f32[8,128]{1,0:T(8,128)S(1)}) custom-call(s32[1]{0:T(128)S(6)} %copy.17.count_ref, s32[1,96]{1,0:T(1,128)} %dest_hbm.1, s32[1,96]{1,0:T(1,128)} %src_hbm.1, ...), custom_call_target="tpu_custom_call" | custom-call | flops 4000000000 | bytes 4194304 | tf_op jit(solution)/shard_map/spread_back/pallas_call | solution.py:385
  67.0 2.2 %collective-permute-start.4 = (bf16[2,16,64,128]{3,2,1,0:T(8,128)(2,1)}, bf16[2,16,64,128]{3,2,1,0:T(8,128)(2,1)S(1)}, u32[]{:S(2)}, u32[]{:S(2)}) collective-permute-start(bf16[2,16,64,128]{3,2,1,0:T(8,128)(2,1)} %get-tuple-element.33), channel_id=1, source_target_pairs={{0,4},{4,0},{1,5},{5,1},{2,6},{6,2},{3,7},{7,3},{8,12},{12,8},{9,1... | collective-permute-start | bytes 1572872 | tf_op jit(solution)/shard_map/ppermute | solution.py:299
  69.2 3.1 %all-to-all-done.2.recv = f32[16,16,128]{2,1,0:T(8,128)S(1)} async-done(((f32[16,16,128]{2,1,0:T(8,128)}), f32[16,16,128]{2,1,0:T(8,128)S(1)}, u32[]{:S(2)}, u32[]{:S(2)}) %all-to-all-start.2) | async-done | bytes 131104 | tf_op jit(solution)/shard_map/all_to_all | solution.py:383
  72.3 0.0 copy-start.2
  72.3 0.7 sum_to_all.1
  73.0 6.1 %all-to-all-start.3 = ((f32[12,16,128]{2,1,0:T(8,128)}), f32[12,16,128]{2,1,0:T(8,128)S(1)}, u32[]{:S(2)}, u32[]{:S(2)}) async-start(f32[12,16,128]{2,1,0:T(8,128)} %get-tuple-element.30), calls=%async_computation.3 | async-start | bytes 196608 | tf_op jit(solution)/shard_map/all_to_all | solution.py:423
  79.1 2.0 %collective-permute-start.5 = (bf16[16,64,128]{2,1,0:T(8,128)(2,1)}, bf16[16,64,128]{2,1,0:T(8,128)(2,1)S(1)}, u32[]{:S(2)}, u32[]{:S(2)}) collective-permute-start(bf16[16,64,128]{2,1,0:T(8,128)(2,1)} %get-tuple-element.35), channel_id=1, source_target_pairs={{0,760},{4,12},{8,0},{12,20},{16,8},{20,28},{24,16},{28,36},{32,24... | collective-permute-start | bytes 786440 | tf_op jit(solution)/shard_map/ppermute | solution.py:296
  81.1 0.0 collective-permute-done.4.pair_hbm
  81.1 0.0 copy-done.2
  81.1 0.1 fusion.token
  81.2 6.6 %collective-permute-start.6 = (bf16[16,64,128]{2,1,0:T(8,128)(2,1)S(1)}, bf16[16,64,128]{2,1,0:T(8,128)(2,1)S(1)}, u32[]{:S(2)}, u32[]{:S(2)}) collective-permute-start(bf16[16,64,128]{2,1,0:T(8,128)(2,1)S(1)} %fusion.token), channel_id=1, source_target_pairs={{0,8},{4,764},{8,16},{12,4},{16,24},{20,12},{24,32},{28,20},{32,40... | collective-permute-start | bytes 786440 | tf_op jit(solution)/shard_map/ppermute | solution.py:296
  87.8 2.0 %all-to-all-done.3.recv = f32[12,16,128]{2,1,0:T(8,128)S(1)} async-done(((f32[12,16,128]{2,1,0:T(8,128)}), f32[12,16,128]{2,1,0:T(8,128)S(1)}, u32[]{:S(2)}, u32[]{:S(2)}) %all-to-all-start.3) | async-done | bytes 98336 | tf_op jit(solution)/shard_map/all_to_all | solution.py:423
  89.8 1.2 %last_sum.1 = (f32[32,8,128]{2,1,0:T(8,128)}, f32[16,64,128]{2,1,0:T(8,128)}, f32[1,256]{1,0:T(1,128)}) custom-call(f32[12,16,128]{2,1,0:T(8,128)S(1)} %all-to-all-done.3.recv, f32[16,64,128]{2,1,0:T(8,128)} %get-tuple-element.31.own_hbm, bf16[16,64,128]{2,1,0:T(8,128)(2,1)S(1)} %fusion.token), custom_call_target="tpu_custom_call", output_to_operand_aliasing={{1}: (1, {})} | custom-call | tf_op jit(solution)/shard_map/last_sum/pallas_call | solution.py:430
  91.0 4.2 %all-to-all-start.4 = ((f32[32,8,128]{2,1,0:T(8,128)}), f32[32,8,128]{2,1,0:T(8,128)S(1)}, u32[]{:S(2)}, u32[]{:S(2)}) async-start(f32[32,8,128]{2,1,0:T(8,128)} %get-tuple-element.37), calls=%async_computation.4 | async-start | bytes 262144 | tf_op jit(solution)/shard_map/all_to_all | solution.py:444
  95.3 0.0 collective-permute-done.5.first_hbm
  95.3 0.0 collective-permute-done.6.last_hbm
  95.3 3.1 %out_of_order.1 = (bf16[64,2048]{1,0:T(8,128)(2,1)}, f32[8,128]{1,0:T(8,128)S(1)}) custom-call(s32[1,2048]{1,0:T(1,128)} %order_hbm.3, f32[16,64,128]{2,1,0:T(8,128)} %get-tuple-element.34.own_hbm, bf16[16,64,128]{2,1,0:T(8,128)(2,1)S(1)} %collective-permute-done.5.first_hbm, bf16[2,16,64,128]{3,2,1,0:T(8,128)(2,1)S(1)} %collective-permute-done.4.pair_hbm, ...), custom_call_target="tpu_custom_call" | custom-call | flops 3000000000 | bytes 2097152 | tf_op jit(solution)/shard_map/out_of_order/pallas_call | solution.py:446
  98.4 6.2 %all-to-all-done.4.recv = f32[32,8,128]{2,1,0:T(8,128)S(1)} async-done(((f32[32,8,128]{2,1,0:T(8,128)}), f32[32,8,128]{2,1,0:T(8,128)S(1)}, u32[]{:S(2)}, u32[]{:S(2)}) %all-to-all-start.4) | async-done | bytes 131104 | tf_op jit(solution)/shard_map/all_to_all | solution.py:444
  104.6 5.1 %all-gather = f32[64,8,128]{2,1,0:T(8,128)S(1)} all-gather(f32[32,8,128]{2,1,0:T(8,128)S(1)} %kept.1), channel_id=2, replica_groups=mesh['z'=12,'y'=8,'c'=2,'x'=4] {'c'}, dimensions={0}, use_global_device_ids=true | all-gather | bytes 393216 | tf_op jit(solution)/shard_map/all_gather | solution.py:481
  109.8 0.7 put_together.1
  (1 shorter events, 0.0 us)
Async XLA Ops:
  2.9 22.9 %collective-permute-start.1 = (bf16[64,2048]{1,0:T(8,128)(2,1)S(1)}, bf16[64,2048]{1,0:T(8,128)(2,1)S(1)}, u32[]{:S(2)}, u32[]{:S(2)}) collective-permute-start(bf16[64,2048]{1,0:T(8,128)(2,1)S(1)} %get-tuple-element.22.permuted), channel_id=1, source_target_pairs={{0,760},{4,12},{8,0},{12,20},{16,8},{20,28},{24,16},{28,36},{32,24... | collective-permute-start | bytes 786440 | tf_op jit(solution)/shard_map/ppermute | solution.py:296
  6.9 24.3 %collective-permute-start.3 = (bf16[64,2048]{1,0:T(8,128)(2,1)S(1)}, bf16[64,2048]{1,0:T(8,128)(2,1)S(1)}, u32[]{:S(2)}, u32[]{:S(2)}) collective-permute-start(bf16[64,2048]{1,0:T(8,128)(2,1)S(1)} %get-tuple-element.22.permuted), channel_id=1, source_target_pairs={{0,8},{4,764},{8,16},{12,4},{16,24},{20,12},{24,32},{28,20},{32,40... | collective-permute-start | bytes 786440 | tf_op jit(solution)/shard_map/ppermute | solution.py:296
  22.9 8.4 %collective-permute-start = (bf16[64,2048]{1,0:T(8,128)(2,1)S(1)}, bf16[64,2048]{1,0:T(8,128)(2,1)S(1)}, u32[]{:S(2)}, u32[]{:S(2)}) collective-permute-start(bf16[64,2048]{1,0:T(8,128)(2,1)S(1)} %get-tuple-element.22.permuted), channel_id=1, source_target_pairs={{0,4},{4,0},{1,5},{5,1},{2,6},{6,2},{3,7},{7,3},{8,12},{12,8},{9,1... | collective-permute-start | bytes 786440 | tf_op jit(solution)/shard_map/ppermute | solution.py:299
  25.7 5.5 %collective-permute-start.2 = (bf16[64,2048]{1,0:T(8,128)(2,1)S(1)}, bf16[64,2048]{1,0:T(8,128)(2,1)S(1)}, u32[]{:S(2)}, u32[]{:S(2)}) collective-permute-start(bf16[64,2048]{1,0:T(8,128)(2,1)S(1)} %collective-permute-done.1.after), channel_id=1, source_target_pairs={{0,4},{4,0},{1,5},{5,1},{2,6},{6,2},{3,7},{7,3},{8,12},{12,8},{9,1... | collective-permute-start | bytes 786440 | tf_op jit(solution)/shard_map/ppermute | solution.py:299
  30.3 0.9 copy-start
  30.3 0.9 copy-start.1
  55.0 17.3 %all-to-all-start.2 = ((f32[16,16,128]{2,1,0:T(8,128)}), f32[16,16,128]{2,1,0:T(8,128)S(1)}, u32[]{:S(2)}, u32[]{:S(2)}) async-start(f32[16,16,128]{2,1,0:T(8,128)} %get-tuple-element.26), calls=%async_computation.2 | async-start | bytes 262144 | tf_op jit(solution)/shard_map/all_to_all | solution.py:383
  67.0 14.1 %collective-permute-start.4 = (bf16[2,16,64,128]{3,2,1,0:T(8,128)(2,1)}, bf16[2,16,64,128]{3,2,1,0:T(8,128)(2,1)S(1)}, u32[]{:S(2)}, u32[]{:S(2)}) collective-permute-start(bf16[2,16,64,128]{3,2,1,0:T(8,128)(2,1)} %get-tuple-element.33), channel_id=1, source_target_pairs={{0,4},{4,0},{1,5},{5,1},{2,6},{6,2},{3,7},{7,3},{8,12},{12,8},{9,1... | collective-permute-start | bytes 1572872 | tf_op jit(solution)/shard_map/ppermute | solution.py:299
  72.3 8.8 %copy-start.2 = (f32[16,64,128]{2,1,0:T(8,128)S(1)}, f32[16,64,128]{2,1,0:T(8,128)}, u32[]{:S(2)}) copy-start(f32[16,64,128]{2,1,0:T(8,128)} %get-tuple-element.32) | copy-start | bytes 1572868
  73.0 16.8 %all-to-all-start.3 = ((f32[12,16,128]{2,1,0:T(8,128)}), f32[12,16,128]{2,1,0:T(8,128)S(1)}, u32[]{:S(2)}, u32[]{:S(2)}) async-start(f32[12,16,128]{2,1,0:T(8,128)} %get-tuple-element.30), calls=%async_computation.3 | async-start | bytes 196608 | tf_op jit(solution)/shard_map/all_to_all | solution.py:423
  79.1 16.2 %collective-permute-start.5 = (bf16[16,64,128]{2,1,0:T(8,128)(2,1)}, bf16[16,64,128]{2,1,0:T(8,128)(2,1)S(1)}, u32[]{:S(2)}, u32[]{:S(2)}) collective-permute-start(bf16[16,64,128]{2,1,0:T(8,128)(2,1)} %get-tuple-element.35), channel_id=1, source_target_pairs={{0,760},{4,12},{8,0},{12,20},{16,8},{20,28},{24,16},{28,36},{32,24... | collective-permute-start | bytes 786440 | tf_op jit(solution)/shard_map/ppermute | solution.py:296
  81.2 14.1 %collective-permute-start.6 = (bf16[16,64,128]{2,1,0:T(8,128)(2,1)S(1)}, bf16[16,64,128]{2,1,0:T(8,128)(2,1)S(1)}, u32[]{:S(2)}, u32[]{:S(2)}) collective-permute-start(bf16[16,64,128]{2,1,0:T(8,128)(2,1)S(1)} %fusion.token), channel_id=1, source_target_pairs={{0,8},{4,764},{8,16},{12,4},{16,24},{20,12},{24,32},{28,20},{32,40... | collective-permute-start | bytes 786440 | tf_op jit(solution)/shard_map/ppermute | solution.py:296
  91.0 13.6 %all-to-all-start.4 = ((f32[32,8,128]{2,1,0:T(8,128)}), f32[32,8,128]{2,1,0:T(8,128)S(1)}, u32[]{:S(2)}, u32[]{:S(2)}) async-start(f32[32,8,128]{2,1,0:T(8,128)} %get-tuple-element.37), calls=%async_computation.4 | async-start | bytes 262144 | tf_op jit(solution)/shard_map/all_to_all | solution.py:444
